TPU v7x, 768 devices: a whole 4x8x12 slice. The times are simulated.
768 devices in a mesh: seq: 96 (over z, y), head: 8 (over x, core).
Axes of the slice: x: 4, y: 8, z: 12, core: 2. Of those that a mesh axis runs over, the one named last changes fastest.
Arguments:
- hidden: bfloat16 [27648, 6144], P('seq', 'head'), may hold values from -4 to 4
- upstream: bfloat16 [27648, 6144], P('seq', 'head'), may hold values from -6 to 6
- w_query: bfloat16 [8, 6144, 128], P('head'), may hold values from -0.0390625 to 0.0390625
- w_key: bfloat16 [8, 6144, 128], P('head'), may hold values from -0.078125 to 0.078125
- w_value: bfloat16 [8, 6144, 128], P('head'), may hold values from -0.078125 to 0.078125
- w_output: bfloat16 [8, 128, 6144], P('head'), may hold values from -0.5 to 0.5
- selected: int32 [8, 3456], replicated, may hold values from 0 to 287, as said below
- select_count: int32 [8, 96], replicated, may hold values from 1 to 36, as said below
Outputs:
- grad_hidden: bfloat16 [27648, 6144], P('seq', 'head')
- grad_query: float32 [8, 6144, 128], P('head', 'seq')
Inputs may be any that keep to these rules, and one draw needn't show every extreme that they name: `selected`: for each head h and block b, entries b * 36 to b * 36 + select_count[h, b] - 1 are distinct and ascending; the remaining entries of the block are 0. `select_count`: every head has some block with 36 used slots.
All inputs are finite; a program needn't handle non-finite values.
Results may differ from a plain program's by a relative error of at most 0.02.
Values may be sent and summed in bfloat16 or wider, within the bound.
No kernel may reach another device: no remote copies, remote signals or barrier semaphores. Data moves between devices by JAX's collectives and lax.ppermute only.
A program may use at most 64 MiB of HBM per device.

v0:
```python
import jax
import jax.numpy as jnp
from jax import lax
from jax.sharding import PartitionSpec as P


def body(hidden, upstream, w_query, w_key, w_value, w_output, selected, select_count):
    seq_count = lax.axis_size("seq")
    seq_index = lax.axis_index("seq")
    head_index = lax.axis_index("head")
    tok_rows = hidden.shape[0]
    slots = selected.shape[1]
    capacity = slots // seq_count
    score_scale = w_query.shape[2] ** (-0.5)
    slot_ids = jnp.arange(slots, dtype=jnp.int32)
    block_ids = slot_ids // capacity
    start_slot = seq_index * capacity
    dev_select = lax.dynamic_slice_in_dim(selected, start_slot, capacity, 1)
    dev_count = lax.dynamic_slice_in_dim(select_count, seq_index, 1, 1)
    dev_live = jnp.arange(capacity, dtype=jnp.int32)[None, :] < dev_count
    picked_in = hidden[dev_select]
    picked_up = upstream[dev_select]
    rows_in, rows_up = (
        lax.all_to_all(picked_in, "head", split_axis=0, concat_axis=2, tiled=True),
        lax.all_to_all(picked_up, "head", split_axis=0, concat_axis=2, tiled=True),
    )
    rows_in = rows_in[0]
    rows_up = rows_up[0]
    own_select = lax.dynamic_index_in_dim(selected, head_index, 0, keepdims=False)
    own_count = lax.dynamic_index_in_dim(select_count, head_index, 0, keepdims=False)
    positions = block_ids * tok_rows + own_select
    live_all = slot_ids % capacity < own_count[block_ids]
    local_pos = lax.dynamic_slice_in_dim(positions, start_slot, capacity, 0)
    local_live = lax.dynamic_slice_in_dim(live_all, start_slot, capacity, 0)
    weight_q = w_query[0]
    weight_k = w_key[0]
    weight_v = w_value[0]
    weight_o = w_output[0]
    contract_last = (((1,), (1,)), ((), ()))
    contract_first = (((0,), (0,)), ((), ()))
    queries = jnp.dot(rows_in, weight_q, preferred_element_type=jnp.float32).astype(jnp.bfloat16)
    keys_loc = jnp.dot(rows_in, weight_k, preferred_element_type=jnp.float32).astype(jnp.bfloat16)
    values_loc = jnp.dot(rows_in, weight_v, preferred_element_type=jnp.float32).astype(jnp.bfloat16)
    grad_attn = jnp.where(
        local_live[:, None],
        lax.dot_general(rows_up, weight_o, contract_last, preferred_element_type=jnp.float32),
        0.0,
    ).astype(jnp.bfloat16)
    keys_all, values_all = (
        lax.all_gather(keys_loc, "seq", axis=0, tiled=True),
        lax.all_gather(values_loc, "seq", axis=0, tiled=True),
    )
    allowed = local_live[:, None] & live_all[None, :] & (positions[None, :] <= local_pos[:, None])
    scores = (
        lax.dot_general(queries, keys_all, contract_last, preferred_element_type=jnp.float32)
        * score_scale
    )
    total = jnp.sum(jnp.where(allowed, jnp.exp(scores), 0.0), axis=-1) + jnp.where(
        local_live, 0.0, 1.0
    )
    log_total = jnp.log(total)
    probs = jnp.where(allowed, jnp.exp(scores - log_total[:, None]), 0.0)
    probs_b = probs.astype(jnp.bfloat16)
    attended = jnp.dot(probs_b, values_all, preferred_element_type=jnp.float32).astype(jnp.bfloat16)
    delta = jnp.sum(grad_attn.astype(jnp.float32) * attended.astype(jnp.float32), axis=-1)
    grad_probs = lax.dot_general(
        grad_attn, values_all, contract_last, preferred_element_type=jnp.float32
    )
    grad_scores = (probs * (grad_probs - delta[:, None])).astype(jnp.bfloat16)
    grad_q = (
        jnp.dot(grad_scores, keys_all, preferred_element_type=jnp.float32) * score_scale
    ).astype(jnp.bfloat16)
    term_k = (
        lax.dot_general(grad_scores, queries, contract_first, preferred_element_type=jnp.float32)
        * score_scale
    )
    term_v = lax.dot_general(probs_b, grad_attn, contract_first, preferred_element_type=jnp.float32)
    summed = lax.psum_scatter(
        jnp.concatenate([term_k, term_v], axis=-1), "seq", scatter_dimension=0, tiled=True
    )
    head_size = queries.shape[1]
    grad_k = summed[:, :head_size].astype(jnp.bfloat16)
    grad_v = summed[:, head_size:].astype(jnp.bfloat16)
    grad_rows = (
        lax.dot_general(grad_q, weight_q, contract_last, preferred_element_type=jnp.float32)
        + lax.dot_general(grad_k, weight_k, contract_last, preferred_element_type=jnp.float32)
        + lax.dot_general(grad_v, weight_v, contract_last, preferred_element_type=jnp.float32)
    )
    grad_rows = jnp.where(local_live[:, None], grad_rows, 0.0)
    returned = lax.all_to_all(grad_rows, "head", split_axis=1, concat_axis=0, tiled=True)
    flat_select = dev_select.reshape(-1)
    flat_live = dev_live.reshape(-1)
    grad_hidden = (
        jnp.zeros((tok_rows, returned.shape[1]), jnp.float32)
        .at[flat_select]
        .add(jnp.where(flat_live[:, None], returned, 0.0))
    )
    weight_terms = lax.dot_general(
        rows_in, grad_q, contract_first, preferred_element_type=jnp.float32
    )
    weight_sums = lax.psum_scatter(weight_terms, "seq", scatter_dimension=0, tiled=True)
    return (grad_hidden.astype(jnp.bfloat16), weight_sums[None])


def solution(mesh):
    in_specs = (
        P("seq", "head"),
        P("seq", "head"),
        P("head", None, None),
        P("head", None, None),
        P("head", None, None),
        P("head", None, None),
        P(),
        P(),
    )
    out_specs = (P("seq", "head"), P("head", "seq", None))
    return jax.shard_map(body, mesh=mesh, in_specs=in_specs, out_specs=out_specs, check_vma=False)
```

profile of v0, /device:TPU:1, one launch (start us, length us, event | category | flops | bytes accessed | tf_op | source)
XLA Modules:
  0.0 911.8 jit_solution(3466547867363731989)
XLA Ops:
  7.2 1.5 compare_select_fusion.1
  8.8 3.5 gather_fusion.2
  13.2 13.9 %all-to-all-start.1 = ((bf16[8,36,768]{2,1,0:T(8,128)(2,1)}), bf16[8,36,768]{2,1,0:T(8,128)(2,1)S(1)}, u32[]{:S(2)}, u32[]{:S(2)}) async-start(bf16[8,36,768]{2,1,0:T(8,128)(2,1)} %reshape.165), calls=%async_computation.1 | async-start | bytes 983040 | tf_op jit(solution)/shard_map/all_to_all | solution.py:25
  27.1 2.1 gather_fusion.1
  30.8 19.7 %gather_fusion = s32[3456]{0:T(1024)S(1)} fusion(s32[96]{0:T(128)S(1)} %fusion.58, s32[4096]{0:T(1024)S(1)} %pad_clamp_fusion), kind=kCustom, calls=%fused_computation | custom fusion | bytes 41472 | tf_op jit(solution)/shard_map/gather | solution.py:32
  50.6 4.8 all-to-all-start
  57.9 6.6 all-to-all-done
  64.7 1.2 copy-done.4
  68.4 60.2 %all-gather = bf16[96,36,128]{2,1,0:T(8,128)(2,1)S(1)} all-gather(bf16[1,36,128]{2,1,0:T(8,128)(2,1)S(1)} %fusion.39), channel_id=1, replica_groups=mesh['seq'=96,'head'=8] {'seq'}, dimensions={0}, use_global_device_ids=true | all-gather | bytes 893952 | tf_op jit(solution)/shard_map/all_gather | solution.py:50
  128.5 1.1 reshape.185
  129.6 2.7 select_reduce_fusion
  132.4 1.3 add_log_fusion
  133.6 54.9 %all-gather.1 = bf16[96,36,128]{2,1,0:T(8,128)(2,1)S(1)} all-gather(bf16[1,36,128]{2,1,0:T(8,128)(2,1)} %fusion.36), channel_id=1, replica_groups=mesh['seq'=96,'head'=8] {'seq'}, dimensions={0}, use_global_device_ids=true | all-gather | bytes 893952 | tf_op jit(solution)/shard_map/all_gather | solution.py:51
  188.6 1.1 reshape.187
  189.7 2.2 fusion.32
  193.4 2.3 fusion.63
  195.8 1.3 dynamic-slice
  198.5 2.0 pad_maximum_fusion
  200.5 372.4 %all-reduce.2 = bf16[3456,256]{0,1:T(8,128)(2,1)S(1)} all-reduce(f32[3456,256]{0,1:T(8,128)} %pad_maximum_fusion), channel_id=2, replica_groups=mesh['seq'=96,'head'=8] {'seq'}, use_global_device_ids=true, to_apply=%region_2.3.clone | all-reduce | flops 884736 | bytes 5308416
  577.2 1.2 copy.16
  578.4 122.0 %all-to-all-start.2 = ((f32[36,8,768]{2,0,1:T(8,128)}), f32[36,8,768]{2,0,1:T(8,128)S(1)}, u32[]{:S(2)}, u32[]{:S(2)}) async-start(f32[36,8,768]{2,0,1:T(8,128)} %copy.16), calls=%async_computation.2 | async-start | bytes 1966080 | tf_op jit(solution)/shard_map/all_to_all | solution.py:90
  700.8 13.9 %all-to-all-done.2 = f32[36,8,768]{2,0,1:T(8,128)S(1)} async-done(((f32[36,8,768]{2,0,1:T(8,128)}), f32[36,8,768]{2,0,1:T(8,128)S(1)}, u32[]{:S(2)}, u32[]{:S(2)}) %all-to-all-start.2) | async-done | bytes 884768 | tf_op jit(solution)/shard_map/all_to_all | solution.py:90
  714.9 2.8 scatter_custom_fusion
  718.5 186.5 %reduce-scatter.3.cloned.1.call-done = f32[64,128]{1,0:T(8,128)} async-done(((f32[6144,128]{1,0:T(8,128)}), f32[64,128]{1,0:T(8,128)}) %reduce-scatter.3.cloned.1.call-update) | async-done | bytes 32784 | tf_op jit(solution)/shard_map/reduce_scatter | solution.py:101
  (77 shorter events, 15.6 us)
Async XLA Ops:
  7.2 59.8 %copy-start = (bf16[1,6144,128]{2,1,0:T(8,128)(2,1)S(1)}, bf16[1,6144,128]{2,1,0:T(8,128)(2,1)}, u32[]{:S(2)}) copy-start(bf16[1,6144,128]{2,1,0:T(8,128)(2,1)} %param.12) | copy-start | bytes 4718596
  12.3 14.8 %copy-start.1 = (bf16[288,768]{1,0:T(8,128)(2,1)S(1)}, bf16[288,768]{1,0:T(8,128)(2,1)}, u32[]{:S(2)}) copy-start(bf16[288,768]{1,0:T(8,128)(2,1)} %param.8) | copy-start | bytes 1327108
  13.2 37.4 %all-to-all-start.1 = ((bf16[8,36,768]{2,1,0:T(8,128)(2,1)}), bf16[8,36,768]{2,1,0:T(8,128)(2,1)S(1)}, u32[]{:S(2)}, u32[]{:S(2)}) async-start(bf16[8,36,768]{2,1,0:T(8,128)(2,1)} %reshape.165), calls=%async_computation.1 | async-start | bytes 983040 | tf_op jit(solution)/shard_map/all_to_all | solution.py:25
  50.6 14.0 %all-to-all-start = ((bf16[8,36,768]{2,1,0:T(8,128)(2,1)}), bf16[8,36,768]{2,1,0:T(8,128)(2,1)S(1)}, u32[]{:S(2)}, u32[]{:S(2)}) async-start(bf16[8,36,768]{2,1,0:T(8,128)(2,1)} %reshape.157), calls=%async_computation | async-start | bytes 983040 | tf_op jit(solution)/shard_map/all_to_all | solution.py:24
  55.4 849.6 %reduce-scatter.3.cloned.1.call-start = ((), (), s32[]{:S(2)}) async-start(), calls=%async_computation.4 | async-start | bytes 3178496 | tf_op jit(solution)/shard_map/reduce_scatter | solution.py:101
  55.4 9.1 copy-start.10
  64.5 1.4 copy-start.4
  65.9 2.0 copy-start.2
  189.7 2.2 copy-start.7
  189.7 2.2 copy-start.8
  189.7 2.2 copy-start.11
  189.7 2.2 copy-start.13
  189.7 2.2 copy-start.15
  189.7 2.2 copy-start.16
  192.0 1.2 copy-start.6
  195.7 1.9 copy-start.9
  572.9 1.4 copy-start.3
  574.3 1.4 copy-start.5
  574.3 1.4 copy-start.14
  577.2 123.2 %copy-start.17 = (s32[8,96]{1,0:T(8,128)S(1)}, s32[8,96]{1,0:T(8,128)}, u32[]{:S(2)}) copy-start(s32[8,96]{1,0:T(8,128)} %param.15) | copy-start | bytes 9220
  577.2 123.5 %copy-start.12 = (s32[8,36]{1,0:T(8,128)S(1)}, s32[8,36]{1,0:T(8,128)}, u32[]{:S(2)}) copy-start(s32[8,36]{1,0:T(8,128)} %get-tuple-element.5) | copy-start | bytes 3460
  578.4 136.4 %all-to-all-start.2 = ((f32[36,8,768]{2,0,1:T(8,128)}), f32[36,8,768]{2,0,1:T(8,128)S(1)}, u32[]{:S(2)}, u32[]{:S(2)}) async-start(f32[36,8,768]{2,0,1:T(8,128)} %copy.16), calls=%async_computation.2 | async-start | bytes 1966080 | tf_op jit(solution)/shard_map/all_to_all | solution.py:90
Sparse Core Ops, SparseCore 0:
  195.9 709.0 reduce-scatter.2
where the time goes:
time: 913 us; the launch traced here: 912 us
  blocking collectives  488 us (53%)
  waiting for transfers between devices  207 us (23%)
  starting transfers between devices  141 us (15%)
  local copies, waits for them, and re-layouts  36.4 us (4%)
  matrix products  15 us (2%)
  between operations  15 us (2%)
  other arithmetic  10.2 us (1%)
    unnamed x1, blocking collectives  372 us
    reduce_scatter x1, waiting for transfers between devices, body(): lax.psum_scatter(weight_terms, 'seq', scatter_dimension=0, tiled=True)  186 us
    all_to_all x1, starting transfers between devices, body(): lax.all_to_all(grad_rows, 'head', split_axis=1, concat_axis=0, tiled=True)  122 us
    all_gather x1, blocking collectives, body(): lax.all_gather(keys_loc, 'seq', axis=0, tiled=True)  60.2 us
    all_gather x1, blocking collectives, body(): lax.all_gather(values_loc, 'seq', axis=0, tiled=True)  54.9 us
    gather x1, local copies, waits for them, and re-layouts, body(): live_all = slot_ids % capacity < own_count[block_ids]  19.7 us
  transfers between devices with their start and end apart: 4, of which 3 were waited for; matrix products, arithmetic and copies ran while one was open for 4% of the time, Pallas kernels for 0%

commit v1 on v0

v1 whole, which is shorter than its diff:
```python
import functools

import jax
import jax.numpy as jnp
from jax import lax
from jax.experimental import pallas as pl
from jax.experimental.pallas import tpu as pltpu
from jax.sharding import Mesh, PartitionSpec as P

NY = 8
SLOT = 48
NEG = -1e30
BF = jnp.bfloat16
F32 = jnp.float32
VMEM = pl.BlockSpec(memory_space=pltpu.VMEM)
SMEM = pl.BlockSpec(memory_space=pltpu.SMEM)
NN = (((1,), (0,)), ((), ()))
NT = (((1,), (1,)), ((), ()))
TN = (((0,), (0,)), ((), ()))


def mm(a, b, dims=NN):
    return lax.dot_general(a, b, dims, preferred_element_type=F32)


def call(kernel, outs, args, specs, scratch=(), limit=20):
    return pl.pallas_call(
        kernel,
        out_shape=outs,
        in_specs=specs,
        out_specs=jax.tree.map(lambda _: VMEM, outs),
        scratch_shapes=list(scratch),
        compiler_params=pltpu.CompilerParams(vmem_limit_bytes=limit << 20),
    )(*args)


def pick_kernel(sel_ref, hid_ref, up_ref, out_ref):
    heads, rows, cols = out_ref.shape
    toks = hid_ref.shape[0]
    sel_t = sel_ref[...].astype(F32).T
    target = jnp.concatenate([sel_t[:rows, h : h + 1] for h in range(heads)], axis=0)
    target = target.astype(jnp.int32)
    lane = lax.broadcasted_iota(jnp.int32, (heads * rows, 2 * toks), 1)
    onehot = jnp.where(lane == target, 1.0, 0.0).astype(BF)
    table = jnp.concatenate([hid_ref[...], up_ref[...]], axis=0)
    out_ref[...] = mm(onehot, table).reshape(heads, rows, cols).astype(BF)


def project_kernel(
    idx_ref, cnt_ref, r_ref, wq_ref, wk_ref, wv_ref, wo_ref, y_ref, z_ref, g_acc
):
    heads, rows, cols = r_ref.shape
    cap, hd = rows // 2, wq_ref.shape[1]
    q = k = v = jnp.zeros((SLOT, hd), F32)
    g = jnp.zeros((rows, hd), F32)
    for c in range(heads):
        part = pl.ds(c * cols, cols)
        x = r_ref[c]
        q = q + mm(x[:SLOT], wq_ref[part, :])
        k = k + mm(x[:SLOT], wk_ref[part, :])
        v = v + mm(x[:SLOT], wv_ref[part, :])
        g = g + mm(x, wo_ref[:, part], NT)
    g_acc[...] = g
    g = g_acc[cap:, :]
    count = cnt_ref[idx_ref[2], idx_ref[0] * NY + idx_ref[1]]
    row = lax.broadcasted_iota(jnp.int32, (cap, hd), 0)
    g = jnp.where(row < count, g, 0.0).astype(BF)
    q, k, v = (a.astype(BF)[:cap] for a in (q, k, v))
    for i in range(y_ref.shape[0]):
        y_ref[i, :, :hd] = q
        y_ref[i, :, hd:] = g
    nz = z_ref.shape[0]
    piece = heads * cols // nz
    for i in range(nz):
        z_ref[i, :, :hd] = k
        z_ref[i, :, hd : 2 * hd] = v
        at, left, put = i * piece, piece, 2 * hd
        while left:
            c, off = at // cols, at % cols
            n = min(left, cols - off)
            z_ref[i, :, put : put + n] = r_ref[c, :cap, off : off + n]
            at, left, put = at + n, left - n, put + n


def padded(pad_ref, ref, lo, hi):
    n, cap = ref.shape[0], ref.shape[1]
    w = hi - lo
    pad_ref[:, SLOT - 16 :, :] = jnp.zeros((n, 16, w), BF)
    for i in range(n):
        pad_ref[i, :cap, :] = ref[i, :, lo:hi]
    return pad_ref[...].reshape(n * SLOT, w)


def orders(idx_ref, cnt_ref, nz, axis_q):
    z, y, h = idx_ref[0], idx_ref[1], idx_ref[2]

    def one(n, axis, block_of, dead):
        shape = (n * SLOT, 1) if axis == 0 else (1, n * SLOT)
        at = lax.broadcasted_iota(jnp.int32, shape, axis)
        out = jnp.full(shape, dead, jnp.int32)
        for i in range(n):
            b = block_of(i)
            c = at - i * SLOT
            live = (c >= 0) & (c < cnt_ref[h, b])
            out = jnp.where(live, c + b * SLOT, out)
        return out

    order_q = one(NY, axis_q, lambda i: z * NY + i, -1)
    order_k = one(nz, 1 - axis_q, lambda i: i * NY + y, 1 << 30)
    return order_q, order_k


def split(x):
    hi = x.astype(BF).astype(F32)
    return hi, x - hi


def partial_kernel(scale, idx_ref, cnt_ref, qg_ref, kv_ref, out_ref, qg_pad, kv_pad):
    nz, hd = kv_ref.shape[0], qg_ref.shape[2] // 2
    qg = padded(qg_pad, qg_ref, 0, 2 * hd)
    kv = padded(kv_pad, kv_ref, 0, 2 * hd)
    q, g, k, v = qg[:, :hd], qg[:, hd:], kv[:, :hd], kv[:, hd:]
    order_q, order_k = orders(idx_ref, cnt_ref, nz, 0)
    allowed = order_k <= order_q
    s = jnp.where(allowed, mm(q, k, NT) * scale, NEG)
    top = jnp.max(s, axis=1, keepdims=True)
    top = (top + jnp.abs(top) * (2.0**-7)).astype(BF).astype(F32)
    e = jnp.where(allowed, jnp.exp(s - top), 0.0)
    total = jnp.sum(e, axis=1, keepdims=True)
    p = e * (1.0 / jnp.where(total > 0.0, total, 1.0))
    gp = mm(g, v, NT)
    delta = jnp.sum(p * gp, axis=1, keepdims=True)
    p_b = p.astype(BF)
    a = mm((p * (gp - delta)).astype(BF), k) * scale
    b = mm(p_b, k) * scale
    t_hi, t_lo = split(total)
    d_hi, d_lo = split(delta)
    rows = q.shape[0]
    lane = lax.broadcasted_iota(jnp.int32, (rows, hd), 1)
    stats = jnp.zeros((rows, hd), F32)
    for i, col in enumerate((top, t_hi, t_lo, d_hi, d_lo)):
        stats = jnp.where(lane == i, col, stats)
    flat = stats.T[:16, :].astype(BF)
    own = jnp.concatenate([a, b, stats], axis=1).astype(BF)
    for i in range(NY):
        out_ref[i, :SLOT, :] = own[i * SLOT : (i + 1) * SLOT, :]
        out_ref[i, SLOT:, :] = flat


def combine(parts):
    top = functools.reduce(jnp.maximum, [p[0] for p in parts])
    weights = [p[1] * jnp.exp(p[0] - top) for p in parts]
    total = sum(weights[1:], weights[0])
    total = jnp.where(total > 0.0, total, 1.0)
    shares = [w / total for w in weights]
    delta = functools.reduce(jnp.add, [w * p[2] for w, p in zip(shares, parts)])
    return shares, top + jnp.log(total), delta


def grads_kernel(scale, idx_ref, cnt_ref, qg_ref, kv_ref, st_ref, out_ref, qg_pad, kv_pad):
    nz, cap, hd = kv_ref.shape[0], qg_ref.shape[1], qg_ref.shape[2] // 2
    qg = padded(qg_pad, qg_ref, 0, 2 * hd)
    kv = padded(kv_pad, kv_ref, 0, 2 * hd)
    q, g, k, v = qg[:, :hd], qg[:, hd:], kv[:, :hd], kv[:, hd:]
    own, flat = [], []
    for i in range(NY):
        c = st_ref[i, :SLOT, 2 * hd :].astype(F32)
        own.append((c[:, 0:1], c[:, 1:2] + c[:, 2:3], c[:, 3:4] + c[:, 4:5]))
        r = st_ref[i, SLOT:, :].astype(F32)
        flat.append((r[0:1], r[1:2] + r[2:3], r[3:4] + r[4:5]))
    shares, _, own_delta = combine(own)
    grad_q = jnp.zeros((SLOT, hd), F32)
    for i in range(NY):
        a = st_ref[i, :SLOT, :hd].astype(F32)
        b = st_ref[i, :SLOT, hd : 2 * hd].astype(F32)
        grad_q = grad_q + shares[i] * (a + (own[i][2] - own_delta) * b)
    _, log_total, delta = combine(flat)
    order_q, order_k = orders(idx_ref, cnt_ref, nz, 1)
    allowed = order_k <= order_q
    s = mm(k, q, NT) * scale
    p = jnp.where(allowed, jnp.exp(jnp.where(allowed, s - log_total, NEG)), 0.0)
    ds = (p * (mm(v, g, NT) - delta)).astype(BF)
    grad_k = (mm(ds, q) * scale).astype(BF).reshape(nz, SLOT, hd)
    grad_v = mm(p.astype(BF), g).astype(BF).reshape(nz, SLOT, hd)
    grad_q = grad_q.astype(BF)
    for i in range(nz):
        out_ref[i, :, :hd] = grad_k[i, :cap]
        out_ref[i, :, hd : 2 * hd] = grad_v[i, :cap]
        out_ref[i, :, 2 * hd :] = grad_q[:cap]


def rows_kernel(
    idx_ref, cnt_ref, z_ref, kv_ref, wq_ref, wk_ref, wv_ref, g_ref, w_ref, x_pad, q_pad
):
    nz, cap, hd = z_ref.shape[0], z_ref.shape[1], wq_ref.shape[1]
    heads, _, cols = g_ref.shape
    k = v = jnp.zeros((cap, hd), F32)
    for i in range(nz):
        k = k + z_ref[i, :, :hd].astype(F32)
        v = v + z_ref[i, :, hd : 2 * hd].astype(F32)
    k, v = k.astype(BF), v.astype(BF)
    q = z_ref[idx_ref[0], :, 2 * hd :]
    for c in range(heads):
        part = pl.ds(c * cols, cols)
        g = mm(q, wq_ref[part, :], NT) + mm(k, wk_ref[part, :], NT) + mm(v, wv_ref[part, :], NT)
        g_ref[c] = g.astype(BF)
    x = padded(x_pad, kv_ref, 2 * hd, kv_ref.shape[2])
    grad_q = padded(q_pad, z_ref, 2 * hd, 3 * hd)
    w = mm(x, grad_q, TN)
    w_ref[...] = w.reshape(w_ref.shape).astype(BF)


def finish_kernel(cnt_ref, idx_ref, sel_ref, g_ref, w_ref, h_out, w_out):
    heads, cap, cols = g_ref.shape
    toks = h_out.shape[0]
    block = idx_ref[0] * NY + idx_ref[1]
    acc = jnp.zeros((toks, cols), F32)
    row = lax.broadcasted_iota(jnp.int32, (toks, cap), 0)
    lane = lax.broadcasted_iota(jnp.int32, (toks, cap), 1)
    for h in range(heads):
        hit = (row == sel_ref[h : h + 1, :cap]) & (lane < cnt_ref[h, block])
        acc = acc + mm(jnp.where(hit, 1.0, 0.0).astype(BF), g_ref[h])
    h_out[...] = acc.astype(BF)
    w = w_ref[...].astype(F32)
    w_out[...] = jnp.sum(w, axis=0)


def body(hidden, upstream, w_query, w_key, w_value, w_output, selected, select_count):
    nz, heads = lax.axis_size("z"), lax.axis_size("head")
    z, y, h = lax.axis_index("z"), lax.axis_index("y"), lax.axis_index("head")
    idx = jnp.stack([z, y, h]).astype(jnp.int32)
    toks, cols = hidden.shape
    hd = w_query.shape[2]
    cap = selected.shape[1] // (nz * NY)
    scale = hd ** (-0.5)
    sel = lax.dynamic_slice_in_dim(selected, (z * NY + y) * cap, cap, 1)
    rest = jnp.full((heads, 128 - 2 * cap), -1, jnp.int32)
    sel = jnp.concatenate([sel, sel + toks, rest], axis=1)
    wq, wk, wv, wo = w_query[0], w_key[0], w_value[0], w_output[0]
    count = select_count
    sds = jax.ShapeDtypeStruct

    def swap(x, axis):
        return lax.all_to_all(x, axis, split_axis=0, concat_axis=0, tiled=True)

    picked = call(
        pick_kernel, sds((heads, 2 * cap, cols), BF), (sel, hidden, upstream), [VMEM] * 3
    )
    rows = swap(picked, "head")
    piece = heads * cols // nz
    to_y, to_z = call(
        project_kernel,
        (sds((NY, cap, 2 * hd), BF), sds((nz, cap, 2 * hd + piece), BF)),
        (idx, count, rows, wq, wk, wv, wo),
        [SMEM] * 2 + [VMEM] * 5,
        [pltpu.VMEM((2 * cap, hd), F32)],
    )
    qg, kv = swap(to_y, "y"), swap(to_z, "z")
    pads = [pltpu.VMEM((NY, SLOT, 2 * hd), BF), pltpu.VMEM((nz, SLOT, 2 * hd), BF)]
    part = call(
        functools.partial(partial_kernel, scale),
        sds((NY, SLOT + 16, 3 * hd), BF),
        (idx, count, qg, kv),
        [SMEM] * 2 + [VMEM] * 2,
        pads,
    )
    joined = swap(part, "y")
    grads = call(
        functools.partial(grads_kernel, scale),
        sds((nz, cap, 3 * hd), BF),
        (idx, count, qg, kv, joined),
        [SMEM] * 2 + [VMEM] * 3,
        pads,
    )
    back = swap(grads, "z")
    grad_rows, weight_terms = call(
        rows_kernel,
        (sds((heads, cap, cols), BF), sds((NY, piece // NY, hd), BF)),
        (idx, count, back, kv, wq, wk, wv),
        [SMEM] * 2 + [VMEM] * 5,
        [pltpu.VMEM((nz, SLOT, piece), BF), pltpu.VMEM((nz, SLOT, hd), BF)],
    )
    returned, terms = swap(grad_rows, "head"), swap(weight_terms, "y")
    grad_hidden, grad_query = call(
        finish_kernel,
        (sds((toks, cols), BF), sds((piece // NY, hd), F32)),
        (count, idx, sel, returned, terms),
        [SMEM] * 2 + [VMEM] * 3,
    )
    return grad_hidden, grad_query[None]


def solution(mesh):
    seq, heads = mesh.devices.shape
    fine = Mesh(mesh.devices.reshape(seq // NY, NY, heads), ("z", "y", "head"))
    both = ("z", "y")
    weight = P("head", None, None)
    in_specs = (P(both, "head"), P(both, "head"), weight, weight, weight, weight, P(), P())
    out_specs = (P(both, "head"), P("head", both, None))
    return jax.shard_map(body, mesh=fine, in_specs=in_specs, out_specs=out_specs, check_vma=False)
```

time: 913 us -> 162 us (0.18)
  blocking collectives: 488 us -> 114 us
  waiting for transfers between devices: 207 us -> 13.4 us
  starting transfers between devices: 141 us -> 14.6 us
  local copies, waits for them, and re-layouts: 36.4 us -> 5.9 us
  matrix products: 15 us -> 0 us
  between operations: 15 us -> 0.73 us
  Pallas kernels: 0 us -> 12.1 us
  other arithmetic: 10.2 us -> 0.92 us
    unnamed x1 -> x0, blocking collectives: 372 us -> none
    reduce_scatter x1 -> x0, waiting for transfers between devices: 186 us -> none  [body(): lax.psum_scatter(weight_terms, 'seq', scatter_dimension=0, tiled=True)]
    all_to_all x3 -> x1, starting transfers between devices: 141 us -> 14.6 us  [swap(): return lax.all_to_all(x, axis, split_axis=0, concat_axis=0, tiled=True)]
    all_gather x2 -> x0, blocking collectives: 115 us -> none  [the longest x1 60.2 us: body(): lax.all_gather(keys_loc, 'seq', axis=0, tiled=True)]
    all_to_all x0 -> x6, blocking collectives: none -> 114 us  [swap(): return lax.all_to_all(x, axis, split_axis=0, concat_axis=0, tiled=True)]
    gather x5 -> x0, local copies, waits for them, and re-layouts: 27.1 us -> none  [the longest x1 19.7 us: body(): live_all = slot_ids % capacity < own_count[block_ids]]
    dot_general x14 -> x0, matrix products: 15 us -> none  [the longest x1 2.72 us: body(): lax.dot_general(queries, keys_all, contract_last, preferred_element_type=...]
    pallas_call x0 -> x6, Pallas kernels: none -> 12.1 us  [call(): pl.pallas_call(kernel, out_shape=outs, in_specs=specs, out_specs=jax.tree...]
  transfers between devices with their start and end apart: 4 -> 1, of which waited for: 3 -> 1; matrix products, arithmetic and copies ran while one was open for 4% -> 0% of each run, Pallas kernels for 0% -> 0%
where the time goes in v1:
time: 162 us
  blocking collectives  114 us (70%)
  starting transfers between devices  14.6 us (9%)
  waiting for transfers between devices  13.4 us (8%)
  Pallas kernels  12.1 us (7%)
  local copies, waits for them, and re-layouts  5.9 us (4%)
    all_to_all x6, blocking collectives, swap(): return lax.all_to_all(x, axis, split_axis=0, concat_axis=0, tiled=True)  114 us
    all_to_all x1, starting transfers between devices, swap(): return lax.all_to_all(x, axis, split_axis=0, concat_axis=0, tiled=True)  14.6 us
    all_to_all x1, waiting for transfers between devices, swap(): return lax.all_to_all(x, axis, split_axis=0, concat_axis=0, tiled=True)  13.4 us
    pallas_call x6, Pallas kernels, call(): pl.pallas_call(kernel, out_shape=outs, in_specs=specs, out_specs=jax.tree...  12.1 us
    unnamed x18, local copies, waits for them, and re-layouts  5.82 us
  transfers between devices with their start and end apart: 1, of which 1 were waited for; matrix products, arithmetic and copies ran while one was open for 0% of the time, Pallas kernels for 0%

profile of v1, /device:TPU:1, one launch (start us, length us, event | category | flops | bytes accessed | tf_op | source)
XLA Modules:
  0.0 161.6 jit_solution(13683486526880516462)
XLA Ops:
  0.7 0.1 pad.2.clone
  0.7 0.8 broadcast_add_fusion
  1.5 0.1 add_add_fusion.sel_ref
  1.6 1.0 copy-done.6
  2.6 1.0 copy-done.7
  3.6 1.1 shard_map.95
  4.7 1.0 copy-done.4
  5.7 14.6 %all-to-all-start = ((bf16[8,72,768]{2,1,0:T(8,128)(2,1)}), bf16[8,72,768]{2,1,0:T(8,128)(2,1)}, u32[]{:S(2)}, u32[]{:S(2)}) async-start(bf16[8,72,768]{2,1,0:T(8,128)(2,1)} %copy-done.4), calls=%async_computation | async-start | bytes 1769472 | tf_op jit(solution)/shard_map/all_to_all | solution.py:244
  20.3 0.1 pad_add_fusion.idx_ref
  20.4 13.4 %all-to-all-done.r_ref = bf16[8,72,768]{2,1,0:T(8,128)(2,1)} async-done(((bf16[8,72,768]{2,1,0:T(8,128)(2,1)}), bf16[8,72,768]{2,1,0:T(8,128)(2,1)}, u32[]{:S(2)}, u32[]{:S(2)}) %all-to-all-start) | async-done | bytes 884768 | tf_op jit(solution)/shard_map/all_to_all | solution.py:244
  33.8 0.0 copy-start.2
  33.8 1.4 copy-done.2
  35.2 1.4 copy-done.5
  36.6 2.5 %shard_map.96 = (bf16[8,36,256]{2,1,0:T(8,128)(2,1)S(1)}, bf16[12,36,768]{2,1,0:T(8,128)(2,1)S(1)}) custom-call(s32[3]{0:T(128)S(1)} %pad_add_fusion.idx_ref, s32[8,96]{1,0:T(8,128)S(1)} %copy-done.8, bf16[8,72,768]{2,1,0:T(8,128)(2,1)} %all-to-all-done.r_ref, bf16[6144,128]{1,0:T(8,128)(2,1)S(1)} %bitcast.8, bf16[6144,128]{1,0:T(8,128)(2,1)S(1)} %bitcast.10, ...), custom_call_target="tpu_custom_call" | custom-call | tf_op jit(solution)/shard_map/pallas_call | solution.py:27
  39.1 10.6 %all_to_all.35.qg_ref = bf16[8,36,256]{2,1,0:T(8,128)(2,1)S(1)} all-to-all(bf16[8,36,256]{2,1,0:T(8,128)(2,1)S(1)} %get-tuple-element.8), channel_id=1, replica_groups=mesh['z'=12,'y'=8,'head'=8] {'y'}, dimensions={0} | all-to-all | bytes 294912 | tf_op jit(solution)/shard_map/all_to_all | solution.py:244
  49.8 37.0 %all_to_all.36.kv_ref = bf16[12,36,768]{2,1,0:T(8,128)(2,1)S(1)} all-to-all(bf16[12,36,768]{2,1,0:T(8,128)(2,1)S(1)} %get-tuple-element.9), channel_id=1, replica_groups=mesh['z'=12,'y'=8,'head'=8] {'z'}, dimensions={0} | all-to-all | bytes 1327104 | tf_op jit(solution)/shard_map/all_to_all | solution.py:244
  86.8 1.9 %shard_map.97 = bf16[8,64,384]{2,1,0:T(8,128)(2,1)S(1)} custom-call(s32[3]{0:T(128)S(1)} %pad_add_fusion.idx_ref, s32[8,96]{1,0:T(8,128)S(1)} %copy-done.8, bf16[8,36,256]{2,1,0:T(8,128)(2,1)S(1)} %all_to_all.35.qg_ref, bf16[12,36,768]{2,1,0:T(8,128)(2,1)S(1)} %all_to_all.36.kv_ref), custom_call_target="tpu_custom_call" | custom-call | tf_op jit(solution)/shard_map/pallas_call | solution.py:27
  88.7 14.6 %all_to_all.37.st_ref = bf16[8,64,384]{2,1,0:T(8,128)(2,1)S(1)} all-to-all(bf16[8,64,384]{2,1,0:T(8,128)(2,1)S(1)} %shard_map.97), channel_id=1, replica_groups=mesh['z'=12,'y'=8,'head'=8] {'y'}, dimensions={0} | all-to-all | bytes 786432 | tf_op jit(solution)/shard_map/all_to_all | solution.py:244
  103.3 1.7 %shard_map.98 = bf16[12,36,384]{2,1,0:T(8,128)(2,1)S(1)} custom-call(s32[3]{0:T(128)S(1)} %pad_add_fusion.idx_ref, s32[8,96]{1,0:T(8,128)S(1)} %copy-done.8, bf16[8,36,256]{2,1,0:T(8,128)(2,1)S(1)} %all_to_all.35.qg_ref, bf16[12,36,768]{2,1,0:T(8,128)(2,1)S(1)} %all_to_all.36.kv_ref, bf16[8,64,384]{2,1,0:T(8,128)(2,1)S(1)} %all_to_all.37.st_ref), custom_call_target="tpu_custom_call" | custom-call | tf_op jit(solution)/shard_map/pallas_call | solution.py:27
  105.0 23.5 %all_to_all.38.z_ref = bf16[12,36,384]{2,1,0:T(8,128)(2,1)S(1)} all-to-all(bf16[12,36,384]{2,1,0:T(8,128)(2,1)S(1)} %shard_map.98), channel_id=1, replica_groups=mesh['z'=12,'y'=8,'head'=8] {'z'}, dimensions={0} | all-to-all | bytes 663552 | tf_op jit(solution)/shard_map/all_to_all | solution.py:244
  128.5 2.5 %shard_map.99 = (bf16[8,36,768]{2,1,0:T(8,128)(2,1)S(1)}, bf16[8,64,128]{2,1,0:T(8,128)(2,1)S(1)}) custom-call(s32[3]{0:T(128)S(1)} %pad_add_fusion.idx_ref, s32[8,96]{1,0:T(8,128)S(1)} %copy-done.8, bf16[12,36,384]{2,1,0:T(8,128)(2,1)S(1)} %all_to_all.38.z_ref, bf16[12,36,768]{2,1,0:T(8,128)(2,1)S(1)} %all_to_all.36.kv_ref, bf16[6144,128]{1,0:T(8,128)(2,1)S(1)} %bitcast.9, ...), custom_call_target="tpu_custom_call" | custom-call | tf_op jit(solution)/shard_map/pallas_call | solution.py:27
  131.0 12.8 %all_to_all.39.w_ref = bf16[8,64,128]{2,1,0:T(8,128)(2,1)S(1)} all-to-all(bf16[8,64,128]{2,1,0:T(8,128)(2,1)S(1)} %get-tuple-element.11), channel_id=1, replica_groups=mesh['z'=12,'y'=8,'head'=8] {'y'}, dimensions={0} | all-to-all | bytes 262144 | tf_op jit(solution)/shard_map/all_to_all | solution.py:244
  143.8 15.5 %all_to_all.40.g_ref = bf16[8,36,768]{2,1,0:T(8,128)(2,1)S(1)} all-to-all(bf16[8,36,768]{2,1,0:T(8,128)(2,1)S(1)} %get-tuple-element.10), channel_id=1, replica_groups=mesh['z'=12,'y'=8,'head'=8] {'head'}, dimensions={0} | all-to-all | bytes 884736 | tf_op jit(solution)/shard_map/all_to_all | solution.py:244
  159.2 2.4 %shard_map.100 = (bf16[288,768]{1,0:T(8,128)(2,1)}, f32[64,128]{1,0:T(8,128)}) custom-call(s32[8,96]{1,0:T(8,128)S(1)} %copy-done.8, s32[3]{0:T(128)S(1)} %pad_add_fusion.idx_ref, s32[8,128]{1,0:T(8,128)S(1)} %add_add_fusion.sel_ref, bf16[8,36,768]{2,1,0:T(8,128)(2,1)S(1)} %all_to_all.40.g_ref, bf16[8,64,128]{2,1,0:T(8,128)(2,1)S(1)} %all_to_all.39.w_ref), custom_call_target="tpu_custom_call" | custom-call | tf_op jit(solution)/shard_map/pallas_call | solution.py:27
  (13 shorter events, 0.0 us)
Async XLA Ops:
  1.6 1.0 copy-start.6
  2.6 1.0 copy-start.7
  3.6 30.2 %copy-start = (bf16[1,6144,128]{2,1,0:T(8,128)(2,1)S(1)}, bf16[1,6144,128]{2,1,0:T(8,128)(2,1)}, u32[]{:S(2)}) copy-start(bf16[1,6144,128]{2,1,0:T(8,128)(2,1)} %param.10) | copy-start | bytes 4718596
  3.6 30.2 %copy-start.1 = (bf16[1,6144,128]{2,1,0:T(8,128)(2,1)S(1)}, bf16[1,6144,128]{2,1,0:T(8,128)(2,1)}, u32[]{:S(2)}) copy-start(bf16[1,6144,128]{2,1,0:T(8,128)(2,1)} %param.11) | copy-start | bytes 4718596
  3.6 30.2 %copy-start.8 = (s32[8,96]{1,0:T(8,128)S(1)}, s32[8,96]{1,0:T(8,128)}, u32[]{:S(2)}) copy-start(s32[8,96]{1,0:T(8,128)} %cnt_ref.9) | copy-start | bytes 9220
  4.7 1.0 copy-start.4
  5.7 28.1 %all-to-all-start = ((bf16[8,72,768]{2,1,0:T(8,128)(2,1)}), bf16[8,72,768]{2,1,0:T(8,128)(2,1)}, u32[]{:S(2)}, u32[]{:S(2)}) async-start(bf16[8,72,768]{2,1,0:T(8,128)(2,1)} %copy-done.4), calls=%async_computation | async-start | bytes 1769472 | tf_op jit(solution)/shard_map/all_to_all | solution.py:244
  33.8 1.4 copy-start.2
  35.2 1.4 copy-start.5
  88.7 39.8 %copy-start.3 = (bf16[1,6144,128]{2,1,0:T(8,128)(2,1)S(1)}, bf16[1,6144,128]{2,1,0:T(8,128)(2,1)}, u32[]{:S(2)}) copy-start(bf16[1,6144,128]{2,1,0:T(8,128)(2,1)} %param.12) | copy-start | bytes 4718596

commit v2 on v1

v2 whole, which is shorter than its diff:
```python
import functools

import jax
import jax.numpy as jnp
from jax import lax
from jax.experimental import pallas as pl
from jax.experimental.pallas import tpu as pltpu
from jax.sharding import Mesh, PartitionSpec as P

NY = 8
SLOT = 48
WIDE = 256
NEG = -1e30
BF = jnp.bfloat16
F32 = jnp.float32
VMEM = pl.BlockSpec(memory_space=pltpu.VMEM)
SMEM = pl.BlockSpec(memory_space=pltpu.SMEM)
HBM = pl.BlockSpec(memory_space=pl.ANY)
NN = (((1,), (0,)), ((), ()))
NT = (((1,), (1,)), ((), ()))
TN = (((0,), (0,)), ((), ()))


def mm(a, b, dims=NN):
    return lax.dot_general(a, b, dims, preferred_element_type=F32)


def call(kernel, outs, args, specs, scratch=(), limit=16):
    return pl.pallas_call(
        kernel,
        out_shape=outs,
        in_specs=specs,
        out_specs=jax.tree.map(lambda _: VMEM, outs),
        scratch_shapes=list(scratch),
        compiler_params=pltpu.CompilerParams(vmem_limit_bytes=limit << 20),
    )(*args)


def pick_kernel(idx_ref, sel_ref, hid_ref, up_ref, out_ref, mine_ref, table, sems):
    heads, rows, cols = out_ref.shape
    cap, toks = rows // 2, hid_ref.shape[0]
    part = toks // 3
    copies = []
    for i, src in enumerate((hid_ref, up_ref)):
        for j in range(3):
            at = pl.ds(j * part, part)
            dst = table.at[pl.ds(i * toks + j * part, part)]
            copies.append(pltpu.make_async_copy(src.at[at], dst, sems.at[3 * i + j]))
    for copy in copies:
        copy.start()
    start = (idx_ref[0] * NY + idx_ref[1]) * cap
    aligned = jnp.minimum(start // 128 * 128, sel_ref.shape[1] - WIDE)
    window = sel_ref[:, pl.ds(pl.multiple_of(aligned, 128), WIDE)]
    shift = lax.rem(WIDE - (start - aligned), WIDE)
    low = pltpu.roll(window, shift, 1)[:, :128]
    high = pltpu.roll(low, cap, 1) + toks
    lane = lax.broadcasted_iota(jnp.int32, (heads, 128), 1)
    mine = jnp.where(lane < cap, low, high)
    mine_ref[...] = mine
    sel_t = mine.astype(F32).T
    target = jnp.concatenate([sel_t[:rows, h : h + 1] for h in range(heads)], axis=0)
    target = target.astype(jnp.int32)
    lane = lax.broadcasted_iota(jnp.int32, (heads * rows, 2 * toks), 1)
    onehot = jnp.where(lane == target, 1.0, 0.0).astype(BF)
    for copy in copies:
        copy.wait()
    out_ref[...] = mm(onehot, table[...]).reshape(heads, rows, cols).astype(BF)


def pack_kernel(wq_ref, wk_ref, wv_ref, wo_ref, w_ref):
    hd = wq_ref.shape[1]
    w_ref[:, :hd] = wq_ref[...]
    w_ref[:, hd : 2 * hd] = wk_ref[...]
    w_ref[:, 2 * hd : 3 * hd] = wv_ref[...]
    w_ref[:, 3 * hd :] = wo_ref[...].T


def project_kernel(idx_ref, cnt_ref, r_ref, w_ref, z_ref, y_ref, acc):
    heads, rows, cols = r_ref.shape
    cap, hd = rows // 2, w_ref.shape[1] // 4
    total = jnp.zeros((rows, 4 * hd), F32)
    for c in range(heads):
        total = total + mm(r_ref[c], w_ref[pl.ds(c * cols, cols), :])
    acc[...] = total[:, 3 * hd :]
    g = acc[cap:, :]
    count = cnt_ref[idx_ref[2], idx_ref[0] * NY + idx_ref[1]]
    row = lax.broadcasted_iota(jnp.int32, (cap, hd), 0)
    g = jnp.where(row < count, g, 0.0).astype(BF)
    qkv = total[:SLOT, : 3 * hd].astype(BF)[:cap]
    nz = z_ref.shape[0]
    for i in range(nz):
        z_ref[i, :, :hd] = qkv[:, :hd]
        z_ref[i, :, hd:] = g
    wide = heads * cols // (nz * NY)
    for i in range(NY):
        y_ref[i, :, : 2 * hd] = qkv[:, hd:]
        chunks = []
        for j in range(nz):
            c, off = divmod((j * NY + i) * wide, cols)
            base = off // 128 * 128
            aligned = r_ref[c, :, base : base + 128]
            chunks.append(aligned[:cap, off - base : off - base + wide])
        y_ref[i, :, 2 * hd :] = jnp.concatenate(chunks, axis=1)


def padded(pad_ref, ref, lo, hi):
    n, cap = ref.shape[0], ref.shape[1]
    w = hi - lo
    pad_ref[:, SLOT - 16 :, :] = jnp.zeros((n, 16, w), BF)
    for i in range(n):
        pad_ref[i, :cap, :] = ref[i, :, lo:hi]
    return pad_ref[...].reshape(n * SLOT, w)


def orders(idx_ref, cnt_ref, nz, axis_q):
    z, y, h = idx_ref[0], idx_ref[1], idx_ref[2]

    def one(n, axis, block_of, dead):
        shape = (n * SLOT, 1) if axis == 0 else (1, n * SLOT)
        at = lax.broadcasted_iota(jnp.int32, shape, axis)
        out = jnp.full(shape, dead, jnp.int32)
        for i in range(n):
            b = block_of(i)
            c = at - i * SLOT
            live = (c >= 0) & (c < cnt_ref[h, b])
            out = jnp.where(live, c + b * SLOT, out)
        return out

    order_q = one(nz, axis_q, lambda i: i * NY + y, -1)
    order_k = one(NY, 1 - axis_q, lambda i: z * NY + i, 1 << 30)
    return order_q, order_k


def split(x):
    hi = x.astype(BF).astype(F32)
    return hi, x - hi


def partial_kernel(scale, idx_ref, cnt_ref, qg_ref, kv_ref, out_ref, qg_pad, kv_pad):
    nz, cap, hd = qg_ref.shape[0], qg_ref.shape[1], qg_ref.shape[2] // 2
    qg = padded(qg_pad, qg_ref, 0, 2 * hd)
    kv = padded(kv_pad, kv_ref, 0, 2 * hd)
    q, g, k, v = qg[:, :hd], qg[:, hd:], kv[:, :hd], kv[:, hd:]
    order_q, order_k = orders(idx_ref, cnt_ref, nz, 0)
    allowed = order_k <= order_q
    s = jnp.where(allowed, mm(q, k, NT) * scale, NEG)
    top = jnp.max(s, axis=1, keepdims=True)
    e = jnp.where(allowed, jnp.exp(s - top), 0.0)
    total = jnp.sum(e, axis=1, keepdims=True)
    total = jnp.where(total > 0.0, total, 1.0)
    p = e * (1.0 / total)
    gp = mm(g, v, NT)
    delta = jnp.sum(p * gp, axis=1, keepdims=True)
    a = mm((p * (gp - delta)).astype(BF), k) * scale
    b = mm(p.astype(BF), k) * scale
    own = jnp.concatenate([a, b], axis=1).astype(BF)
    n = nz * SLOT
    lane = lax.broadcasted_iota(jnp.int32, (n, 128), 1) % 4
    stats = jnp.zeros((n, 128), F32)
    for i, col in enumerate(split(top + jnp.log(total)) + split(delta)):
        stats = jnp.where(lane == i, col, stats)
    whole = -(-n // WIDE) * WIDE
    if whole > n:
        stats = jnp.concatenate([stats, jnp.zeros((whole - n, 128), F32)], axis=0)
    stats = stats.T[:16, :]
    row = lax.broadcasted_iota(jnp.int32, (16, WIDE), 0) // 4
    flat = jnp.zeros((16, WIDE), F32)
    for j in range(whole // WIDE):
        flat = jnp.where(row == j, stats[:, j * WIDE : (j + 1) * WIDE], flat)
    flat = flat.astype(BF)
    for i in range(nz):
        out_ref[i, :16, :] = flat
        out_ref[i, 16:, :] = own[i * SLOT : (i + 1) * SLOT, :][:cap]


def grads_kernel(
    scale, idx_ref, cnt_ref, qg_ref, kv_ref, st_ref, out_ref, qg_pad, kv_pad, turn
):
    nz, cap, hd = qg_ref.shape[0], qg_ref.shape[1], qg_ref.shape[2] // 2
    n = nz * SLOT
    qg = padded(qg_pad, qg_ref, 0, 2 * hd)
    kv = padded(kv_pad, kv_ref, 0, 2 * hd)
    q, g, k, v = qg[:, :hd], qg[:, hd:], kv[:, :hd], kv[:, hd:]
    chunks = -(-n // WIDE)
    logs, deltas = [], []
    for i in range(nz):
        r = st_ref[i, :16, :].astype(F32)
        line = [jnp.concatenate([r[4 * j + s : 4 * j + s + 1] for j in range(chunks)], axis=1) for s in range(4)]
        logs.append(line[0] + line[1])
        deltas.append(line[2] + line[3])
    top = functools.reduce(jnp.maximum, logs)
    weights = [jnp.exp(x - top) for x in logs]
    total = functools.reduce(jnp.add, weights)
    shares = [w / total for w in weights]
    delta = functools.reduce(jnp.add, [w * d for w, d in zip(shares, deltas)])
    log_total = (top + jnp.log(total))[:, :n]
    width = chunks * WIDE
    lines = shares + [d - delta for d in deltas] + [jnp.zeros((128 - 2 * nz, width), F32)]
    turn[...] = jnp.concatenate(lines, axis=0).T
    delta = delta[:, :n]
    mine = turn[pl.ds(pl.multiple_of(idx_ref[0] * SLOT, SLOT), SLOT), :]
    grad_q = jnp.zeros((cap, hd), F32)
    for i in range(nz):
        a = st_ref[i, 16:, :hd].astype(F32)
        b = st_ref[i, 16:, hd:].astype(F32)
        grad_q = grad_q + mine[:cap, i : i + 1] * (a + mine[:cap, nz + i : nz + i + 1] * b)
    order_q, order_k = orders(idx_ref, cnt_ref, nz, 1)
    allowed = order_k <= order_q
    s = mm(k, q, NT) * scale
    p = jnp.where(allowed, jnp.exp(jnp.where(allowed, s - log_total, NEG)), 0.0)
    ds = (p * (mm(v, g, NT) - delta)).astype(BF)
    grad_k = (mm(ds, q) * scale).astype(BF).reshape(NY, SLOT, hd)
    grad_v = mm(p.astype(BF), g).astype(BF).reshape(NY, SLOT, hd)
    grad_q = grad_q.astype(BF)
    for i in range(NY):
        out_ref[i, :, :hd] = grad_k[i, :cap]
        out_ref[i, :, hd : 2 * hd] = grad_v[i, :cap]
        out_ref[i, :, 2 * hd :] = grad_q


def rows_kernel(idx_ref, back_ref, kv_ref, w_ref, g_ref, t_ref, x_pad, q_pad):
    heads, cap, cols = g_ref.shape
    hd = w_ref.shape[1] // 4
    kv = jnp.zeros((cap, 2 * hd), F32)
    for i in range(NY):
        kv = kv + back_ref[i, :, : 2 * hd].astype(F32)
    qkv = jnp.concatenate([back_ref[idx_ref[1], :, 2 * hd :], kv.astype(BF)], axis=1)
    x = padded(x_pad, kv_ref, 2 * hd, kv_ref.shape[2])
    grad_q = padded(q_pad, back_ref, 2 * hd, 3 * hd)
    t_ref[...] = mm(x, grad_q, TN).reshape(t_ref.shape).astype(BF)
    for c in range(heads):
        g_ref[c] = mm(qkv, w_ref[pl.ds(c * cols, cols), : 3 * hd], NT).astype(BF)


def finish_kernel(idx_ref, cnt_ref, sel_ref, g_ref, t_ref, h_out, w_out):
    heads, cap, cols = g_ref.shape
    toks = h_out.shape[0]
    block = idx_ref[0] * NY + idx_ref[1]
    acc = jnp.zeros((toks, cols), F32)
    row = lax.broadcasted_iota(jnp.int32, (toks, cap), 0)
    lane = lax.broadcasted_iota(jnp.int32, (toks, cap), 1)
    for h in range(heads):
        hit = (row == sel_ref[h : h + 1, :cap]) & (lane < cnt_ref[h, block])
        acc = acc + mm(jnp.where(hit, 1.0, 0.0).astype(BF), g_ref[h])
    h_out[...] = acc.astype(BF)
    w_out[...] = jnp.sum(t_ref[...].astype(F32), axis=0)


def body(hidden, upstream, w_query, w_key, w_value, w_output, selected, select_count):
    nz, heads = lax.axis_size("z"), lax.axis_size("head")
    idx = jnp.stack([lax.axis_index(a) for a in ("z", "y", "head")]).astype(jnp.int32)
    toks, cols = hidden.shape
    hd = w_query.shape[2]
    cap = selected.shape[1] // (nz * NY)
    scale = hd ** (-0.5)
    count = select_count
    sds = jax.ShapeDtypeStruct

    def swap(x, axis):
        return lax.all_to_all(x, axis, split_axis=0, concat_axis=0, tiled=True)

    picked, mine = call(
        pick_kernel,
        (sds((heads, 2 * cap, cols), BF), sds((heads, 128), jnp.int32)),
        (idx, selected, hidden, upstream),
        [SMEM, VMEM, HBM, HBM],
        [pltpu.VMEM((2 * toks, cols), BF), pltpu.SemaphoreType.DMA((6,))],
    )
    rows = swap(picked, "head")
    tall = pl.BlockSpec((cols, hd), lambda i: (i, 0))
    weights = pl.pallas_call(
        pack_kernel,
        grid=(heads,),
        out_shape=sds((heads * cols, 4 * hd), BF),
        in_specs=[tall, tall, tall, pl.BlockSpec((hd, cols), lambda i: (0, i))],
        out_specs=pl.BlockSpec((cols, 4 * hd), lambda i: (i, 0)),
        compiler_params=pltpu.CompilerParams(vmem_limit_bytes=8 << 20),
        cost_estimate=pl.CostEstimate(
            flops=0, bytes_accessed=16 * heads * cols * hd, transcendentals=0
        ),
    )(w_query[0], w_key[0], w_value[0], w_output[0])
    piece = heads * cols // NY
    to_z, to_y = call(
        project_kernel,
        (sds((nz, cap, 2 * hd), BF), sds((NY, cap, 2 * hd + piece), BF)),
        (idx, count, rows, weights),
        [SMEM] * 2 + [VMEM] * 2,
        [pltpu.VMEM((2 * cap, hd), F32)],
    )
    qg, kv = swap(to_z, "z"), swap(to_y, "y")
    pads = [pltpu.VMEM((nz, SLOT, 2 * hd), BF), pltpu.VMEM((NY, SLOT, 2 * hd), BF)]
    part = call(
        functools.partial(partial_kernel, scale),
        sds((nz, cap + 16, 2 * hd), BF),
        (idx, count, qg, kv),
        [SMEM] * 2 + [VMEM] * 2,
        pads,
    )
    joined = swap(part, "z")
    grads = call(
        functools.partial(grads_kernel, scale),
        sds((NY, cap, 3 * hd), BF),
        (idx, count, qg, kv, joined),
        [SMEM] * 2 + [VMEM] * 3,
        pads + [pltpu.VMEM((-(-nz * SLOT // WIDE) * WIDE, 128), F32)],
    )
    back = swap(grads, "y")
    grad_rows, weight_terms = call(
        rows_kernel,
        (sds((heads, cap, cols), BF), sds((nz, piece // nz, hd), BF)),
        (idx, back, kv, weights),
        [SMEM] + [VMEM] * 3,
        [pltpu.VMEM((NY, SLOT, piece), BF), pltpu.VMEM((NY, SLOT, hd), BF)],
    )
    returned, terms = swap(grad_rows, "head"), swap(weight_terms, "z")
    grad_hidden, grad_query = call(
        finish_kernel,
        (sds((toks, cols), BF), sds((piece // nz, hd), F32)),
        (idx, count, mine, returned, terms),
        [SMEM] * 2 + [VMEM] * 3,
    )
    return grad_hidden, grad_query[None]


def solution(mesh):
    seq, heads = mesh.devices.shape
    fine = Mesh(mesh.devices.reshape(seq // NY, NY, heads), ("z", "y", "head"))
    both = ("z", "y")
    weight = P("head", None, None)
    in_specs = (P(both, "head"), P(both, "head"), weight, weight, weight, weight, P(), P())
    out_specs = (P(both, "head"), P("head", both, None))
    return jax.shard_map(body, mesh=fine, in_specs=in_specs, out_specs=out_specs, check_vma=False)
```

time: 162 us -> 160 us (0.988)
  waiting for transfers between devices: 13.4 us -> 5.15 us
  local copies, waits for them, and re-layouts: 5.9 us -> 12.7 us
  Pallas kernels: 12.1 us -> 15.6 us
  blocking collectives: 114 us -> 111 us
    all_to_all x1, waiting for transfers between devices: 13.4 us -> 5.15 us  [swap(): return lax.all_to_all(x, axis, split_axis=0, concat_axis=0, tiled=True)]
    unnamed x18 -> x22, local copies, waits for them, and re-layouts: 5.82 us -> 12.7 us
    all_to_all x6, blocking collectives: 114 us -> 111 us  [swap(): return lax.all_to_all(x, axis, split_axis=0, concat_axis=0, tiled=True)]
    pallas_call x6, Pallas kernels: 12.1 us -> 14.3 us  [call(): pl.pallas_call(kernel, out_shape=outs, in_specs=specs, out_specs=jax.tree...]
  transfers between devices with their start and end apart: 1 -> 1, of which waited for: 1 -> 1; matrix products, arithmetic and copies ran while one was open for 0% -> 0% of each run, Pallas kernels for 0% -> 1%
where the time goes in v2:
time: 160 us; the launch traced here: 159 us
  blocking collectives  111 us (69%)
  Pallas kernels  15.6 us (10%)
  starting transfers between devices  14 us (9%)
  local copies, waits for them, and re-layouts  12.7 us (8%)
  waiting for transfers between devices  5.15 us (3%)
    all_to_all x6, blocking collectives, swap(): return lax.all_to_all(x, axis, split_axis=0, concat_axis=0, tiled=True)  111 us
    pallas_call x6, Pallas kernels, call(): pl.pallas_call(kernel, out_shape=outs, in_specs=specs, out_specs=jax.tree...  14.3 us
    all_to_all x1, starting transfers between devices, swap(): return lax.all_to_all(x, axis, split_axis=0, concat_axis=0, tiled=True)  14 us
    unnamed x22, local copies, waits for them, and re-layouts  12.7 us
    all_to_all x1, waiting for transfers between devices, swap(): return lax.all_to_all(x, axis, split_axis=0, concat_axis=0, tiled=True)  5.15 us
  transfers between devices with their start and end apart: 1, of which 1 were waited for; matrix products, arithmetic and copies ran while one was open for 0% of the time, Pallas kernels for 1%

profile of v2, /device:TPU:1, one launch (start us, length us, event | category | flops | bytes accessed | tf_op | source)
XLA Modules:
  0.0 158.7 jit_solution(14430675054645736506)
XLA Ops:
  0.7 0.1 pad_add_fusion.idx_ref
  0.7 1.1 copy-done.7
  1.8 1.0 copy-done.8
  2.9 0.9 copy-done.9
  3.8 4.1 %shard_map.95 = (bf16[8,72,768]{2,1,0:T(8,128)(2,1)}, s32[8,128]{1,0:T(8,128)S(1)}) custom-call(s32[3]{0:T(128)S(1)} %pad_add_fusion.idx_ref, s32[8,3456]{1,0:T(8,128)S(1)} %copy-done.9, bf16[288,768]{1,0:T(8,128)(2,1)S(1)} %copy-done.7, bf16[288,768]{1,0:T(8,128)(2,1)S(1)} %copy-done.8), custom_call_target="tpu_custom_call" | custom-call | tf_op jit(solution)/shard_map/pallas_call | solution.py:29
  7.8 14.0 %all-to-all-start = ((bf16[8,72,768]{2,1,0:T(8,128)(2,1)}), bf16[8,72,768]{2,1,0:T(8,128)(2,1)S(1)}, u32[]{:S(2)}, u32[]{:S(2)}) async-start(bf16[8,72,768]{2,1,0:T(8,128)(2,1)} %get-tuple-element.11), calls=%async_computation | async-start | bytes 1769472 | tf_op jit(solution)/shard_map/all_to_all | solution.py:260
  21.8 1.4 copy-done.4
  23.2 1.4 copy-done.5
  24.6 1.4 copy-done.6
  26.1 1.3 shard_map.96.w_ref
  27.4 2.7 %copy-done = bf16[6144,512]{1,0:T(8,128)(2,1)} copy-done((bf16[6144,512]{1,0:T(8,128)(2,1)}, bf16[6144,512]{1,0:T(8,128)(2,1)S(1)}, u32[]{:S(2)}) %copy-start) | copy-done | bytes 6291480
  30.0 5.1 %all-to-all-done.r_ref = bf16[8,72,768]{2,1,0:T(8,128)(2,1)S(1)} async-done(((bf16[8,72,768]{2,1,0:T(8,128)(2,1)}), bf16[8,72,768]{2,1,0:T(8,128)(2,1)S(1)}, u32[]{:S(2)}, u32[]{:S(2)}) %all-to-all-start) | async-done | bytes 884768 | tf_op jit(solution)/shard_map/all_to_all | solution.py:260
  35.2 2.8 %copy-done.1 = bf16[6144,512]{1,0:T(8,128)(2,1)S(1)} copy-done((bf16[6144,512]{1,0:T(8,128)(2,1)S(1)}, bf16[6144,512]{1,0:T(8,128)(2,1)}, u32[]{:S(2)}) %copy-start.1) | copy-done | bytes 6291480
  38.0 1.8 %shard_map.97 = (bf16[12,36,256]{2,1,0:T(8,128)(2,1)S(1)}, bf16[8,36,1024]{2,1,0:T(8,128)(2,1)S(1)}) custom-call(s32[3]{0:T(128)S(1)} %pad_add_fusion.idx_ref, s32[8,96]{1,0:T(8,128)S(1)} %copy-done.10, bf16[8,72,768]{2,1,0:T(8,128)(2,1)S(1)} %all-to-all-done.r_ref, bf16[6144,512]{1,0:T(8,128)(2,1)S(1)} %copy-done.1), custom_call_target="tpu_custom_call" | custom-call | tf_op jit(solution)/shard_map/pallas_call | solution.py:29
  39.8 19.5 %all_to_all.35.qg_ref = bf16[12,36,256]{2,1,0:T(8,128)(2,1)S(1)} all-to-all(bf16[12,36,256]{2,1,0:T(8,128)(2,1)S(1)} %get-tuple-element.12), channel_id=1, replica_groups=mesh['z'=12,'y'=8,'head'=8] {'z'}, dimensions={0} | all-to-all | bytes 442368 | tf_op jit(solution)/shard_map/all_to_all | solution.py:260
  59.3 22.9 %all_to_all.36.kv_ref = bf16[8,36,1024]{2,1,0:T(8,128)(2,1)S(1)} all-to-all(bf16[8,36,1024]{2,1,0:T(8,128)(2,1)S(1)} %get-tuple-element.13), channel_id=1, replica_groups=mesh['z'=12,'y'=8,'head'=8] {'y'}, dimensions={0} | all-to-all | bytes 1179648 | tf_op jit(solution)/shard_map/all_to_all | solution.py:260
  82.2 1.9 %shard_map.98 = bf16[12,52,256]{2,1,0:T(8,128)(2,1)S(1)} custom-call(s32[3]{0:T(128)S(1)} %pad_add_fusion.idx_ref, s32[8,96]{1,0:T(8,128)S(1)} %copy-done.10, bf16[12,36,256]{2,1,0:T(8,128)(2,1)S(1)} %all_to_all.35.qg_ref, bf16[8,36,1024]{2,1,0:T(8,128)(2,1)S(1)} %all_to_all.36.kv_ref), custom_call_target="tpu_custom_call" | custom-call | tf_op jit(solution)/shard_map/pallas_call | solution.py:29
  84.1 22.7 %all_to_all.37.st_ref = bf16[12,52,256]{2,1,0:T(8,128)(2,1)S(1)} all-to-all(bf16[12,52,256]{2,1,0:T(8,128)(2,1)S(1)} %shard_map.98), channel_id=1, replica_groups=mesh['z'=12,'y'=8,'head'=8] {'z'}, dimensions={0} | all-to-all | bytes 638976 | tf_op jit(solution)/shard_map/all_to_all | solution.py:260
  106.8 1.7 %shard_map.99 = bf16[8,36,384]{2,1,0:T(8,128)(2,1)S(1)} custom-call(s32[3]{0:T(128)S(1)} %pad_add_fusion.idx_ref, s32[8,96]{1,0:T(8,128)S(1)} %copy-done.10, bf16[12,36,256]{2,1,0:T(8,128)(2,1)S(1)} %all_to_all.35.qg_ref, bf16[8,36,1024]{2,1,0:T(8,128)(2,1)S(1)} %all_to_all.36.kv_ref, bf16[12,52,256]{2,1,0:T(8,128)(2,1)S(1)} %all_to_all.37.st_ref), custom_call_target="tpu_custom_call" | custom-call | tf_op jit(solution)/shard_map/pallas_call | solution.py:29
  108.5 13.7 %all_to_all.38.back_ref = bf16[8,36,384]{2,1,0:T(8,128)(2,1)S(1)} all-to-all(bf16[8,36,384]{2,1,0:T(8,128)(2,1)S(1)} %shard_map.99), channel_id=1, replica_groups=mesh['z'=12,'y'=8,'head'=8] {'y'}, dimensions={0} | all-to-all | bytes 442368 | tf_op jit(solution)/shard_map/all_to_all | solution.py:260
  122.2 2.3 %shard_map.100 = (bf16[8,36,768]{2,1,0:T(8,128)(2,1)S(1)}, bf16[12,64,128]{2,1,0:T(8,128)(2,1)S(1)}) custom-call(s32[3]{0:T(128)S(1)} %pad_add_fusion.idx_ref, bf16[8,36,384]{2,1,0:T(8,128)(2,1)S(1)} %all_to_all.38.back_ref, bf16[8,36,1024]{2,1,0:T(8,128)(2,1)S(1)} %all_to_all.36.kv_ref, bf16[6144,512]{1,0:T(8,128)(2,1)S(1)} %copy-done.2), custom_call_target="tpu_custom_call" | custom-call | tf_op jit(solution)/shard_map/pallas_call | solution.py:29
  124.6 15.7 %all_to_all.39.g_ref = bf16[8,36,768]{2,1,0:T(8,128)(2,1)S(1)} all-to-all(bf16[8,36,768]{2,1,0:T(8,128)(2,1)S(1)} %get-tuple-element.14), channel_id=1, replica_groups=mesh['z'=12,'y'=8,'head'=8] {'head'}, dimensions={0} | all-to-all | bytes 884736 | tf_op jit(solution)/shard_map/all_to_all | solution.py:260
  140.2 16.1 %all_to_all.40.t_ref = bf16[12,64,128]{2,1,0:T(8,128)(2,1)S(1)} all-to-all(bf16[12,64,128]{2,1,0:T(8,128)(2,1)S(1)} %get-tuple-element.15), channel_id=1, replica_groups=mesh['z'=12,'y'=8,'head'=8] {'z'}, dimensions={0} | all-to-all | bytes 393216 | tf_op jit(solution)/shard_map/all_to_all | solution.py:260
  156.3 2.4 %shard_map.101 = (bf16[288,768]{1,0:T(8,128)(2,1)}, f32[64,128]{1,0:T(8,128)}) custom-call(s32[3]{0:T(128)S(1)} %pad_add_fusion.idx_ref, s32[8,96]{1,0:T(8,128)S(1)} %copy-done.10, s32[8,128]{1,0:T(8,128)S(1)} %get-tuple-element.10.sel_ref, bf16[8,36,768]{2,1,0:T(8,128)(2,1)S(1)} %all_to_all.39.g_ref, bf16[12,64,128]{2,1,0:T(8,128)(2,1)S(1)} %all_to_all.40.t_ref), custom_call_target="tpu_custom_call" | custom-call | tf_op jit(solution)/shard_map/pallas_call | solution.py:29
  (14 shorter events, 0.0 us)
Async XLA Ops:
  0.6 21.2 %copy-start.3 = (bf16[1,6144,128]{2,1,0:T(8,128)(2,1)S(1)}, bf16[1,6144,128]{2,1,0:T(8,128)(2,1)}, u32[]{:S(2)}) copy-start(bf16[1,6144,128]{2,1,0:T(8,128)(2,1)} %param.10) | copy-start | bytes 4718596
  0.7 1.1 copy-start.7
  1.8 1.0 copy-start.8
  2.9 0.9 copy-start.9
  7.8 27.4 %all-to-all-start = ((bf16[8,72,768]{2,1,0:T(8,128)(2,1)}), bf16[8,72,768]{2,1,0:T(8,128)(2,1)S(1)}, u32[]{:S(2)}, u32[]{:S(2)}) async-start(bf16[8,72,768]{2,1,0:T(8,128)(2,1)} %get-tuple-element.11), calls=%async_computation | async-start | bytes 1769472 | tf_op jit(solution)/shard_map/all_to_all | solution.py:260
  21.8 1.4 copy-start.4
  23.2 1.4 copy-start.5
  24.6 1.4 copy-start.6
  26.1 9.1 %copy-start.10 = (s32[8,96]{1,0:T(8,128)S(1)}, s32[8,96]{1,0:T(8,128)}, u32[]{:S(2)}) copy-start(s32[8,96]{1,0:T(8,128)} %cnt_ref.7) | copy-start | bytes 9220
  27.4 2.7 %copy-start = (bf16[6144,512]{1,0:T(8,128)(2,1)}, bf16[6144,512]{1,0:T(8,128)(2,1)S(1)}, u32[]{:S(2)}) copy-start(bf16[6144,512]{1,0:T(8,128)(2,1)S(1)} %shard_map.96.w_ref) | copy-start | bytes 18874372
  35.2 2.8 %copy-start.1 = (bf16[6144,512]{1,0:T(8,128)(2,1)S(1)}, bf16[6144,512]{1,0:T(8,128)(2,1)}, u32[]{:S(2)}) copy-start(bf16[6144,512]{1,0:T(8,128)(2,1)} %copy-done) | copy-start | bytes 18874372
  38.0 84.3 %copy-start.2 = (bf16[6144,512]{1,0:T(8,128)(2,1)S(1)}, bf16[6144,512]{1,0:T(8,128)(2,1)}, u32[]{:S(2)}) copy-start(bf16[6144,512]{1,0:T(8,128)(2,1)} %copy-done) | copy-start | bytes 18874372

commit v3 on v2

--- a/solution.py
+++ b/solution.py
@@ -15,7 +15,7 @@
 F32 = jnp.float32
 VMEM = pl.BlockSpec(memory_space=pltpu.VMEM)
 SMEM = pl.BlockSpec(memory_space=pltpu.SMEM)
-HBM = pl.BlockSpec(memory_space=pl.ANY)
+HBM = pl.BlockSpec(memory_space=pltpu.HBM)
 NN = (((1,), (0,)), ((), ()))
 NT = (((1,), (1,)), ((), ()))
 TN = (((0,), (0,)), ((), ()))
@@ -25,34 +25,43 @@
     return lax.dot_general(a, b, dims, preferred_element_type=F32)
 
 
-def call(kernel, outs, args, specs, scratch=(), limit=16):
+def call(kernel, outs, args, specs, scratch=(), limit=16, out_specs=None, cost=None):
     return pl.pallas_call(
         kernel,
         out_shape=outs,
         in_specs=specs,
-        out_specs=jax.tree.map(lambda _: VMEM, outs),
+        out_specs=out_specs or jax.tree.map(lambda _: VMEM, outs),
         scratch_shapes=list(scratch),
         compiler_params=pltpu.CompilerParams(vmem_limit_bytes=limit << 20),
+        cost_estimate=cost
+        and pl.CostEstimate(flops=cost[0], bytes_accessed=cost[1], transcendentals=0),
     )(*args)
 
 
-def pick_kernel(idx_ref, sel_ref, hid_ref, up_ref, out_ref, mine_ref, table, sems):
+def pick_kernel(
+    idx_ref, sel_ref, hid_ref, up_ref, out_ref, mine_ref, table, ready, view, sems, out_sems
+):
     heads, rows, cols = out_ref.shape
     cap, toks = rows // 2, hid_ref.shape[0]
+    start = (idx_ref[0] * NY + idx_ref[1]) * cap
+    aligned = jnp.minimum(start // 128 * 128, sel_ref.shape[1] - WIDE)
+    window = pltpu.make_async_copy(
+        sel_ref.at[:, pl.ds(pl.multiple_of(aligned, 128), WIDE)], view, sems.at[0]
+    )
+    window.start()
     part = toks // 3
     copies = []
     for i, src in enumerate((hid_ref, up_ref)):
         for j in range(3):
-            at = pl.ds(j * part, part)
             dst = table.at[pl.ds(i * toks + j * part, part)]
-            copies.append(pltpu.make_async_copy(src.at[at], dst, sems.at[3 * i + j]))
+            copies.append(
+                pltpu.make_async_copy(src.at[pl.ds(j * part, part)], dst, sems.at[3 * i + j + 1])
+            )
     for copy in copies:
         copy.start()
-    start = (idx_ref[0] * NY + idx_ref[1]) * cap
-    aligned = jnp.minimum(start // 128 * 128, sel_ref.shape[1] - WIDE)
-    window = sel_ref[:, pl.ds(pl.multiple_of(aligned, 128), WIDE)]
+    window.wait()
     shift = lax.rem(WIDE - (start - aligned), WIDE)
-    low = pltpu.roll(window, shift, 1)[:, :128]
+    low = pltpu.roll(view[...], shift, 1)[:, :128]
     high = pltpu.roll(low, cap, 1) + toks
     lane = lax.broadcasted_iota(jnp.int32, (heads, 128), 1)
     mine = jnp.where(lane < cap, low, high)
@@ -64,36 +73,54 @@
     onehot = jnp.where(lane == target, 1.0, 0.0).astype(BF)
     for copy in copies:
         copy.wait()
-    out_ref[...] = mm(onehot, table[...]).reshape(heads, rows, cols).astype(BF)
-
-
-def pack_kernel(wq_ref, wk_ref, wv_ref, wo_ref, w_ref):
-    hd = wq_ref.shape[1]
-    w_ref[:, :hd] = wq_ref[...]
-    w_ref[:, hd : 2 * hd] = wk_ref[...]
-    w_ref[:, 2 * hd : 3 * hd] = wv_ref[...]
-    w_ref[:, 3 * hd :] = wo_ref[...].T
-
-
-def project_kernel(idx_ref, cnt_ref, r_ref, w_ref, z_ref, y_ref, acc):
+    some = heads // 2
+    outs = []
+    for i in range(2):
+        got = mm(onehot[i * some * rows : (i + 1) * some * rows], table[...])
+        at = pl.ds(i * some, some)
+        ready[at] = got.reshape(some, rows, cols).astype(BF)
+        outs.append(pltpu.make_async_copy(ready.at[at], out_ref.at[at], out_sems.at[i]))
+        outs[i].start()
+    for copy in outs:
+        copy.wait()
+
+
+def project_kernel(
+    idx_ref,
+    cnt_ref,
+    r_hbm,
+    wq_ref,
+    wk_ref,
+    wv_ref,
+    wo_ref,
+    z_ref,
+    y_hbm,
+    acc,
+    r_ref,
+    w_in,
+    w_up,
+    y_ref,
+    r_sems,
+    w_sems,
+    y_sems,
+):
     heads, rows, cols = r_ref.shape
-    cap, hd = rows // 2, w_ref.shape[1] // 4
-    total = jnp.zeros((rows, 4 * hd), F32)
+    cap, hd = rows // 2, wq_ref.shape[1]
+    arrive, loads = [], []
     for c in range(heads):
-        total = total + mm(r_ref[c], w_ref[pl.ds(c * cols, cols), :])
-    acc[...] = total[:, 3 * hd :]
-    g = acc[cap:, :]
-    count = cnt_ref[idx_ref[2], idx_ref[0] * NY + idx_ref[1]]
-    row = lax.broadcasted_iota(jnp.int32, (cap, hd), 0)
-    g = jnp.where(row < count, g, 0.0).astype(BF)
-    qkv = total[:SLOT, : 3 * hd].astype(BF)[:cap]
-    nz = z_ref.shape[0]
-    for i in range(nz):
-        z_ref[i, :, :hd] = qkv[:, :hd]
-        z_ref[i, :, hd:] = g
+        arrive.append(pltpu.make_async_copy(r_hbm.at[c], r_ref.at[c], r_sems.at[c]))
+        part = pl.ds(c * cols, cols)
+        for j, src in enumerate((wq_ref, wk_ref, wv_ref)):
+            dst = w_in.at[part, pl.ds(j * hd, hd)]
+            loads.append(pltpu.make_async_copy(src.at[part], dst, w_sems.at[c, j]))
+        loads.append(pltpu.make_async_copy(wo_ref.at[:, part], w_up.at[:, part], w_sems.at[c, 3]))
+    for copy in arrive + loads:
+        copy.start()
+    for copy in arrive:
+        copy.wait()
+    nz = cnt_ref.shape[1] // NY
     wide = heads * cols // (nz * NY)
     for i in range(NY):
-        y_ref[i, :, : 2 * hd] = qkv[:, hd:]
         chunks = []
         for j in range(nz):
             c, off = divmod((j * NY + i) * wide, cols)
@@ -101,6 +128,30 @@
             aligned = r_ref[c, :, base : base + 128]
             chunks.append(aligned[:cap, off - base : off - base + wide])
         y_ref[i, :, 2 * hd :] = jnp.concatenate(chunks, axis=1)
+    qkv = jnp.zeros((SLOT, 3 * hd), F32)
+    g = jnp.zeros((rows, hd), F32)
+    for c in range(heads):
+        part = pl.ds(c * cols, cols)
+        x = r_ref[c]
+        for load in loads[4 * c : 4 * c + 4]:
+            load.wait()
+        qkv = qkv + mm(x[:SLOT], w_in[part, :])
+        g = g + mm(x, w_up[:, part], NT)
+    acc[...] = g
+    g = acc[cap:, :]
+    count = cnt_ref[idx_ref[2], idx_ref[0] * NY + idx_ref[1]]
+    row = lax.broadcasted_iota(jnp.int32, (cap, hd), 0)
+    g = jnp.where(row < count, g, 0.0).astype(BF)
+    qkv = qkv.astype(BF)[:cap]
+    leave = []
+    for i in range(NY):
+        y_ref[i, :, : 2 * hd] = qkv[:, hd:]
+        leave.append(pltpu.make_async_copy(y_ref.at[i], y_hbm.at[i], y_sems.at[i]))
+        leave[i].start()
+    z_ref[0, :, :hd] = qkv[:, :hd]
+    z_ref[0, :, hd:] = g
+    for copy in leave:
+        copy.wait()
 
 
 def padded(pad_ref, ref, lo, hi):
@@ -218,21 +269,27 @@
         out_ref[i, :, 2 * hd :] = grad_q
 
 
-def rows_kernel(idx_ref, back_ref, kv_ref, w_ref, g_ref, t_ref, x_pad, q_pad):
+def rows_kernel(idx_ref, back_ref, wq_ref, wk_ref, wv_ref, g_ref):
     heads, cap, cols = g_ref.shape
-    hd = w_ref.shape[1] // 4
+    hd = wq_ref.shape[1]
     kv = jnp.zeros((cap, 2 * hd), F32)
     for i in range(NY):
         kv = kv + back_ref[i, :, : 2 * hd].astype(F32)
     qkv = jnp.concatenate([back_ref[idx_ref[1], :, 2 * hd :], kv.astype(BF)], axis=1)
+    for c in range(heads):
+        part = pl.ds(c * cols, cols)
+        w = jnp.concatenate([wq_ref[part, :], wk_ref[part, :], wv_ref[part, :]], axis=1)
+        g_ref[c] = mm(qkv, w, NT).astype(BF)
+
+
+def weight_kernel(back_ref, kv_ref, t_ref, x_pad, q_pad):
+    hd = t_ref.shape[2]
     x = padded(x_pad, kv_ref, 2 * hd, kv_ref.shape[2])
     grad_q = padded(q_pad, back_ref, 2 * hd, 3 * hd)
     t_ref[...] = mm(x, grad_q, TN).reshape(t_ref.shape).astype(BF)
-    for c in range(heads):
-        g_ref[c] = mm(qkv, w_ref[pl.ds(c * cols, cols), : 3 * hd], NT).astype(BF)
-
-
-def finish_kernel(idx_ref, cnt_ref, sel_ref, g_ref, t_ref, h_out, w_out):
+
+
+def scatter_kernel(idx_ref, cnt_ref, sel_ref, g_ref, h_out):
     heads, cap, cols = g_ref.shape
     toks = h_out.shape[0]
     block = idx_ref[0] * NY + idx_ref[1]
@@ -243,7 +300,6 @@
         hit = (row == sel_ref[h : h + 1, :cap]) & (lane < cnt_ref[h, block])
         acc = acc + mm(jnp.where(hit, 1.0, 0.0).astype(BF), g_ref[h])
     h_out[...] = acc.astype(BF)
-    w_out[...] = jnp.sum(t_ref[...].astype(F32), axis=0)
 
 
 def body(hidden, upstream, w_query, w_key, w_value, w_output, selected, select_count):
@@ -263,31 +319,39 @@
         pick_kernel,
         (sds((heads, 2 * cap, cols), BF), sds((heads, 128), jnp.int32)),
         (idx, selected, hidden, upstream),
-        [SMEM, VMEM, HBM, HBM],
-        [pltpu.VMEM((2 * toks, cols), BF), pltpu.SemaphoreType.DMA((6,))],
+        [SMEM, HBM, HBM, HBM],
+        [
+            pltpu.VMEM((2 * toks, cols), BF),
+            pltpu.VMEM((heads, 2 * cap, cols), BF),
+            pltpu.VMEM((heads, WIDE), jnp.int32),
+            pltpu.SemaphoreType.DMA((7,)),
+            pltpu.SemaphoreType.DMA((2,)),
+        ],
+        limit=60,
+        out_specs=(HBM, VMEM),
     )
     rows = swap(picked, "head")
-    tall = pl.BlockSpec((cols, hd), lambda i: (i, 0))
-    weights = pl.pallas_call(
-        pack_kernel,
-        grid=(heads,),
-        out_shape=sds((heads * cols, 4 * hd), BF),
-        in_specs=[tall, tall, tall, pl.BlockSpec((hd, cols), lambda i: (0, i))],
-        out_specs=pl.BlockSpec((cols, 4 * hd), lambda i: (i, 0)),
-        compiler_params=pltpu.CompilerParams(vmem_limit_bytes=8 << 20),
-        cost_estimate=pl.CostEstimate(
-            flops=0, bytes_accessed=16 * heads * cols * hd, transcendentals=0
-        ),
-    )(w_query[0], w_key[0], w_value[0], w_output[0])
     piece = heads * cols // NY
     to_z, to_y = call(
         project_kernel,
-        (sds((nz, cap, 2 * hd), BF), sds((NY, cap, 2 * hd + piece), BF)),
-        (idx, count, rows, weights),
-        [SMEM] * 2 + [VMEM] * 2,
-        [pltpu.VMEM((2 * cap, hd), F32)],
-    )
-    qg, kv = swap(to_z, "z"), swap(to_y, "y")
+        (sds((1, cap, 2 * hd), BF), sds((NY, cap, 2 * hd + piece), BF)),
+        (idx, count, rows, w_query[0], w_key[0], w_value[0], w_output[0]),
+        [SMEM] * 2 + [HBM] * 5,
+        [
+            pltpu.VMEM((2 * cap, hd), F32),
+            pltpu.VMEM((heads, 2 * cap, cols), BF),
+            pltpu.VMEM((heads * cols, 3 * hd), BF),
+            pltpu.VMEM((hd, heads * cols), BF),
+            pltpu.VMEM((NY, cap, 2 * hd + piece), BF),
+            pltpu.SemaphoreType.DMA((heads,)),
+            pltpu.SemaphoreType.DMA((heads, 4)),
+            pltpu.SemaphoreType.DMA((NY,)),
+        ],
+        limit=60,
+        out_specs=(VMEM, HBM),
+    )
+    qg = lax.all_gather(to_z, "z", axis=0, tiled=True)
+    kv = swap(to_y, "y")
     pads = [pltpu.VMEM((nz, SLOT, 2 * hd), BF), pltpu.VMEM((NY, SLOT, 2 * hd), BF)]
     part = call(
         functools.partial(partial_kernel, scale),
@@ -305,20 +369,33 @@
         pads + [pltpu.VMEM((-(-nz * SLOT // WIDE) * WIDE, 128), F32)],
     )
     back = swap(grads, "y")
-    grad_rows, weight_terms = call(
+    size = heads * cap * cols
+    grad_rows = call(
         rows_kernel,
-        (sds((heads, cap, cols), BF), sds((nz, piece // nz, hd), BF)),
-        (idx, back, kv, weights),
-        [SMEM] + [VMEM] * 3,
+        sds((heads, cap, cols), BF),
+        (idx, back, w_query[0], w_key[0], w_value[0]),
+        [SMEM] + [VMEM] * 4,
+        cost=(6 * hd * size, 8 * size),
+    )
+    weight_terms = call(
+        weight_kernel,
+        sds((nz, piece // nz, hd), BF),
+        (back, kv),
+        [VMEM] * 2,
         [pltpu.VMEM((NY, SLOT, piece), BF), pltpu.VMEM((NY, SLOT, hd), BF)],
-    )
-    returned, terms = swap(grad_rows, "head"), swap(weight_terms, "z")
-    grad_hidden, grad_query = call(
-        finish_kernel,
-        (sds((toks, cols), BF), sds((piece // nz, hd), F32)),
-        (idx, count, mine, returned, terms),
-        [SMEM] * 2 + [VMEM] * 3,
-    )
+        cost=(2 * NY * SLOT * piece * hd, 4 * NY * SLOT * piece),
+    )
+    returned = swap(grad_rows, "head")
+    returned, weight_terms = lax.optimization_barrier((returned, weight_terms))
+    terms = swap(weight_terms, "z")
+    grad_hidden = call(
+        scatter_kernel,
+        sds((toks, cols), BF),
+        (idx, count, mine, returned),
+        [SMEM] * 2 + [VMEM] * 2,
+        cost=(2 * toks * size, 4 * size),
+    )
+    grad_query = jnp.sum(terms.astype(F32), axis=0)
     return grad_hidden, grad_query[None]
 
 

time: 160 us -> 148 us (0.925)
  blocking collectives: 111 us -> 83.6 us
  waiting for transfers between devices: 5.15 us -> 18 us
  local copies, waits for them, and re-layouts: 12.7 us -> 0.03 us
  Pallas kernels: 15.6 us -> 22.3 us
  starting transfers between devices: 14 us -> 20 us
    all_to_all x6 -> x3, blocking collectives: 111 us -> 59.9 us  [swap(): return lax.all_to_all(x, axis, split_axis=0, concat_axis=0, tiled=True)]
    all_gather x0 -> x1, blocking collectives: none -> 23.7 us  [body(): qg = lax.all_gather(to_z, 'z', axis=0, tiled=True)]
    all_to_all x1 -> x3, waiting for transfers between devices: 5.15 us -> 18 us  [swap(): return lax.all_to_all(x, axis, split_axis=0, concat_axis=0, tiled=True)]
    unnamed x22 -> x12, local copies, waits for them, and re-layouts: 12.7 us -> 0.03 us
    pallas_call x7, Pallas kernels: 15.6 us -> 22.3 us  [call(): pl.pallas_call(kernel, out_shape=outs, in_specs=specs, out_specs=out_spec...]
    all_to_all x1 -> x3, starting transfers between devices: 14 us -> 20 us  [swap(): return lax.all_to_all(x, axis, split_axis=0, concat_axis=0, tiled=True)]
  transfers between devices with their start and end apart: 1 -> 3, of which waited for: 1 -> 2; matrix products, arithmetic and copies ran while one was open for 0% -> 0% of each run, Pallas kernels for 1% -> 2%
where the time goes in v3:
time: 148 us; the launch traced here: 146 us
  blocking collectives  83.6 us (56%)
  Pallas kernels  22.3 us (15%)
  starting transfers between devices  20 us (14%)
  waiting for transfers between devices  18 us (12%)
    all_to_all x3, blocking collectives, swap(): return lax.all_to_all(x, axis, split_axis=0, concat_axis=0, tiled=True)  59.9 us
    all_gather x1, blocking collectives, body(): qg = lax.all_gather(to_z, 'z', axis=0, tiled=True)  23.7 us
    pallas_call x7, Pallas kernels, call(): pl.pallas_call(kernel, out_shape=outs, in_specs=specs, out_specs=out_spec...  22.3 us
    all_to_all x3, starting transfers between devices, swap(): return lax.all_to_all(x, axis, split_axis=0, concat_axis=0, tiled=True)  20 us
    all_to_all x3, waiting for transfers between devices, swap(): return lax.all_to_all(x, axis, split_axis=0, concat_axis=0, tiled=True)  18 us
  transfers between devices with their start and end apart: 3, of which 2 were waited for; matrix products, arithmetic and copies ran while one was open for 0% of the time, Pallas kernels for 2%

profile of v3, /device:TPU:1, one launch (start us, length us, event | category | flops | bytes accessed | tf_op | source)
XLA Modules:
  0.0 146.0 jit_solution(11454640739560812672)
XLA Ops:
  0.6 0.6 pad_add_fusion.idx_ref
  1.3 4.2 %shard_map.95 = (bf16[8,72,768]{2,1,0:T(8,128)(2,1)}, s32[8,128]{1,0:T(8,128)}) custom-call(s32[3]{0:T(128)} %pad_add_fusion.idx_ref, s32[8,3456]{1,0:T(8,128)} %sel_ref.1, bf16[288,768]{1,0:T(8,128)(2,1)} %hid_ref.1, bf16[288,768]{1,0:T(8,128)(2,1)} %up_ref.1), custom_call_target="tpu_custom_call" | custom-call | tf_op jit(solution)/shard_map/pallas_call | solution.py:29
  5.5 28.2 %all_to_all.30.r_hbm = bf16[8,72,768]{2,1,0:T(8,128)(2,1)} all-to-all(bf16[8,72,768]{2,1,0:T(8,128)(2,1)} %get-tuple-element.9), channel_id=1, replica_groups=mesh['z'=12,'y'=8,'head'=8] {'head'}, dimensions={0} | all-to-all | bytes 1769472 | tf_op jit(solution)/shard_map/all_to_all | solution.py:316
  33.7 8.1 %shard_map.96 = (bf16[1,36,256]{2,1,0:T(8,128)(2,1)}, bf16[8,36,1024]{2,1,0:T(8,128)(2,1)}) custom-call(s32[3]{0:T(128)} %pad_add_fusion.idx_ref, s32[8,96]{1,0:T(8,128)} %cnt_ref.7, bf16[8,72,768]{2,1,0:T(8,128)(2,1)} %all_to_all.30.r_hbm, bf16[6144,128]{1,0:T(8,128)(2,1)} %bitcast.8, bf16[6144,128]{1,0:T(8,128)(2,1)} %bitcast.10, ...), custom_call_target="tpu_custom_call" | custom-call | tf_op jit(solution)/shard_map/pallas_call | solution.py:29
  41.8 0.0 copy-start.3
  41.8 0.0 copy-start.4
  41.8 0.0 copy-start.2
  41.8 3.7 %all-to-all-start.1 = ((bf16[8,36,1024]{2,1,0:T(8,128)(2,1)}), bf16[8,36,1024]{2,1,0:T(8,128)(2,1)S(1)}, u32[]{:S(2)}, u32[]{:S(2)}) async-start(bf16[8,36,1024]{2,1,0:T(8,128)(2,1)} %get-tuple-element.11), calls=%async_computation.1 | async-start | bytes 1310720 | tf_op jit(solution)/shard_map/all_to_all | solution.py:316
  45.5 23.7 %all_gather.3.qg_ref = bf16[12,36,256]{2,1,0:T(8,128)(2,1)S(1)} all-gather(bf16[1,36,256]{2,1,0:T(8,128)(2,1)} %get-tuple-element.10), channel_id=1, replica_groups=mesh['z'=12,'y'=8,'head'=8] {'z'}, dimensions={0}, use_global_device_ids=true | all-gather | bytes 239616 | tf_op jit(solution)/shard_map/all_gather | solution.py:353
  69.2 0.0 all-to-all-done.1.kv_ref
  69.2 0.0 copy-start.1
  69.2 1.9 %shard_map.97 = bf16[12,52,256]{2,1,0:T(8,128)(2,1)S(1)} custom-call(s32[3]{0:T(128)S(1)} %copy-done.4, s32[8,96]{1,0:T(8,128)S(1)} %copy-done.3, bf16[12,36,256]{2,1,0:T(8,128)(2,1)S(1)} %all_gather.3.qg_ref, bf16[8,36,1024]{2,1,0:T(8,128)(2,1)S(1)} %all-to-all-done.1.kv_ref), custom_call_target="tpu_custom_call" | custom-call | tf_op jit(solution)/shard_map/pallas_call | solution.py:29
  71.1 0.0 copy-start
  71.1 20.2 %all_to_all.31.st_ref = bf16[12,52,256]{2,1,0:T(8,128)(2,1)S(1)} all-to-all(bf16[12,52,256]{2,1,0:T(8,128)(2,1)S(1)} %shard_map.97), channel_id=1, replica_groups=mesh['z'=12,'y'=8,'head'=8] {'z'}, dimensions={0} | all-to-all | bytes 638976 | tf_op jit(solution)/shard_map/all_to_all | solution.py:316
  91.3 1.7 %shard_map.98 = bf16[8,36,384]{2,1,0:T(8,128)(2,1)S(1)} custom-call(s32[3]{0:T(128)S(1)} %copy-done.4, s32[8,96]{1,0:T(8,128)S(1)} %copy-done.3, bf16[12,36,256]{2,1,0:T(8,128)(2,1)S(1)} %all_gather.3.qg_ref, bf16[8,36,1024]{2,1,0:T(8,128)(2,1)S(1)} %all-to-all-done.1.kv_ref, bf16[12,52,256]{2,1,0:T(8,128)(2,1)S(1)} %all_to_all.31.st_ref), custom_call_target="tpu_custom_call" | custom-call | tf_op jit(solution)/shard_map/pallas_call | solution.py:29
  93.0 11.6 %all_to_all.32.back_ref = bf16[8,36,384]{2,1,0:T(8,128)(2,1)S(1)} all-to-all(bf16[8,36,384]{2,1,0:T(8,128)(2,1)S(1)} %shard_map.98), channel_id=1, replica_groups=mesh['z'=12,'y'=8,'head'=8] {'y'}, dimensions={0} | all-to-all | bytes 442368 | tf_op jit(solution)/shard_map/all_to_all | solution.py:316
  104.6 2.9 %shard_map.99 = bf16[8,36,768]{2,1,0:T(8,128)(2,1)} custom-call(s32[3]{0:T(128)S(1)} %copy-done.4, bf16[8,36,384]{2,1,0:T(8,128)(2,1)S(1)} %all_to_all.32.back_ref, bf16[6144,128]{1,0:T(8,128)(2,1)S(1)} %bitcast.9, bf16[6144,128]{1,0:T(8,128)(2,1)S(1)} %bitcast.11, bf16[6144,128]{1,0:T(8,128)(2,1)S(1)} %bitcast.13), custom_call_target="tpu_custom_call" | custom-call | flops 169869312 | bytes 1769472 | tf_op jit(solution)/shard_map/pallas_call | solution.py:29
  107.5 12.8 %all-to-all-start.4 = ((bf16[8,36,768]{2,1,0:T(8,128)(2,1)}), bf16[8,36,768]{2,1,0:T(8,128)(2,1)S(1)}, u32[]{:S(2)}, u32[]{:S(2)}) async-start(bf16[8,36,768]{2,1,0:T(8,128)(2,1)} %shard_map.99), calls=%async_computation.4 | async-start | bytes 983040 | tf_op jit(solution)/shard_map/all_to_all | solution.py:316
  120.3 1.1 shard_map.100
  121.4 8.1 %all-to-all-done.4.g_ref = bf16[8,36,768]{2,1,0:T(8,128)(2,1)S(1)} async-done(((bf16[8,36,768]{2,1,0:T(8,128)(2,1)}), bf16[8,36,768]{2,1,0:T(8,128)(2,1)S(1)}, u32[]{:S(2)}, u32[]{:S(2)}) %all-to-all-start.4) | async-done | bytes 442400 | tf_op jit(solution)/shard_map/all_to_all | solution.py:316
  129.5 3.5 %all-to-all-start.5 = ((bf16[12,64,128]{2,1,0:T(8,128)(2,1)}), bf16[12,64,128]{2,1,0:T(8,128)(2,1)S(1)}, u32[]{:S(2)}, u32[]{:S(2)}) async-start(bf16[12,64,128]{2,1,0:T(8,128)(2,1)} %shard_map.100), calls=%async_computation.5 | async-start | bytes 393216 | tf_op jit(solution)/shard_map/all_to_all | solution.py:316
  133.0 2.4 %shard_map.101 = bf16[288,768]{1,0:T(8,128)(2,1)} custom-call(s32[3]{0:T(128)S(1)} %copy-done.4, s32[8,96]{1,0:T(8,128)S(1)} %copy-done.3, s32[8,128]{1,0:T(8,128)S(1)} %copy-done.5, bf16[8,36,768]{2,1,0:T(8,128)(2,1)S(1)} %all-to-all-done.4.g_ref), custom_call_target="tpu_custom_call" | custom-call | flops 127401984 | bytes 884736 | tf_op jit(solution)/shard_map/pallas_call | solution.py:29
  135.5 9.9 %all-to-all-done.5 = bf16[12,64,128]{2,1,0:T(8,128)(2,1)S(1)} async-done(((bf16[12,64,128]{2,1,0:T(8,128)(2,1)}), bf16[12,64,128]{2,1,0:T(8,128)(2,1)S(1)}, u32[]{:S(2)}, u32[]{:S(2)}) %all-to-all-start.5) | async-done | bytes 196640 | tf_op jit(solution)/shard_map/all_to_all | solution.py:316
  145.3 0.6 convert_reduce_fusion
  (7 shorter events, 0.0 us)
Async XLA Ops:
  41.8 27.4 %copy-start.3 = (s32[8,96]{1,0:T(8,128)S(1)}, s32[8,96]{1,0:T(8,128)}, u32[]{:S(2)}) copy-start(s32[8,96]{1,0:T(8,128)} %cnt_ref.7) | copy-start | bytes 9220
  41.8 27.4 %copy-start.4 = (s32[3]{0:T(128)S(1)}, s32[3]{0:T(128)}, u32[]{:S(2)}) copy-start(s32[3]{0:T(128)} %pad_add_fusion.idx_ref) | copy-start | bytes 40
  41.8 62.8 %copy-start.2 = (bf16[1,6144,128]{2,1,0:T(8,128)(2,1)S(1)}, bf16[1,6144,128]{2,1,0:T(8,128)(2,1)}, u32[]{:S(2)}) copy-start(bf16[1,6144,128]{2,1,0:T(8,128)(2,1)} %param.12) | copy-start | bytes 4718596
  41.8 27.4 %all-to-all-start.1 = ((bf16[8,36,1024]{2,1,0:T(8,128)(2,1)}), bf16[8,36,1024]{2,1,0:T(8,128)(2,1)S(1)}, u32[]{:S(2)}, u32[]{:S(2)}) async-start(bf16[8,36,1024]{2,1,0:T(8,128)(2,1)} %get-tuple-element.11), calls=%async_computation.1 | async-start | bytes 1310720 | tf_op jit(solution)/shard_map/all_to_all | solution.py:316
  69.2 35.4 %copy-start.1 = (bf16[1,6144,128]{2,1,0:T(8,128)(2,1)S(1)}, bf16[1,6144,128]{2,1,0:T(8,128)(2,1)}, u32[]{:S(2)}) copy-start(bf16[1,6144,128]{2,1,0:T(8,128)(2,1)} %param.11) | copy-start | bytes 4718596
  71.1 33.5 %copy-start = (bf16[1,6144,128]{2,1,0:T(8,128)(2,1)S(1)}, bf16[1,6144,128]{2,1,0:T(8,128)(2,1)}, u32[]{:S(2)}) copy-start(bf16[1,6144,128]{2,1,0:T(8,128)(2,1)} %param.10) | copy-start | bytes 4718596
  107.5 25.5 %copy-start.5 = (s32[8,128]{1,0:T(8,128)S(1)}, s32[8,128]{1,0:T(8,128)}, u32[]{:S(2)}) copy-start(s32[8,128]{1,0:T(8,128)} %get-tuple-element.8.sel_ref) | copy-start | bytes 12292
  107.5 22.0 %all-to-all-start.4 = ((bf16[8,36,768]{2,1,0:T(8,128)(2,1)}), bf16[8,36,768]{2,1,0:T(8,128)(2,1)S(1)}, u32[]{:S(2)}, u32[]{:S(2)}) async-start(bf16[8,36,768]{2,1,0:T(8,128)(2,1)} %shard_map.99), calls=%async_computation.4 | async-start | bytes 983040 | tf_op jit(solution)/shard_map/all_to_all | solution.py:316
  129.5 15.8 %all-to-all-start.5 = ((bf16[12,64,128]{2,1,0:T(8,128)(2,1)}), bf16[12,64,128]{2,1,0:T(8,128)(2,1)S(1)}, u32[]{:S(2)}, u32[]{:S(2)}) async-start(bf16[12,64,128]{2,1,0:T(8,128)(2,1)} %shard_map.100), calls=%async_computation.5 | async-start | bytes 393216 | tf_op jit(solution)/shard_map/all_to_all | solution.py:316

commit v4 on v3

--- a/solution.py
+++ b/solution.py
@@ -25,7 +25,7 @@
     return lax.dot_general(a, b, dims, preferred_element_type=F32)
 
 
-def call(kernel, outs, args, specs, scratch=(), limit=16, out_specs=None, cost=None):
+def call(kernel, outs, args, specs, scratch=(), limit=16, out_specs=None):
     return pl.pallas_call(
         kernel,
         out_shape=outs,
@@ -33,17 +33,15 @@
         out_specs=out_specs or jax.tree.map(lambda _: VMEM, outs),
         scratch_shapes=list(scratch),
         compiler_params=pltpu.CompilerParams(vmem_limit_bytes=limit << 20),
-        cost_estimate=cost
-        and pl.CostEstimate(flops=cost[0], bytes_accessed=cost[1], transcendentals=0),
     )(*args)
 
 
 def pick_kernel(
-    idx_ref, sel_ref, hid_ref, up_ref, out_ref, mine_ref, table, ready, view, sems, out_sems
+    sel_ref, hid_ref, up_ref, out_ref, mine_ref, table, ready, view, sems, out_sems
 ):
     heads, rows, cols = out_ref.shape
     cap, toks = rows // 2, hid_ref.shape[0]
-    start = (idx_ref[0] * NY + idx_ref[1]) * cap
+    start = (lax.axis_index("z") * NY + lax.axis_index("y")) * cap
     aligned = jnp.minimum(start // 128 * 128, sel_ref.shape[1] - WIDE)
     window = pltpu.make_async_copy(
         sel_ref.at[:, pl.ds(pl.multiple_of(aligned, 128), WIDE)], view, sems.at[0]
@@ -73,9 +71,10 @@
     onehot = jnp.where(lane == target, 1.0, 0.0).astype(BF)
     for copy in copies:
         copy.wait()
-    some = heads // 2
+    parts = out_sems.shape[0]
+    some = heads // parts
     outs = []
-    for i in range(2):
+    for i in range(parts):
         got = mm(onehot[i * some * rows : (i + 1) * some * rows], table[...])
         at = pl.ds(i * some, some)
         ready[at] = got.reshape(some, rows, cols).astype(BF)
@@ -86,41 +85,28 @@
 
 
 def project_kernel(
-    idx_ref,
-    cnt_ref,
-    r_hbm,
-    wq_ref,
-    wk_ref,
-    wv_ref,
-    wo_ref,
-    z_ref,
-    y_hbm,
-    acc,
-    r_ref,
-    w_in,
-    w_up,
-    y_ref,
-    r_sems,
-    w_sems,
-    y_sems,
+    live_ref, cnt_ref, r_ref, wq_ref, wk_ref, wv_ref, wo_ref, z_ref, y_hbm, acc, w_in, w_up, y_ref, w_sems, y_sems
 ):
     heads, rows, cols = r_ref.shape
     cap, hd = rows // 2, wq_ref.shape[1]
-    arrive, loads = [], []
+    loads = []
     for c in range(heads):
-        arrive.append(pltpu.make_async_copy(r_hbm.at[c], r_ref.at[c], r_sems.at[c]))
         part = pl.ds(c * cols, cols)
-        for j, src in enumerate((wq_ref, wk_ref, wv_ref)):
-            dst = w_in.at[part, pl.ds(j * hd, hd)]
+        for j, src in enumerate((wk_ref, wv_ref)):
+            dst = w_in.at[j, part]
             loads.append(pltpu.make_async_copy(src.at[part], dst, w_sems.at[c, j]))
-        loads.append(pltpu.make_async_copy(wo_ref.at[:, part], w_up.at[:, part], w_sems.at[c, 3]))
-    for copy in arrive + loads:
+        loads.append(pltpu.make_async_copy(wo_ref.at[:, part], w_up.at[:, part], w_sems.at[c, 2]))
+    for copy in loads:
         copy.start()
-    for copy in arrive:
-        copy.wait()
     nz = cnt_ref.shape[1] // NY
     wide = heads * cols // (nz * NY)
+    leave = []
     for i in range(NY):
+        for at in (pl.ds(2 * hd, nz * wide), pl.ds(0, 2 * hd)):
+            sem = y_sems.at[len(leave)]
+            leave.append(pltpu.make_async_copy(y_ref.at[i, :, at], y_hbm.at[i, :, at], sem))
+
+    def spread(i):
         chunks = []
         for j in range(nz):
             c, off = divmod((j * NY + i) * wide, cols)
@@ -128,26 +114,28 @@
             aligned = r_ref[c, :, base : base + 128]
             chunks.append(aligned[:cap, off - base : off - base + wide])
         y_ref[i, :, 2 * hd :] = jnp.concatenate(chunks, axis=1)
+        leave[2 * i].start()
+
     qkv = jnp.zeros((SLOT, 3 * hd), F32)
     g = jnp.zeros((rows, hd), F32)
     for c in range(heads):
         part = pl.ds(c * cols, cols)
+        for i in range(c * NY // heads, (c + 1) * NY // heads):
+            spread(i)
         x = r_ref[c]
-        for load in loads[4 * c : 4 * c + 4]:
+        for load in loads[3 * c : 3 * c + 3]:
             load.wait()
-        qkv = qkv + mm(x[:SLOT], w_in[part, :])
+        w = jnp.concatenate([wq_ref[part, :], w_in[0, part, :], w_in[1, part, :]], axis=1)
+        qkv = qkv + mm(x[:SLOT], w)
         g = g + mm(x, w_up[:, part], NT)
     acc[...] = g
     g = acc[cap:, :]
-    count = cnt_ref[idx_ref[2], idx_ref[0] * NY + idx_ref[1]]
     row = lax.broadcasted_iota(jnp.int32, (cap, hd), 0)
-    g = jnp.where(row < count, g, 0.0).astype(BF)
+    g = jnp.where(row < live_ref[0, 0], g, 0.0).astype(BF)
     qkv = qkv.astype(BF)[:cap]
-    leave = []
     for i in range(NY):
         y_ref[i, :, : 2 * hd] = qkv[:, hd:]
-        leave.append(pltpu.make_async_copy(y_ref.at[i], y_hbm.at[i], y_sems.at[i]))
-        leave[i].start()
+        leave[2 * i + 1].start()
     z_ref[0, :, :hd] = qkv[:, :hd]
     z_ref[0, :, hd:] = g
     for copy in leave:
@@ -204,24 +192,22 @@
     delta = jnp.sum(p * gp, axis=1, keepdims=True)
     a = mm((p * (gp - delta)).astype(BF), k) * scale
     b = mm(p.astype(BF), k) * scale
-    own = jnp.concatenate([a, b], axis=1).astype(BF)
+    own = jnp.concatenate([a, b], axis=1)
     n = nz * SLOT
-    lane = lax.broadcasted_iota(jnp.int32, (n, 128), 1) % 4
+    lane = (lax.broadcasted_iota(jnp.int32, (n, 128), 1) - cap) % 4
     stats = jnp.zeros((n, 128), F32)
     for i, col in enumerate(split(top + jnp.log(total)) + split(delta)):
         stats = jnp.where(lane == i, col, stats)
     whole = -(-n // WIDE) * WIDE
     if whole > n:
         stats = jnp.concatenate([stats, jnp.zeros((whole - n, 128), F32)], axis=0)
-    stats = stats.T[:16, :]
-    row = lax.broadcasted_iota(jnp.int32, (16, WIDE), 0) // 4
-    flat = jnp.zeros((16, WIDE), F32)
+    stats = stats.T[:SLOT, :]
+    row = lax.broadcasted_iota(jnp.int32, (SLOT, WIDE), 0)
+    flat = jnp.zeros((SLOT, WIDE), F32)
     for j in range(whole // WIDE):
-        flat = jnp.where(row == j, stats[:, j * WIDE : (j + 1) * WIDE], flat)
-    flat = flat.astype(BF)
+        flat = jnp.where((row - cap) // 4 == j, stats[:, j * WIDE : (j + 1) * WIDE], flat)
     for i in range(nz):
-        out_ref[i, :16, :] = flat
-        out_ref[i, 16:, :] = own[i * SLOT : (i + 1) * SLOT, :][:cap]
+        out_ref[i] = jnp.where(row < cap, own[i * SLOT : (i + 1) * SLOT, :], flat).astype(BF)
 
 
 def grads_kernel(
@@ -235,7 +221,7 @@
     chunks = -(-n // WIDE)
     logs, deltas = [], []
     for i in range(nz):
-        r = st_ref[i, :16, :].astype(F32)
+        r = st_ref[i].astype(F32)[cap:]
         line = [jnp.concatenate([r[4 * j + s : 4 * j + s + 1] for j in range(chunks)], axis=1) for s in range(4)]
         logs.append(line[0] + line[1])
         deltas.append(line[2] + line[3])
@@ -252,8 +238,8 @@
     mine = turn[pl.ds(pl.multiple_of(idx_ref[0] * SLOT, SLOT), SLOT), :]
     grad_q = jnp.zeros((cap, hd), F32)
     for i in range(nz):
-        a = st_ref[i, 16:, :hd].astype(F32)
-        b = st_ref[i, 16:, hd:].astype(F32)
+        a = st_ref[i, :cap, :hd].astype(F32)
+        b = st_ref[i, :cap, hd:].astype(F32)
         grad_q = grad_q + mine[:cap, i : i + 1] * (a + mine[:cap, nz + i : nz + i + 1] * b)
     order_q, order_k = orders(idx_ref, cnt_ref, nz, 1)
     allowed = order_k <= order_q
@@ -269,37 +255,38 @@
         out_ref[i, :, 2 * hd :] = grad_q
 
 
-def rows_kernel(idx_ref, back_ref, wq_ref, wk_ref, wv_ref, g_ref):
+def rows_kernel(idx_ref, back_ref, kv_ref, wq_ref, wk_ref, wv_ref, g_ref, t_ref, x_pad, q_pad):
     heads, cap, cols = g_ref.shape
     hd = wq_ref.shape[1]
     kv = jnp.zeros((cap, 2 * hd), F32)
     for i in range(NY):
         kv = kv + back_ref[i, :, : 2 * hd].astype(F32)
     qkv = jnp.concatenate([back_ref[idx_ref[1], :, 2 * hd :], kv.astype(BF)], axis=1)
+    x = padded(x_pad, kv_ref, 2 * hd, kv_ref.shape[2])
+    grad_q = padded(q_pad, back_ref, 2 * hd, 3 * hd)
+    t_ref[...] = mm(x, grad_q, TN).reshape(t_ref.shape).astype(BF)
     for c in range(heads):
         part = pl.ds(c * cols, cols)
         w = jnp.concatenate([wq_ref[part, :], wk_ref[part, :], wv_ref[part, :]], axis=1)
         g_ref[c] = mm(qkv, w, NT).astype(BF)
 
 
-def weight_kernel(back_ref, kv_ref, t_ref, x_pad, q_pad):
-    hd = t_ref.shape[2]
-    x = padded(x_pad, kv_ref, 2 * hd, kv_ref.shape[2])
-    grad_q = padded(q_pad, back_ref, 2 * hd, 3 * hd)
-    t_ref[...] = mm(x, grad_q, TN).reshape(t_ref.shape).astype(BF)
-
-
-def scatter_kernel(idx_ref, cnt_ref, sel_ref, g_ref, h_out):
+def finish_kernel(idx_ref, cnt_ref, sel_ref, g_ref, t_ref, h_out, w_out, pad_ref):
     heads, cap, cols = g_ref.shape
     toks = h_out.shape[0]
     block = idx_ref[0] * NY + idx_ref[1]
-    acc = jnp.zeros((toks, cols), F32)
-    row = lax.broadcasted_iota(jnp.int32, (toks, cap), 0)
-    lane = lax.broadcasted_iota(jnp.int32, (toks, cap), 1)
+    column = sel_ref[...].astype(F32).T
+    row = lax.broadcasted_iota(jnp.int32, (SLOT, 1), 0)
+    target = []
     for h in range(heads):
-        hit = (row == sel_ref[h : h + 1, :cap]) & (lane < cnt_ref[h, block])
-        acc = acc + mm(jnp.where(hit, 1.0, 0.0).astype(BF), g_ref[h])
-    h_out[...] = acc.astype(BF)
+        at = column[:SLOT, h : h + 1].astype(jnp.int32)
+        target.append(jnp.where(row < cnt_ref[h, block], at, -1))
+    target = jnp.concatenate(target, axis=0)
+    lane = lax.broadcasted_iota(jnp.int32, (heads * SLOT, toks), 1)
+    hit = jnp.where(lane == target, 1.0, 0.0).astype(BF)
+    grads = padded(pad_ref, g_ref, 0, cols)
+    h_out[...] = mm(hit, grads, TN).astype(BF)
+    w_out[...] = jnp.sum(t_ref[...].astype(F32), axis=0)
 
 
 def body(hidden, upstream, w_query, w_key, w_value, w_output, selected, select_count):
@@ -310,6 +297,7 @@
     cap = selected.shape[1] // (nz * NY)
     scale = hd ** (-0.5)
     count = select_count
+    live = lax.dynamic_slice(select_count, (idx[2], idx[0] * NY + idx[1]), (1, 1))
     sds = jax.ShapeDtypeStruct
 
     def swap(x, axis):
@@ -318,16 +306,16 @@
     picked, mine = call(
         pick_kernel,
         (sds((heads, 2 * cap, cols), BF), sds((heads, 128), jnp.int32)),
-        (idx, selected, hidden, upstream),
-        [SMEM, HBM, HBM, HBM],
+        (selected, hidden, upstream),
+        [HBM, HBM, HBM],
         [
             pltpu.VMEM((2 * toks, cols), BF),
             pltpu.VMEM((heads, 2 * cap, cols), BF),
             pltpu.VMEM((heads, WIDE), jnp.int32),
             pltpu.SemaphoreType.DMA((7,)),
-            pltpu.SemaphoreType.DMA((2,)),
+            pltpu.SemaphoreType.DMA((min(heads, 4),)),
         ],
-        limit=60,
+        limit=54,
         out_specs=(HBM, VMEM),
     )
     rows = swap(picked, "head")
@@ -335,19 +323,17 @@
     to_z, to_y = call(
         project_kernel,
         (sds((1, cap, 2 * hd), BF), sds((NY, cap, 2 * hd + piece), BF)),
-        (idx, count, rows, w_query[0], w_key[0], w_value[0], w_output[0]),
-        [SMEM] * 2 + [HBM] * 5,
+        (live, count, rows, w_query[0], w_key[0], w_value[0], w_output[0]),
+        [SMEM] * 2 + [VMEM] * 2 + [HBM] * 3,
         [
             pltpu.VMEM((2 * cap, hd), F32),
-            pltpu.VMEM((heads, 2 * cap, cols), BF),
-            pltpu.VMEM((heads * cols, 3 * hd), BF),
+            pltpu.VMEM((2, heads * cols, hd), BF),
             pltpu.VMEM((hd, heads * cols), BF),
             pltpu.VMEM((NY, cap, 2 * hd + piece), BF),
-            pltpu.SemaphoreType.DMA((heads,)),
-            pltpu.SemaphoreType.DMA((heads, 4)),
-            pltpu.SemaphoreType.DMA((NY,)),
+            pltpu.SemaphoreType.DMA((heads, 3)),
+            pltpu.SemaphoreType.DMA((2 * NY,)),
         ],
-        limit=60,
+        limit=50,
         out_specs=(VMEM, HBM),
     )
     qg = lax.all_gather(to_z, "z", axis=0, tiled=True)
@@ -355,7 +341,7 @@
     pads = [pltpu.VMEM((nz, SLOT, 2 * hd), BF), pltpu.VMEM((NY, SLOT, 2 * hd), BF)]
     part = call(
         functools.partial(partial_kernel, scale),
-        sds((nz, cap + 16, 2 * hd), BF),
+        sds((nz, SLOT, 2 * hd), BF),
         (idx, count, qg, kv),
         [SMEM] * 2 + [VMEM] * 2,
         pads,
@@ -369,33 +355,21 @@
         pads + [pltpu.VMEM((-(-nz * SLOT // WIDE) * WIDE, 128), F32)],
     )
     back = swap(grads, "y")
-    size = heads * cap * cols
-    grad_rows = call(
+    grad_rows, weight_terms = call(
         rows_kernel,
-        sds((heads, cap, cols), BF),
-        (idx, back, w_query[0], w_key[0], w_value[0]),
-        [SMEM] + [VMEM] * 4,
-        cost=(6 * hd * size, 8 * size),
-    )
-    weight_terms = call(
-        weight_kernel,
-        sds((nz, piece // nz, hd), BF),
-        (back, kv),
-        [VMEM] * 2,
+        (sds((heads, cap, cols), BF), sds((nz, piece // nz, hd), BF)),
+        (idx, back, kv, w_query[0], w_key[0], w_value[0]),
+        [SMEM] + [VMEM] * 5,
         [pltpu.VMEM((NY, SLOT, piece), BF), pltpu.VMEM((NY, SLOT, hd), BF)],
-        cost=(2 * NY * SLOT * piece * hd, 4 * NY * SLOT * piece),
-    )
-    returned = swap(grad_rows, "head")
-    returned, weight_terms = lax.optimization_barrier((returned, weight_terms))
-    terms = swap(weight_terms, "z")
-    grad_hidden = call(
-        scatter_kernel,
-        sds((toks, cols), BF),
-        (idx, count, mine, returned),
-        [SMEM] * 2 + [VMEM] * 2,
-        cost=(2 * toks * size, 4 * size),
-    )
-    grad_query = jnp.sum(terms.astype(F32), axis=0)
+    )
+    returned, terms = swap(grad_rows, "head"), swap(weight_terms, "z")
+    grad_hidden, grad_query = call(
+        finish_kernel,
+        (sds((toks, cols), BF), sds((piece // nz, hd), F32)),
+        (idx, count, mine, returned, terms),
+        [SMEM] * 2 + [VMEM] * 3,
+        [pltpu.VMEM((heads, SLOT, cols), BF)],
+    )
     return grad_hidden, grad_query[None]
 
 

time: 148 us -> 140 us (0.946)
  blocking collectives: 83.6 us -> 90.1 us
  waiting for transfers between devices: 18 us -> 12.7 us
  Pallas kernels: 22.3 us -> 17.4 us
  starting transfers between devices: 20 us -> 17.5 us
    all_to_all x3 -> x4, blocking collectives: 59.9 us -> 66.1 us  [swap(): return lax.all_to_all(x, axis, split_axis=0, concat_axis=0, tiled=True)]
    all_to_all x3 -> x2, waiting for transfers between devices: 18 us -> 12.7 us  [swap(): return lax.all_to_all(x, axis, split_axis=0, concat_axis=0, tiled=True)]
    pallas_call x7 -> x6, Pallas kernels: 22.3 us -> 17.4 us  [call(): pl.pallas_call(kernel, out_shape=outs, in_specs=specs, out_specs=out_spec...]
    all_to_all x3 -> x2, starting transfers between devices: 20 us -> 17.5 us  [swap(): return lax.all_to_all(x, axis, split_axis=0, concat_axis=0, tiled=True)]
  transfers between devices with their start and end apart: 3 -> 2, of which waited for: 2 -> 1; matrix products, arithmetic and copies ran while one was open for 0% -> 1% of each run, Pallas kernels for 2% -> 0%
where the time goes in v4:
time: 140 us; the launch traced here: 139 us
  blocking collectives  90.1 us (64%)
  starting transfers between devices  17.5 us (12%)
  Pallas kernels  17.4 us (12%)
  waiting for transfers between devices  12.7 us (9%)
    all_to_all x4, blocking collectives, swap(): return lax.all_to_all(x, axis, split_axis=0, concat_axis=0, tiled=True)  66.1 us
    all_gather x1, blocking collectives, body(): qg = lax.all_gather(to_z, 'z', axis=0, tiled=True)  24.1 us
    all_to_all x2, starting transfers between devices, swap(): return lax.all_to_all(x, axis, split_axis=0, concat_axis=0, tiled=True)  17.5 us
    pallas_call x6, Pallas kernels, call(): pl.pallas_call(kernel, out_shape=outs, in_specs=specs, out_specs=out_spec...  17.4 us
    all_to_all x2, waiting for transfers between devices, swap(): return lax.all_to_all(x, axis, split_axis=0, concat_axis=0, tiled=True)  12.7 us
  transfers between devices with their start and end apart: 2, of which 1 were waited for; matrix products, arithmetic and copies ran while one was open for 1% of the time, Pallas kernels for 0%

profile of v4, /device:TPU:1, one launch (start us, length us, event | category | flops | bytes accessed | tf_op | source)
XLA Modules:
  0.0 139.3 jit_solution(12098568684047698888)
XLA Ops:
  0.6 0.0 copy-start.3
  0.6 0.0 copy-start
  0.7 3.6 %shard_map.95 = (bf16[8,72,768]{2,1,0:T(8,128)(2,1)}, s32[8,128]{1,0:T(8,128)}) custom-call(s32[8,3456]{1,0:T(8,128)} %sel_ref.1, bf16[288,768]{1,0:T(8,128)(2,1)} %hid_ref.1, bf16[288,768]{1,0:T(8,128)(2,1)} %up_ref.1), custom_call_target="tpu_custom_call" | custom-call | tf_op jit(solution)/shard_map/pallas_call | solution.py:29
  4.3 14.0 %all-to-all-start = ((bf16[8,72,768]{2,1,0:T(8,128)(2,1)}), bf16[8,72,768]{2,1,0:T(8,128)(2,1)S(1)}, u32[]{:S(2)}, u32[]{:S(2)}) async-start(bf16[8,72,768]{2,1,0:T(8,128)(2,1)} %get-tuple-element.11), calls=%async_computation | async-start | bytes 1769472 | tf_op jit(solution)/shard_map/all_to_all | solution.py:304
  18.3 0.0 copy-done.3
  18.3 0.7 dynamic_slice.3.live_ref
  18.9 12.7 %all-to-all-done.r_ref = bf16[8,72,768]{2,1,0:T(8,128)(2,1)S(1)} async-done(((bf16[8,72,768]{2,1,0:T(8,128)(2,1)}), bf16[8,72,768]{2,1,0:T(8,128)(2,1)S(1)}, u32[]{:S(2)}, u32[]{:S(2)}) %all-to-all-start) | async-done | bytes 884768 | tf_op jit(solution)/shard_map/all_to_all | solution.py:304
  31.6 0.0 copy-done
  31.6 5.8 %shard_map.96 = (bf16[1,36,256]{2,1,0:T(8,128)(2,1)S(1)}, bf16[8,36,1024]{2,1,0:T(8,128)(2,1)}) custom-call(s32[1,1]{1,0:T(1,128)} %dynamic_slice.3.live_ref, s32[8,96]{1,0:T(8,128)S(1)} %copy-done.3, bf16[8,72,768]{2,1,0:T(8,128)(2,1)S(1)} %all-to-all-done.r_ref, bf16[6144,128]{1,0:T(8,128)(2,1)S(1)} %bitcast.8, bf16[6144,128]{1,0:T(8,128)(2,1)} %bitcast.10, ...), custom_call_target="tpu_custom_call" | custom-call | tf_op jit(solution)/shard_map/pallas_call | solution.py:29
  37.4 3.6 %all-to-all-start.1 = ((bf16[8,36,1024]{2,1,0:T(8,128)(2,1)}), bf16[8,36,1024]{2,1,0:T(8,128)(2,1)S(1)}, u32[]{:S(2)}, u32[]{:S(2)}) async-start(bf16[8,36,1024]{2,1,0:T(8,128)(2,1)} %get-tuple-element.13), calls=%async_computation.1 | async-start | bytes 1310720 | tf_op jit(solution)/shard_map/all_to_all | solution.py:304
  41.0 0.1 pad_add_fusion.idx_ref
  41.1 24.1 %all_gather.3.qg_ref = bf16[12,36,256]{2,1,0:T(8,128)(2,1)S(1)} all-gather(bf16[1,36,256]{2,1,0:T(8,128)(2,1)S(1)} %get-tuple-element.12), channel_id=1, replica_groups=mesh['z'=12,'y'=8,'head'=8] {'z'}, dimensions={0}, use_global_device_ids=true | all-gather | bytes 239616 | tf_op jit(solution)/shard_map/all_gather | solution.py:339
  65.2 0.0 all-to-all-done.1.kv_ref
  65.2 1.9 %shard_map.97 = bf16[12,48,256]{2,1,0:T(8,128)(2,1)S(1)} custom-call(s32[3]{0:T(128)S(1)} %pad_add_fusion.idx_ref, s32[8,96]{1,0:T(8,128)S(1)} %copy-done.3, bf16[12,36,256]{2,1,0:T(8,128)(2,1)S(1)} %all_gather.3.qg_ref, bf16[8,36,1024]{2,1,0:T(8,128)(2,1)S(1)} %all-to-all-done.1.kv_ref), custom_call_target="tpu_custom_call" | custom-call | tf_op jit(solution)/shard_map/pallas_call | solution.py:29
  67.1 19.2 %all_to_all.30.st_ref = bf16[12,48,256]{2,1,0:T(8,128)(2,1)S(1)} all-to-all(bf16[12,48,256]{2,1,0:T(8,128)(2,1)S(1)} %shard_map.97), channel_id=1, replica_groups=mesh['z'=12,'y'=8,'head'=8] {'z'}, dimensions={0} | all-to-all | bytes 589824 | tf_op jit(solution)/shard_map/all_to_all | solution.py:304
  86.2 1.7 %shard_map.98 = bf16[8,36,384]{2,1,0:T(8,128)(2,1)S(1)} custom-call(s32[3]{0:T(128)S(1)} %pad_add_fusion.idx_ref, s32[8,96]{1,0:T(8,128)S(1)} %copy-done.3, bf16[12,36,256]{2,1,0:T(8,128)(2,1)S(1)} %all_gather.3.qg_ref, bf16[8,36,1024]{2,1,0:T(8,128)(2,1)S(1)} %all-to-all-done.1.kv_ref, bf16[12,48,256]{2,1,0:T(8,128)(2,1)S(1)} %all_to_all.30.st_ref), custom_call_target="tpu_custom_call" | custom-call | tf_op jit(solution)/shard_map/pallas_call | solution.py:29
  88.0 11.9 %all_to_all.31.back_ref = bf16[8,36,384]{2,1,0:T(8,128)(2,1)S(1)} all-to-all(bf16[8,36,384]{2,1,0:T(8,128)(2,1)S(1)} %shard_map.98), channel_id=1, replica_groups=mesh['z'=12,'y'=8,'head'=8] {'y'}, dimensions={0} | all-to-all | bytes 442368 | tf_op jit(solution)/shard_map/all_to_all | solution.py:304
  99.9 0.0 copy-done.1
  99.9 0.0 copy-done.2
  99.9 2.3 %shard_map.99 = (bf16[8,36,768]{2,1,0:T(8,128)(2,1)S(1)}, bf16[12,64,128]{2,1,0:T(8,128)(2,1)S(1)}) custom-call(s32[3]{0:T(128)S(1)} %pad_add_fusion.idx_ref, bf16[8,36,384]{2,1,0:T(8,128)(2,1)S(1)} %all_to_all.31.back_ref, bf16[8,36,1024]{2,1,0:T(8,128)(2,1)S(1)} %all-to-all-done.1.kv_ref, bf16[6144,128]{1,0:T(8,128)(2,1)S(1)} %bitcast.9, ...), custom_call_target="tpu_custom_call" | custom-call | tf_op jit(solution)/shard_map/pallas_call | solution.py:29
  102.2 20.3 %all_to_all.32.g_ref = bf16[8,36,768]{2,1,0:T(8,128)(2,1)S(1)} all-to-all(bf16[8,36,768]{2,1,0:T(8,128)(2,1)S(1)} %get-tuple-element.14), channel_id=1, replica_groups=mesh['z'=12,'y'=8,'head'=8] {'head'}, dimensions={0} | all-to-all | bytes 884736 | tf_op jit(solution)/shard_map/all_to_all | solution.py:304
  122.5 14.7 %all_to_all.33.t_ref = bf16[12,64,128]{2,1,0:T(8,128)(2,1)S(1)} all-to-all(bf16[12,64,128]{2,1,0:T(8,128)(2,1)S(1)} %get-tuple-element.15), channel_id=1, replica_groups=mesh['z'=12,'y'=8,'head'=8] {'z'}, dimensions={0} | all-to-all | bytes 393216 | tf_op jit(solution)/shard_map/all_to_all | solution.py:304
  137.2 0.0 copy-done.4
  137.2 2.1 %shard_map.100 = (bf16[288,768]{1,0:T(8,128)(2,1)}, f32[64,128]{1,0:T(8,128)}) custom-call(s32[3]{0:T(128)S(1)} %pad_add_fusion.idx_ref, s32[8,96]{1,0:T(8,128)S(1)} %copy-done.3, s32[8,128]{1,0:T(8,128)S(1)} %copy-done.4, bf16[8,36,768]{2,1,0:T(8,128)(2,1)S(1)} %all_to_all.32.g_ref, bf16[12,64,128]{2,1,0:T(8,128)(2,1)S(1)} %all_to_all.33.t_ref), custom_call_target="tpu_custom_call" | custom-call | tf_op jit(solution)/shard_map/pallas_call | solution.py:29
  (3 shorter events, 0.0 us)
Async XLA Ops:
  0.6 17.6 %copy-start.3 = (s32[8,96]{1,0:T(8,128)S(1)}, s32[8,96]{1,0:T(8,128)}, u32[]{:S(2)}) copy-start(s32[8,96]{1,0:T(8,128)} %cnt_ref.7) | copy-start | bytes 9220
  0.6 31.0 %copy-start = (bf16[1,6144,128]{2,1,0:T(8,128)(2,1)S(1)}, bf16[1,6144,128]{2,1,0:T(8,128)(2,1)}, u32[]{:S(2)}) copy-start(bf16[1,6144,128]{2,1,0:T(8,128)(2,1)} %param.10) | copy-start | bytes 4718596
  4.3 27.3 %all-to-all-start = ((bf16[8,72,768]{2,1,0:T(8,128)(2,1)}), bf16[8,72,768]{2,1,0:T(8,128)(2,1)S(1)}, u32[]{:S(2)}, u32[]{:S(2)}) async-start(bf16[8,72,768]{2,1,0:T(8,128)(2,1)} %get-tuple-element.11), calls=%async_computation | async-start | bytes 1769472 | tf_op jit(solution)/shard_map/all_to_all | solution.py:304
  37.4 27.7 %all-to-all-start.1 = ((bf16[8,36,1024]{2,1,0:T(8,128)(2,1)}), bf16[8,36,1024]{2,1,0:T(8,128)(2,1)S(1)}, u32[]{:S(2)}, u32[]{:S(2)}) async-start(bf16[8,36,1024]{2,1,0:T(8,128)(2,1)} %get-tuple-element.13), calls=%async_computation.1 | async-start | bytes 1310720 | tf_op jit(solution)/shard_map/all_to_all | solution.py:304
  65.2 34.7 %copy-start.1 = (bf16[1,6144,128]{2,1,0:T(8,128)(2,1)S(1)}, bf16[1,6144,128]{2,1,0:T(8,128)(2,1)}, u32[]{:S(2)}) copy-start(bf16[1,6144,128]{2,1,0:T(8,128)(2,1)} %param.11) | copy-start | bytes 4718596
  65.2 34.7 %copy-start.2 = (bf16[1,6144,128]{2,1,0:T(8,128)(2,1)S(1)}, bf16[1,6144,128]{2,1,0:T(8,128)(2,1)}, u32[]{:S(2)}) copy-start(bf16[1,6144,128]{2,1,0:T(8,128)(2,1)} %param.12) | copy-start | bytes 4718596
  99.9 37.3 %copy-start.4 = (s32[8,128]{1,0:T(8,128)S(1)}, s32[8,128]{1,0:T(8,128)}, u32[]{:S(2)}) copy-start(s32[8,128]{1,0:T(8,128)} %get-tuple-element.10.sel_ref) | copy-start | bytes 12292

commit v5 on v4

--- a/solution.py
+++ b/solution.py
@@ -85,20 +85,12 @@
 
 
 def project_kernel(
-    live_ref, cnt_ref, r_ref, wq_ref, wk_ref, wv_ref, wo_ref, z_ref, y_hbm, acc, w_in, w_up, y_ref, w_sems, y_sems
+    nz, block_ref, cnt_ref, r_ref, wq_ref, wk_ref, wv_ref, wo_ref, z_ref, y_hbm, acc, y_ref, counts, y_sems, sem
 ):
     heads, rows, cols = r_ref.shape
     cap, hd = rows // 2, wq_ref.shape[1]
-    loads = []
-    for c in range(heads):
-        part = pl.ds(c * cols, cols)
-        for j, src in enumerate((wk_ref, wv_ref)):
-            dst = w_in.at[j, part]
-            loads.append(pltpu.make_async_copy(src.at[part], dst, w_sems.at[c, j]))
-        loads.append(pltpu.make_async_copy(wo_ref.at[:, part], w_up.at[:, part], w_sems.at[c, 2]))
-    for copy in loads:
-        copy.start()
-    nz = cnt_ref.shape[1] // NY
+    number = pltpu.make_async_copy(cnt_ref, counts, sem)
+    number.start()
     wide = heads * cols // (nz * NY)
     leave = []
     for i in range(NY):
@@ -123,15 +115,19 @@
         for i in range(c * NY // heads, (c + 1) * NY // heads):
             spread(i)
         x = r_ref[c]
-        for load in loads[3 * c : 3 * c + 3]:
-            load.wait()
-        w = jnp.concatenate([wq_ref[part, :], w_in[0, part, :], w_in[1, part, :]], axis=1)
+        w = jnp.concatenate([wq_ref[part, :], wk_ref[part, :], wv_ref[part, :]], axis=1)
         qkv = qkv + mm(x[:SLOT], w)
-        g = g + mm(x, w_up[:, part], NT)
+        g = g + mm(x, wo_ref[:, part], NT)
     acc[...] = g
     g = acc[cap:, :]
+    number.wait()
+    row = lax.broadcasted_iota(jnp.int32, counts.shape, 0)
+    lane = lax.broadcasted_iota(jnp.int32, counts.shape, 1)
+    here = (row == lax.axis_index("head")) & (lane == block_ref[:, : counts.shape[1]])
+    live = jnp.sum(jnp.where(here, counts[...].astype(F32), 0.0), axis=1, keepdims=True)
+    live = jnp.sum(live, axis=0, keepdims=True).astype(jnp.int32)
     row = lax.broadcasted_iota(jnp.int32, (cap, hd), 0)
-    g = jnp.where(row < live_ref[0, 0], g, 0.0).astype(BF)
+    g = jnp.where(row < live, g, 0.0).astype(BF)
     qkv = qkv.astype(BF)[:cap]
     for i in range(NY):
         y_ref[i, :, : 2 * hd] = qkv[:, hd:]
@@ -142,6 +138,10 @@
         copy.wait()
 
 
+def block_kernel(in_ref, out_ref):
+    out_ref[...] = in_ref[...] + (lax.axis_index("z") * NY + lax.axis_index("y"))
+
+
 def padded(pad_ref, ref, lo, hi):
     n, cap = ref.shape[0], ref.shape[1]
     w = hi - lo
@@ -151,8 +151,8 @@
     return pad_ref[...].reshape(n * SLOT, w)
 
 
-def orders(idx_ref, cnt_ref, nz, axis_q):
-    z, y, h = idx_ref[0], idx_ref[1], idx_ref[2]
+def orders(cnt_ref, nz, axis_q):
+    z, y, h = (lax.axis_index(a) for a in ("z", "y", "head"))
 
     def one(n, axis, block_of, dead):
         shape = (n * SLOT, 1) if axis == 0 else (1, n * SLOT)
@@ -175,12 +175,12 @@
     return hi, x - hi
 
 
-def partial_kernel(scale, idx_ref, cnt_ref, qg_ref, kv_ref, out_ref, qg_pad, kv_pad):
+def partial_kernel(scale, cnt_ref, qg_ref, kv_ref, out_ref, qg_pad, kv_pad):
     nz, cap, hd = qg_ref.shape[0], qg_ref.shape[1], qg_ref.shape[2] // 2
     qg = padded(qg_pad, qg_ref, 0, 2 * hd)
     kv = padded(kv_pad, kv_ref, 0, 2 * hd)
     q, g, k, v = qg[:, :hd], qg[:, hd:], kv[:, :hd], kv[:, hd:]
-    order_q, order_k = orders(idx_ref, cnt_ref, nz, 0)
+    order_q, order_k = orders(cnt_ref, nz, 0)
     allowed = order_k <= order_q
     s = jnp.where(allowed, mm(q, k, NT) * scale, NEG)
     top = jnp.max(s, axis=1, keepdims=True)
@@ -211,7 +211,7 @@
 
 
 def grads_kernel(
-    scale, idx_ref, cnt_ref, qg_ref, kv_ref, st_ref, out_ref, qg_pad, kv_pad, turn
+    scale, cnt_ref, qg_ref, kv_ref, st_ref, out_ref, qg_pad, kv_pad, turn
 ):
     nz, cap, hd = qg_ref.shape[0], qg_ref.shape[1], qg_ref.shape[2] // 2
     n = nz * SLOT
@@ -235,13 +235,13 @@
     lines = shares + [d - delta for d in deltas] + [jnp.zeros((128 - 2 * nz, width), F32)]
     turn[...] = jnp.concatenate(lines, axis=0).T
     delta = delta[:, :n]
-    mine = turn[pl.ds(pl.multiple_of(idx_ref[0] * SLOT, SLOT), SLOT), :]
+    mine = turn[pl.ds(pl.multiple_of(lax.axis_index("z") * SLOT, SLOT), SLOT), :]
     grad_q = jnp.zeros((cap, hd), F32)
     for i in range(nz):
         a = st_ref[i, :cap, :hd].astype(F32)
         b = st_ref[i, :cap, hd:].astype(F32)
         grad_q = grad_q + mine[:cap, i : i + 1] * (a + mine[:cap, nz + i : nz + i + 1] * b)
-    order_q, order_k = orders(idx_ref, cnt_ref, nz, 1)
+    order_q, order_k = orders(cnt_ref, nz, 1)
     allowed = order_k <= order_q
     s = mm(k, q, NT) * scale
     p = jnp.where(allowed, jnp.exp(jnp.where(allowed, s - log_total, NEG)), 0.0)
@@ -255,13 +255,13 @@
         out_ref[i, :, 2 * hd :] = grad_q
 
 
-def rows_kernel(idx_ref, back_ref, kv_ref, wq_ref, wk_ref, wv_ref, g_ref, t_ref, x_pad, q_pad):
+def rows_kernel(back_ref, kv_ref, wq_ref, wk_ref, wv_ref, g_ref, t_ref, x_pad, q_pad):
     heads, cap, cols = g_ref.shape
     hd = wq_ref.shape[1]
     kv = jnp.zeros((cap, 2 * hd), F32)
     for i in range(NY):
         kv = kv + back_ref[i, :, : 2 * hd].astype(F32)
-    qkv = jnp.concatenate([back_ref[idx_ref[1], :, 2 * hd :], kv.astype(BF)], axis=1)
+    qkv = jnp.concatenate([back_ref[lax.axis_index("y"), :, 2 * hd :], kv.astype(BF)], axis=1)
     x = padded(x_pad, kv_ref, 2 * hd, kv_ref.shape[2])
     grad_q = padded(q_pad, back_ref, 2 * hd, 3 * hd)
     t_ref[...] = mm(x, grad_q, TN).reshape(t_ref.shape).astype(BF)
@@ -271,10 +271,10 @@
         g_ref[c] = mm(qkv, w, NT).astype(BF)
 
 
-def finish_kernel(idx_ref, cnt_ref, sel_ref, g_ref, t_ref, h_out, w_out, pad_ref):
+def finish_kernel(cnt_ref, sel_ref, g_ref, t_ref, h_out, w_out, pad_ref):
     heads, cap, cols = g_ref.shape
     toks = h_out.shape[0]
-    block = idx_ref[0] * NY + idx_ref[1]
+    block = lax.axis_index("z") * NY + lax.axis_index("y")
     column = sel_ref[...].astype(F32).T
     row = lax.broadcasted_iota(jnp.int32, (SLOT, 1), 0)
     target = []
@@ -291,13 +291,10 @@
 
 def body(hidden, upstream, w_query, w_key, w_value, w_output, selected, select_count):
     nz, heads = lax.axis_size("z"), lax.axis_size("head")
-    idx = jnp.stack([lax.axis_index(a) for a in ("z", "y", "head")]).astype(jnp.int32)
     toks, cols = hidden.shape
     hd = w_query.shape[2]
     cap = selected.shape[1] // (nz * NY)
     scale = hd ** (-0.5)
-    count = select_count
-    live = lax.dynamic_slice(select_count, (idx[2], idx[0] * NY + idx[1]), (1, 1))
     sds = jax.ShapeDtypeStruct
 
     def swap(x, axis):
@@ -307,7 +304,7 @@
         pick_kernel,
         (sds((heads, 2 * cap, cols), BF), sds((heads, 128), jnp.int32)),
         (selected, hidden, upstream),
-        [HBM, HBM, HBM],
+        [HBM] * 3,
         [
             pltpu.VMEM((2 * toks, cols), BF),
             pltpu.VMEM((heads, 2 * cap, cols), BF),
@@ -318,56 +315,66 @@
         limit=54,
         out_specs=(HBM, VMEM),
     )
+    picked, block = lax.optimization_barrier((picked, jnp.zeros((heads, 128), jnp.int32)))
+    block = pl.pallas_call(
+        block_kernel,
+        out_shape=sds(block.shape, jnp.int32),
+        in_specs=[VMEM],
+        out_specs=VMEM,
+        compiler_params=pltpu.CompilerParams(vmem_limit_bytes=1 << 20),
+        cost_estimate=pl.CostEstimate(flops=10000000000, bytes_accessed=0, transcendentals=0),
+    )(block)
+    picked, block = lax.optimization_barrier((picked, block))
     rows = swap(picked, "head")
     piece = heads * cols // NY
     to_z, to_y = call(
-        project_kernel,
+        functools.partial(project_kernel, nz),
         (sds((1, cap, 2 * hd), BF), sds((NY, cap, 2 * hd + piece), BF)),
-        (live, count, rows, w_query[0], w_key[0], w_value[0], w_output[0]),
-        [SMEM] * 2 + [VMEM] * 2 + [HBM] * 3,
+        (block, select_count, rows, w_query[0], w_key[0], w_value[0], w_output[0]),
+        [VMEM, HBM] + [VMEM] * 5,
         [
             pltpu.VMEM((2 * cap, hd), F32),
-            pltpu.VMEM((2, heads * cols, hd), BF),
-            pltpu.VMEM((hd, heads * cols), BF),
             pltpu.VMEM((NY, cap, 2 * hd + piece), BF),
-            pltpu.SemaphoreType.DMA((heads, 3)),
+            pltpu.VMEM(select_count.shape, jnp.int32),
             pltpu.SemaphoreType.DMA((2 * NY,)),
+            pltpu.SemaphoreType.DMA,
         ],
-        limit=50,
+        limit=16,
         out_specs=(VMEM, HBM),
     )
+    count, to_z, to_y = lax.optimization_barrier((select_count, to_z, to_y))
     qg = lax.all_gather(to_z, "z", axis=0, tiled=True)
     kv = swap(to_y, "y")
     pads = [pltpu.VMEM((nz, SLOT, 2 * hd), BF), pltpu.VMEM((NY, SLOT, 2 * hd), BF)]
     part = call(
         functools.partial(partial_kernel, scale),
         sds((nz, SLOT, 2 * hd), BF),
-        (idx, count, qg, kv),
-        [SMEM] * 2 + [VMEM] * 2,
+        (count, qg, kv),
+        [SMEM] + [VMEM] * 2,
         pads,
     )
     joined = swap(part, "z")
     grads = call(
         functools.partial(grads_kernel, scale),
         sds((NY, cap, 3 * hd), BF),
-        (idx, count, qg, kv, joined),
-        [SMEM] * 2 + [VMEM] * 3,
+        (count, qg, kv, joined),
+        [SMEM] + [VMEM] * 3,
         pads + [pltpu.VMEM((-(-nz * SLOT // WIDE) * WIDE, 128), F32)],
     )
     back = swap(grads, "y")
     grad_rows, weight_terms = call(
         rows_kernel,
         (sds((heads, cap, cols), BF), sds((nz, piece // nz, hd), BF)),
-        (idx, back, kv, w_query[0], w_key[0], w_value[0]),
-        [SMEM] + [VMEM] * 5,
+        (back, kv, w_query[0], w_key[0], w_value[0]),
+        [VMEM] * 5,
         [pltpu.VMEM((NY, SLOT, piece), BF), pltpu.VMEM((NY, SLOT, hd), BF)],
     )
     returned, terms = swap(grad_rows, "head"), swap(weight_terms, "z")
     grad_hidden, grad_query = call(
         finish_kernel,
         (sds((toks, cols), BF), sds((piece // nz, hd), F32)),
-        (idx, count, mine, returned, terms),
-        [SMEM] * 2 + [VMEM] * 3,
+        (count, mine, returned, terms),
+        [SMEM] + [VMEM] * 3,
         [pltpu.VMEM((heads, SLOT, cols), BF)],
     )
     return grad_hidden, grad_query[None]

time: 140 us -> 137 us (0.979)
  blocking collectives: 90.1 us -> 118 us
  starting transfers between devices: 17.5 us -> 3.55 us
  waiting for transfers between devices: 12.7 us -> 0.01 us
  Pallas kernels: 17.4 us -> 13.2 us
    all_to_all x4 -> x5, blocking collectives: 66.1 us -> 92.6 us  [swap(): return lax.all_to_all(x, axis, split_axis=0, concat_axis=0, tiled=True)]
    all_to_all x2 -> x1, starting transfers between devices: 17.5 us -> 3.55 us  [swap(): return lax.all_to_all(x, axis, split_axis=0, concat_axis=0, tiled=True)]
    all_to_all x2 -> x1, waiting for transfers between devices: 12.7 us -> 0.01 us  [swap(): return lax.all_to_all(x, axis, split_axis=0, concat_axis=0, tiled=True)]
    pallas_call x6, Pallas kernels: 17.4 us -> 13.2 us  [call(): pl.pallas_call(kernel, out_shape=outs, in_specs=specs, out_specs=out_spec...]
  transfers between devices with their start and end apart: 2 -> 1, of which waited for: 1 -> 0; matrix products, arithmetic and copies ran while one was open for 1% -> 0% of each run, Pallas kernels for 0% -> 0%
where the time goes in v5:
time: 137 us; the launch traced here: 136 us
  blocking collectives  118 us (86%)
  Pallas kernels  13.2 us (10%)
  starting transfers between devices  3.55 us (3%)
    all_to_all x5, blocking collectives, swap(): return lax.all_to_all(x, axis, split_axis=0, concat_axis=0, tiled=True)  92.6 us
    all_gather x1, blocking collectives, body(): qg = lax.all_gather(to_z, 'z', axis=0, tiled=True)  24.9 us
    pallas_call x6, Pallas kernels, call(): pl.pallas_call(kernel, out_shape=outs, in_specs=specs, out_specs=out_spec...  13.2 us
    all_to_all x1, starting transfers between devices, swap(): return lax.all_to_all(x, axis, split_axis=0, concat_axis=0, tiled=True)  3.55 us
  transfers between devices with their start and end apart: 1, of which 0 were waited for; matrix products, arithmetic and copies ran while one was open for 0% of the time, Pallas kernels for 0%

profile of v5, /device:TPU:1, one launch (start us, length us, event | category | flops | bytes accessed | tf_op | source)
XLA Modules:
  0.0 136.2 jit_solution(3491217405236578468)
XLA Ops:
  0.6 3.5 %shard_map.95 = (bf16[8,72,768]{2,1,0:T(8,128)(2,1)}, s32[8,128]{1,0:T(8,128)}) custom-call(s32[8,3456]{1,0:T(8,128)} %sel_ref.1, bf16[288,768]{1,0:T(8,128)(2,1)} %hid_ref.1, bf16[288,768]{1,0:T(8,128)(2,1)} %up_ref.1), custom_call_target="tpu_custom_call" | custom-call | tf_op jit(solution)/shard_map/pallas_call | solution.py:29
  4.2 0.0 copy-start.8
  4.2 0.0 copy-start.1
  4.2 0.0 copy-start.3
  4.2 0.0 copy-start.5
  4.2 1.1 copy-done.8
  5.3 26.6 %all_to_all.30.r_ref = bf16[8,72,768]{2,1,0:T(8,128)(2,1)S(1)} all-to-all(bf16[8,72,768]{2,1,0:T(8,128)(2,1)S(1)} %copy-done.8), channel_id=1, replica_groups=mesh['z'=12,'y'=8,'head'=8] {'head'}, dimensions={0} | all-to-all | bytes 1769472 | tf_op jit(solution)/shard_map/all_to_all | solution.py:301
  32.0 0.0 copy-done.1
  32.0 0.0 copy-done.3
  32.0 0.0 copy-done.5
  32.0 0.0 copy-done
  32.0 2.2 %shard_map.97 = (bf16[1,36,256]{2,1,0:T(8,128)(2,1)S(1)}, bf16[8,36,1024]{2,1,0:T(8,128)(2,1)}) custom-call(s32[8,128]{1,0:T(8,128)S(1)} %shard_map.96.block_ref, s32[8,96]{1,0:T(8,128)S(1)} %copy-done.6, bf16[8,72,768]{2,1,0:T(8,128)(2,1)S(1)} %all_to_all.30.r_ref, bf16[6144,128]{1,0:T(8,128)(2,1)S(1)} %bitcast.5, bf16[6144,128]{1,0:T(8,128)(2,1)S(1)} %bitcast.7, ...), custom_call_target="tpu_custom_call" | custom-call | tf_op jit(solution)/shard_map/pallas_call | solution.py:29
  34.2 3.6 %all-to-all-start.1 = ((bf16[8,36,1024]{2,1,0:T(8,128)(2,1)}), bf16[8,36,1024]{2,1,0:T(8,128)(2,1)S(1)}, u32[]{:S(2)}, u32[]{:S(2)}) async-start(bf16[8,36,1024]{2,1,0:T(8,128)(2,1)} %get-tuple-element.27), calls=%async_computation.1 | async-start | bytes 1310720 | tf_op jit(solution)/shard_map/all_to_all | solution.py:301
  37.8 24.9 %all_gather.3.qg_ref = bf16[12,36,256]{2,1,0:T(8,128)(2,1)S(1)} all-gather(bf16[1,36,256]{2,1,0:T(8,128)(2,1)S(1)} %get-tuple-element.26), channel_id=1, replica_groups=mesh['z'=12,'y'=8,'head'=8] {'z'}, dimensions={0}, use_global_device_ids=true | all-gather | bytes 239616 | tf_op jit(solution)/shard_map/all_gather | solution.py:346
  62.7 0.0 all-to-all-done.1.kv_ref
  62.7 1.9 %shard_map.98 = bf16[12,48,256]{2,1,0:T(8,128)(2,1)S(1)} custom-call(s32[8,96]{1,0:T(8,128)S(1)} %copy-done.6, bf16[12,36,256]{2,1,0:T(8,128)(2,1)S(1)} %all_gather.3.qg_ref, bf16[8,36,1024]{2,1,0:T(8,128)(2,1)S(1)} %all-to-all-done.1.kv_ref), custom_call_target="tpu_custom_call" | custom-call | tf_op jit(solution)/shard_map/pallas_call | solution.py:29
  64.6 19.4 %all_to_all.31.st_ref = bf16[12,48,256]{2,1,0:T(8,128)(2,1)S(1)} all-to-all(bf16[12,48,256]{2,1,0:T(8,128)(2,1)S(1)} %shard_map.98), channel_id=1, replica_groups=mesh['z'=12,'y'=8,'head'=8] {'z'}, dimensions={0} | all-to-all | bytes 589824 | tf_op jit(solution)/shard_map/all_to_all | solution.py:301
  84.0 1.7 %shard_map.99 = bf16[8,36,384]{2,1,0:T(8,128)(2,1)S(1)} custom-call(s32[8,96]{1,0:T(8,128)S(1)} %copy-done.6, bf16[12,36,256]{2,1,0:T(8,128)(2,1)S(1)} %all_gather.3.qg_ref, bf16[8,36,1024]{2,1,0:T(8,128)(2,1)S(1)} %all-to-all-done.1.kv_ref, bf16[12,48,256]{2,1,0:T(8,128)(2,1)S(1)} %all_to_all.31.st_ref), custom_call_target="tpu_custom_call" | custom-call | tf_op jit(solution)/shard_map/pallas_call | solution.py:29
  85.7 11.8 %all_to_all.32.back_ref = bf16[8,36,384]{2,1,0:T(8,128)(2,1)S(1)} all-to-all(bf16[8,36,384]{2,1,0:T(8,128)(2,1)S(1)} %shard_map.99), channel_id=1, replica_groups=mesh['z'=12,'y'=8,'head'=8] {'y'}, dimensions={0} | all-to-all | bytes 442368 | tf_op jit(solution)/shard_map/all_to_all | solution.py:301
  97.5 1.8 %shard_map.100 = (bf16[8,36,768]{2,1,0:T(8,128)(2,1)S(1)}, bf16[12,64,128]{2,1,0:T(8,128)(2,1)S(1)}) custom-call(bf16[8,36,384]{2,1,0:T(8,128)(2,1)S(1)} %all_to_all.32.back_ref, bf16[8,36,1024]{2,1,0:T(8,128)(2,1)S(1)} %all-to-all-done.1.kv_ref, bf16[6144,128]{1,0:T(8,128)(2,1)S(1)} %bitcast.6, bf16[6144,128]{1,0:T(8,128)(2,1)S(1)} %bitcast.8, ...), custom_call_target="tpu_custom_call" | custom-call | tf_op jit(solution)/shard_map/pallas_call | solution.py:29
  99.3 20.2 %all_to_all.33.g_ref = bf16[8,36,768]{2,1,0:T(8,128)(2,1)S(1)} all-to-all(bf16[8,36,768]{2,1,0:T(8,128)(2,1)S(1)} %get-tuple-element.28), channel_id=1, replica_groups=mesh['z'=12,'y'=8,'head'=8] {'head'}, dimensions={0} | all-to-all | bytes 884736 | tf_op jit(solution)/shard_map/all_to_all | solution.py:301
  119.5 14.7 %all_to_all.34.t_ref = bf16[12,64,128]{2,1,0:T(8,128)(2,1)S(1)} all-to-all(bf16[12,64,128]{2,1,0:T(8,128)(2,1)S(1)} %get-tuple-element.29), channel_id=1, replica_groups=mesh['z'=12,'y'=8,'head'=8] {'z'}, dimensions={0} | all-to-all | bytes 393216 | tf_op jit(solution)/shard_map/all_to_all | solution.py:301
  134.1 0.0 copy-done.7
  134.2 2.1 %shard_map.101 = (bf16[288,768]{1,0:T(8,128)(2,1)}, f32[64,128]{1,0:T(8,128)}) custom-call(s32[8,96]{1,0:T(8,128)S(1)} %copy-done.6, s32[8,128]{1,0:T(8,128)S(1)} %copy-done.7, bf16[8,36,768]{2,1,0:T(8,128)(2,1)S(1)} %all_to_all.33.g_ref, bf16[12,64,128]{2,1,0:T(8,128)(2,1)S(1)} %all_to_all.34.t_ref), custom_call_target="tpu_custom_call" | custom-call | tf_op jit(solution)/shard_map/pallas_call | solution.py:29
  (10 shorter events, 0.0 us)
Async XLA Ops:
  4.2 1.2 copy-start.8
  4.2 27.8 %copy-start.1 = (bf16[1,6144,128]{2,1,0:T(8,128)(2,1)S(1)}, bf16[1,6144,128]{2,1,0:T(8,128)(2,1)}, u32[]{:S(2)}) copy-start(bf16[1,6144,128]{2,1,0:T(8,128)(2,1)} %param.11) | copy-start | bytes 4718596
  4.2 27.8 %copy-start.3 = (bf16[1,6144,128]{2,1,0:T(8,128)(2,1)S(1)}, bf16[1,6144,128]{2,1,0:T(8,128)(2,1)}, u32[]{:S(2)}) copy-start(bf16[1,6144,128]{2,1,0:T(8,128)(2,1)} %param.12) | copy-start | bytes 4718596
  4.2 27.8 %copy-start.5 = (bf16[1,128,6144]{2,1,0:T(8,128)(2,1)S(1)}, bf16[1,128,6144]{2,1,0:T(8,128)(2,1)}, u32[]{:S(2)}) copy-start(bf16[1,128,6144]{2,1,0:T(8,128)(2,1)} %param.13) | copy-start | bytes 4718596
  5.3 26.7 %copy-start = (bf16[1,6144,128]{2,1,0:T(8,128)(2,1)S(1)}, bf16[1,6144,128]{2,1,0:T(8,128)(2,1)}, u32[]{:S(2)}) copy-start(bf16[1,6144,128]{2,1,0:T(8,128)(2,1)} %param.10) | copy-start | bytes 4718596
  5.3 26.7 %copy-start.6 = (s32[8,96]{1,0:T(8,128)S(1)}, s32[8,96]{1,0:T(8,128)}, u32[]{:S(2)}) copy-start(s32[8,96]{1,0:T(8,128)} %cnt_ref.4) | copy-start | bytes 9220
  34.2 28.5 %all-to-all-start.1 = ((bf16[8,36,1024]{2,1,0:T(8,128)(2,1)}), bf16[8,36,1024]{2,1,0:T(8,128)(2,1)S(1)}, u32[]{:S(2)}, u32[]{:S(2)}) async-start(bf16[8,36,1024]{2,1,0:T(8,128)(2,1)} %get-tuple-element.27), calls=%async_computation.1 | async-start | bytes 1310720 | tf_op jit(solution)/shard_map/all_to_all | solution.py:301
  62.7 34.8 %copy-start.2 = (bf16[1,6144,128]{2,1,0:T(8,128)(2,1)S(1)}, bf16[1,6144,128]{2,1,0:T(8,128)(2,1)}, u32[]{:S(2)}) copy-start(bf16[1,6144,128]{2,1,0:T(8,128)(2,1)} %param.11) | copy-start | bytes 4718596
  62.7 34.8 %copy-start.4 = (bf16[1,6144,128]{2,1,0:T(8,128)(2,1)S(1)}, bf16[1,6144,128]{2,1,0:T(8,128)(2,1)}, u32[]{:S(2)}) copy-start(bf16[1,6144,128]{2,1,0:T(8,128)(2,1)} %param.12) | copy-start | bytes 4718596
  97.5 36.6 %copy-start.7 = (s32[8,128]{1,0:T(8,128)S(1)}, s32[8,128]{1,0:T(8,128)}, u32[]{:S(2)}) copy-start(s32[8,128]{1,0:T(8,128)} %get-tuple-element.25.sel_ref) | copy-start | bytes 12292

commit v6 on v5

--- a/solution.py
+++ b/solution.py
@@ -25,14 +25,17 @@
     return lax.dot_general(a, b, dims, preferred_element_type=F32)
 
 
-def call(kernel, outs, args, specs, scratch=(), limit=16, out_specs=None):
+def call(kernel, outs, args, specs, scratch=(), limit=16 << 20, out_specs=None, flops=0):
     return pl.pallas_call(
         kernel,
         out_shape=outs,
         in_specs=specs,
         out_specs=out_specs or jax.tree.map(lambda _: VMEM, outs),
         scratch_shapes=list(scratch),
-        compiler_params=pltpu.CompilerParams(vmem_limit_bytes=limit << 20),
+        compiler_params=pltpu.CompilerParams(vmem_limit_bytes=limit),
+        cost_estimate=pl.CostEstimate(flops=flops, bytes_accessed=0, transcendentals=0)
+        if flops
+        else None,
     )(*args)
 
 
@@ -85,7 +88,7 @@
 
 
 def project_kernel(
-    nz, block_ref, cnt_ref, r_ref, wq_ref, wk_ref, wv_ref, wo_ref, z_ref, y_hbm, acc, y_ref, counts, y_sems, sem
+    nz, cnt_ref, r_ref, wq_ref, wk_ref, wv_ref, wo_ref, z_ref, y_hbm, acc, y_ref, counts, y_sems, sem
 ):
     heads, rows, cols = r_ref.shape
     cap, hd = rows // 2, wq_ref.shape[1]
@@ -123,7 +126,7 @@
     number.wait()
     row = lax.broadcasted_iota(jnp.int32, counts.shape, 0)
     lane = lax.broadcasted_iota(jnp.int32, counts.shape, 1)
-    here = (row == lax.axis_index("head")) & (lane == block_ref[:, : counts.shape[1]])
+    here = (row == lax.axis_index("head")) & (lane == lax.axis_index("z") * NY + lax.axis_index("y"))
     live = jnp.sum(jnp.where(here, counts[...].astype(F32), 0.0), axis=1, keepdims=True)
     live = jnp.sum(live, axis=0, keepdims=True).astype(jnp.int32)
     row = lax.broadcasted_iota(jnp.int32, (cap, hd), 0)
@@ -136,10 +139,6 @@
     z_ref[0, :, hd:] = g
     for copy in leave:
         copy.wait()
-
-
-def block_kernel(in_ref, out_ref):
-    out_ref[...] = in_ref[...] + (lax.axis_index("z") * NY + lax.axis_index("y"))
 
 
 def padded(pad_ref, ref, lo, hi):
@@ -312,26 +311,17 @@
             pltpu.SemaphoreType.DMA((7,)),
             pltpu.SemaphoreType.DMA((min(heads, 4),)),
         ],
-        limit=54,
+        limit=54 << 20,
+        flops=20000000000,
         out_specs=(HBM, VMEM),
     )
-    picked, block = lax.optimization_barrier((picked, jnp.zeros((heads, 128), jnp.int32)))
-    block = pl.pallas_call(
-        block_kernel,
-        out_shape=sds(block.shape, jnp.int32),
-        in_specs=[VMEM],
-        out_specs=VMEM,
-        compiler_params=pltpu.CompilerParams(vmem_limit_bytes=1 << 20),
-        cost_estimate=pl.CostEstimate(flops=10000000000, bytes_accessed=0, transcendentals=0),
-    )(block)
-    picked, block = lax.optimization_barrier((picked, block))
     rows = swap(picked, "head")
     piece = heads * cols // NY
     to_z, to_y = call(
         functools.partial(project_kernel, nz),
         (sds((1, cap, 2 * hd), BF), sds((NY, cap, 2 * hd + piece), BF)),
-        (block, select_count, rows, w_query[0], w_key[0], w_value[0], w_output[0]),
-        [VMEM, HBM] + [VMEM] * 5,
+        (select_count, rows, w_query[0], w_key[0], w_value[0], w_output[0]),
+        [HBM] + [VMEM] * 5,
         [
             pltpu.VMEM((2 * cap, hd), F32),
             pltpu.VMEM((NY, cap, 2 * hd + piece), BF),
@@ -339,7 +329,6 @@
             pltpu.SemaphoreType.DMA((2 * NY,)),
             pltpu.SemaphoreType.DMA,
         ],
-        limit=16,
         out_specs=(VMEM, HBM),
     )
     count, to_z, to_y = lax.optimization_barrier((select_count, to_z, to_y))

time: 137 us -> 136 us (level)
  no operation moved by 1% of the time
where the time goes in v6:
time: 136 us; the launch traced here: 135 us
  blocking collectives  118 us (87%)
  Pallas kernels  13.3 us (10%)
  starting transfers between devices  3.55 us (3%)
    all_to_all x5, blocking collectives, swap(): return lax.all_to_all(x, axis, split_axis=0, concat_axis=0, tiled=True)  93.6 us
    all_gather x1, blocking collectives, body(): qg = lax.all_gather(to_z, 'z', axis=0, tiled=True)  24 us
    pallas_call x6, Pallas kernels, call(): pl.pallas_call(kernel, out_shape=outs, in_specs=specs, out_specs=out_spec...  13.3 us
    all_to_all x1, starting transfers between devices, swap(): return lax.all_to_all(x, axis, split_axis=0, concat_axis=0, tiled=True)  3.55 us
  transfers between devices with their start and end apart: 1, of which 0 were waited for; matrix products, arithmetic and copies ran while one was open for 0% of the time, Pallas kernels for 0%

profile of v6, /device:TPU:1, one launch (start us, length us, event | category | flops | bytes accessed | tf_op | source)
XLA Modules:
  0.0 135.3 jit_solution(3372081281801496924)
XLA Ops:
  0.6 0.0 copy-start.1
  0.6 0.0 copy-start.3
  0.7 0.0 copy-start.5
  0.7 3.7 %shard_map.95 = (bf16[8,72,768]{2,1,0:T(8,128)(2,1)}, s32[8,128]{1,0:T(8,128)}) custom-call(s32[8,3456]{1,0:T(8,128)} %sel_ref.1, bf16[288,768]{1,0:T(8,128)(2,1)} %hid_ref.1, bf16[288,768]{1,0:T(8,128)(2,1)} %up_ref.1), custom_call_target="tpu_custom_call" | custom-call | flops 20000000000 | tf_op jit(solution)/shard_map/pallas_call | solution.py:29
  4.3 0.0 copy-start
  4.3 0.0 copy-start.6
  4.4 27.6 %all_to_all.30.r_ref = bf16[8,72,768]{2,1,0:T(8,128)(2,1)S(1)} all-to-all(bf16[8,72,768]{2,1,0:T(8,128)(2,1)} %get-tuple-element.13), channel_id=1, replica_groups=mesh['z'=12,'y'=8,'head'=8] {'head'}, dimensions={0} | all-to-all | bytes 1769472 | tf_op jit(solution)/shard_map/all_to_all | solution.py:300
  31.9 0.0 copy-done.1
  32.0 0.0 copy-done.3
  32.0 0.0 copy-done.5
  32.0 0.0 copy-done
  32.0 2.2 %shard_map.96 = (bf16[1,36,256]{2,1,0:T(8,128)(2,1)S(1)}, bf16[8,36,1024]{2,1,0:T(8,128)(2,1)}) custom-call(s32[8,96]{1,0:T(8,128)S(1)} %copy-done.6, bf16[8,72,768]{2,1,0:T(8,128)(2,1)S(1)} %all_to_all.30.r_ref, bf16[6144,128]{1,0:T(8,128)(2,1)S(1)} %bitcast.5, bf16[6144,128]{1,0:T(8,128)(2,1)S(1)} %bitcast.7, bf16[6144,128]{1,0:T(8,128)(2,1)S(1)} %bitcast.9, ...), custom_call_target="tpu_custom_call" | custom-call | tf_op jit(solution)/shard_map/pallas_call | solution.py:29
  34.2 3.6 %all-to-all-start.1 = ((bf16[8,36,1024]{2,1,0:T(8,128)(2,1)}), bf16[8,36,1024]{2,1,0:T(8,128)(2,1)S(1)}, u32[]{:S(2)}, u32[]{:S(2)}) async-start(bf16[8,36,1024]{2,1,0:T(8,128)(2,1)} %get-tuple-element.19), calls=%async_computation.1 | async-start | bytes 1310720 | tf_op jit(solution)/shard_map/all_to_all | solution.py:300
  37.7 24.0 %all_gather.3.qg_ref = bf16[12,36,256]{2,1,0:T(8,128)(2,1)S(1)} all-gather(bf16[1,36,256]{2,1,0:T(8,128)(2,1)S(1)} %get-tuple-element.18), channel_id=1, replica_groups=mesh['z'=12,'y'=8,'head'=8] {'z'}, dimensions={0}, use_global_device_ids=true | all-gather | bytes 239616 | tf_op jit(solution)/shard_map/all_gather | solution.py:335
  61.8 0.0 all-to-all-done.1.kv_ref
  61.8 1.9 %shard_map.97 = bf16[12,48,256]{2,1,0:T(8,128)(2,1)S(1)} custom-call(s32[8,96]{1,0:T(8,128)S(1)} %copy-done.6, bf16[12,36,256]{2,1,0:T(8,128)(2,1)S(1)} %all_gather.3.qg_ref, bf16[8,36,1024]{2,1,0:T(8,128)(2,1)S(1)} %all-to-all-done.1.kv_ref), custom_call_target="tpu_custom_call" | custom-call | tf_op jit(solution)/shard_map/pallas_call | solution.py:29
  63.7 19.4 %all_to_all.31.st_ref = bf16[12,48,256]{2,1,0:T(8,128)(2,1)S(1)} all-to-all(bf16[12,48,256]{2,1,0:T(8,128)(2,1)S(1)} %shard_map.97), channel_id=1, replica_groups=mesh['z'=12,'y'=8,'head'=8] {'z'}, dimensions={0} | all-to-all | bytes 589824 | tf_op jit(solution)/shard_map/all_to_all | solution.py:300
  83.1 1.7 %shard_map.98 = bf16[8,36,384]{2,1,0:T(8,128)(2,1)S(1)} custom-call(s32[8,96]{1,0:T(8,128)S(1)} %copy-done.6, bf16[12,36,256]{2,1,0:T(8,128)(2,1)S(1)} %all_gather.3.qg_ref, bf16[8,36,1024]{2,1,0:T(8,128)(2,1)S(1)} %all-to-all-done.1.kv_ref, bf16[12,48,256]{2,1,0:T(8,128)(2,1)S(1)} %all_to_all.31.st_ref), custom_call_target="tpu_custom_call" | custom-call | tf_op jit(solution)/shard_map/pallas_call | solution.py:29
  84.8 11.7 %all_to_all.32.back_ref = bf16[8,36,384]{2,1,0:T(8,128)(2,1)S(1)} all-to-all(bf16[8,36,384]{2,1,0:T(8,128)(2,1)S(1)} %shard_map.98), channel_id=1, replica_groups=mesh['z'=12,'y'=8,'head'=8] {'y'}, dimensions={0} | all-to-all | bytes 442368 | tf_op jit(solution)/shard_map/all_to_all | solution.py:300
  96.6 0.0 copy-done.4
  96.6 1.8 %shard_map.99 = (bf16[8,36,768]{2,1,0:T(8,128)(2,1)S(1)}, bf16[12,64,128]{2,1,0:T(8,128)(2,1)S(1)}) custom-call(bf16[8,36,384]{2,1,0:T(8,128)(2,1)S(1)} %all_to_all.32.back_ref, bf16[8,36,1024]{2,1,0:T(8,128)(2,1)S(1)} %all-to-all-done.1.kv_ref, bf16[6144,128]{1,0:T(8,128)(2,1)S(1)} %bitcast.6, bf16[6144,128]{1,0:T(8,128)(2,1)S(1)} %bitcast.8, ...), custom_call_target="tpu_custom_call" | custom-call | tf_op jit(solution)/shard_map/pallas_call | solution.py:29
  98.4 20.2 %all_to_all.33.g_ref = bf16[8,36,768]{2,1,0:T(8,128)(2,1)S(1)} all-to-all(bf16[8,36,768]{2,1,0:T(8,128)(2,1)S(1)} %get-tuple-element.20), channel_id=1, replica_groups=mesh['z'=12,'y'=8,'head'=8] {'head'}, dimensions={0} | all-to-all | bytes 884736 | tf_op jit(solution)/shard_map/all_to_all | solution.py:300
  118.5 14.7 %all_to_all.34.t_ref = bf16[12,64,128]{2,1,0:T(8,128)(2,1)S(1)} all-to-all(bf16[12,64,128]{2,1,0:T(8,128)(2,1)S(1)} %get-tuple-element.21), channel_id=1, replica_groups=mesh['z'=12,'y'=8,'head'=8] {'z'}, dimensions={0} | all-to-all | bytes 393216 | tf_op jit(solution)/shard_map/all_to_all | solution.py:300
  133.2 2.1 %shard_map.100 = (bf16[288,768]{1,0:T(8,128)(2,1)}, f32[64,128]{1,0:T(8,128)}) custom-call(s32[8,96]{1,0:T(8,128)S(1)} %copy-done.6, s32[8,128]{1,0:T(8,128)S(1)} %copy-done.7, bf16[8,36,768]{2,1,0:T(8,128)(2,1)S(1)} %all_to_all.33.g_ref, bf16[12,64,128]{2,1,0:T(8,128)(2,1)S(1)} %all_to_all.34.t_ref), custom_call_target="tpu_custom_call" | custom-call | tf_op jit(solution)/shard_map/pallas_call | solution.py:29
  (6 shorter events, 0.0 us)
Async XLA Ops:
  0.6 31.3 %copy-start.1 = (bf16[1,6144,128]{2,1,0:T(8,128)(2,1)S(1)}, bf16[1,6144,128]{2,1,0:T(8,128)(2,1)}, u32[]{:S(2)}) copy-start(bf16[1,6144,128]{2,1,0:T(8,128)(2,1)} %param.11) | copy-start | bytes 4718596
  0.6 31.3 %copy-start.3 = (bf16[1,6144,128]{2,1,0:T(8,128)(2,1)S(1)}, bf16[1,6144,128]{2,1,0:T(8,128)(2,1)}, u32[]{:S(2)}) copy-start(bf16[1,6144,128]{2,1,0:T(8,128)(2,1)} %param.12) | copy-start | bytes 4718596
  0.7 31.3 %copy-start.5 = (bf16[1,128,6144]{2,1,0:T(8,128)(2,1)S(1)}, bf16[1,128,6144]{2,1,0:T(8,128)(2,1)}, u32[]{:S(2)}) copy-start(bf16[1,128,6144]{2,1,0:T(8,128)(2,1)} %param.13) | copy-start | bytes 4718596
  4.3 27.6 %copy-start = (bf16[1,6144,128]{2,1,0:T(8,128)(2,1)S(1)}, bf16[1,6144,128]{2,1,0:T(8,128)(2,1)}, u32[]{:S(2)}) copy-start(bf16[1,6144,128]{2,1,0:T(8,128)(2,1)} %param.10) | copy-start | bytes 4718596
  4.3 27.6 %copy-start.6 = (s32[8,96]{1,0:T(8,128)S(1)}, s32[8,96]{1,0:T(8,128)}, u32[]{:S(2)}) copy-start(s32[8,96]{1,0:T(8,128)} %cnt_ref.4) | copy-start | bytes 9220
  34.2 27.6 %all-to-all-start.1 = ((bf16[8,36,1024]{2,1,0:T(8,128)(2,1)}), bf16[8,36,1024]{2,1,0:T(8,128)(2,1)S(1)}, u32[]{:S(2)}, u32[]{:S(2)}) async-start(bf16[8,36,1024]{2,1,0:T(8,128)(2,1)} %get-tuple-element.19), calls=%async_computation.1 | async-start | bytes 1310720 | tf_op jit(solution)/shard_map/all_to_all | solution.py:300
  61.8 34.8 %copy-start.2 = (bf16[1,6144,128]{2,1,0:T(8,128)(2,1)S(1)}, bf16[1,6144,128]{2,1,0:T(8,128)(2,1)}, u32[]{:S(2)}) copy-start(bf16[1,6144,128]{2,1,0:T(8,128)(2,1)} %param.11) | copy-start | bytes 4718596
  61.8 34.8 %copy-start.4 = (bf16[1,6144,128]{2,1,0:T(8,128)(2,1)S(1)}, bf16[1,6144,128]{2,1,0:T(8,128)(2,1)}, u32[]{:S(2)}) copy-start(bf16[1,6144,128]{2,1,0:T(8,128)(2,1)} %param.12) | copy-start | bytes 4718596
  96.6 36.6 %copy-start.7 = (s32[8,128]{1,0:T(8,128)S(1)}, s32[8,128]{1,0:T(8,128)}, u32[]{:S(2)}) copy-start(s32[8,128]{1,0:T(8,128)} %get-tuple-element.17.sel_ref) | copy-start | bytes 12292

commit v7 on v6

--- a/solution.py
+++ b/solution.py
@@ -358,7 +358,9 @@
         [VMEM] * 5,
         [pltpu.VMEM((NY, SLOT, piece), BF), pltpu.VMEM((NY, SLOT, hd), BF)],
     )
-    returned, terms = swap(grad_rows, "head"), swap(weight_terms, "z")
+    terms = swap(weight_terms, "z")
+    grad_rows, terms = lax.optimization_barrier((grad_rows, terms))
+    returned = swap(grad_rows, "head")
     grad_hidden, grad_query = call(
         finish_kernel,
         (sds((toks, cols), BF), sds((piece // nz, hd), F32)),

time: 136 us -> 136 us (level)
  no operation moved by 1% of the time
where the time goes in v7:
time: 136 us
  blocking collectives  118 us (87%)
  Pallas kernels  13.3 us (10%)
  starting transfers between devices  3.55 us (3%)
    all_to_all x5, blocking collectives, swap(): return lax.all_to_all(x, axis, split_axis=0, concat_axis=0, tiled=True)  94.3 us
    all_gather x1, blocking collectives, body(): qg = lax.all_gather(to_z, 'z', axis=0, tiled=True)  24 us
    pallas_call x6, Pallas kernels, call(): pl.pallas_call(kernel, out_shape=outs, in_specs=specs, out_specs=out_spec...  13.3 us
    all_to_all x1, starting transfers between devices, swap(): return lax.all_to_all(x, axis, split_axis=0, concat_axis=0, tiled=True)  3.55 us
  transfers between devices with their start and end apart: 1, of which 0 were waited for; matrix products, arithmetic and copies ran while one was open for 0% of the time, Pallas kernels for 0%

profile of v7, /device:TPU:1, one launch (start us, length us, event | category | flops | bytes accessed | tf_op | source)
XLA Modules:
  0.0 136.0 jit_solution(11037443758785993491)
XLA Ops:
  0.6 0.0 copy-start.1
  0.6 0.0 copy-start.3
  0.7 0.0 copy-start.5
  0.7 3.7 %shard_map.95 = (bf16[8,72,768]{2,1,0:T(8,128)(2,1)}, s32[8,128]{1,0:T(8,128)}) custom-call(s32[8,3456]{1,0:T(8,128)} %sel_ref.1, bf16[288,768]{1,0:T(8,128)(2,1)} %hid_ref.1, bf16[288,768]{1,0:T(8,128)(2,1)} %up_ref.1), custom_call_target="tpu_custom_call" | custom-call | flops 20000000000 | tf_op jit(solution)/shard_map/pallas_call | solution.py:29
  4.3 0.0 copy-start
  4.3 0.0 copy-start.6
  4.4 27.6 %all_to_all.30.r_ref = bf16[8,72,768]{2,1,0:T(8,128)(2,1)S(1)} all-to-all(bf16[8,72,768]{2,1,0:T(8,128)(2,1)} %get-tuple-element.15), channel_id=1, replica_groups=mesh['z'=12,'y'=8,'head'=8] {'head'}, dimensions={0} | all-to-all | bytes 1769472 | tf_op jit(solution)/shard_map/all_to_all | solution.py:300
  31.9 0.0 copy-done.1
  32.0 0.0 copy-done.3
  32.0 0.0 copy-done.5
  32.0 0.0 copy-done
  32.0 2.2 %shard_map.96 = (bf16[1,36,256]{2,1,0:T(8,128)(2,1)S(1)}, bf16[8,36,1024]{2,1,0:T(8,128)(2,1)}) custom-call(s32[8,96]{1,0:T(8,128)S(1)} %copy-done.6, bf16[8,72,768]{2,1,0:T(8,128)(2,1)S(1)} %all_to_all.30.r_ref, bf16[6144,128]{1,0:T(8,128)(2,1)S(1)} %bitcast.5, bf16[6144,128]{1,0:T(8,128)(2,1)S(1)} %bitcast.7, bf16[6144,128]{1,0:T(8,128)(2,1)S(1)} %bitcast.9, ...), custom_call_target="tpu_custom_call" | custom-call | tf_op jit(solution)/shard_map/pallas_call | solution.py:29
  34.2 3.6 %all-to-all-start.1 = ((bf16[8,36,1024]{2,1,0:T(8,128)(2,1)}), bf16[8,36,1024]{2,1,0:T(8,128)(2,1)S(1)}, u32[]{:S(2)}, u32[]{:S(2)}) async-start(bf16[8,36,1024]{2,1,0:T(8,128)(2,1)} %get-tuple-element.21), calls=%async_computation.1 | async-start | bytes 1310720 | tf_op jit(solution)/shard_map/all_to_all | solution.py:300
  37.7 24.0 %all_gather.3.qg_ref = bf16[12,36,256]{2,1,0:T(8,128)(2,1)S(1)} all-gather(bf16[1,36,256]{2,1,0:T(8,128)(2,1)S(1)} %get-tuple-element.20), channel_id=1, replica_groups=mesh['z'=12,'y'=8,'head'=8] {'z'}, dimensions={0}, use_global_device_ids=true | all-gather | bytes 239616 | tf_op jit(solution)/shard_map/all_gather | solution.py:335
  61.8 0.0 all-to-all-done.1.kv_ref
  61.8 1.9 %shard_map.97 = bf16[12,48,256]{2,1,0:T(8,128)(2,1)S(1)} custom-call(s32[8,96]{1,0:T(8,128)S(1)} %copy-done.6, bf16[12,36,256]{2,1,0:T(8,128)(2,1)S(1)} %all_gather.3.qg_ref, bf16[8,36,1024]{2,1,0:T(8,128)(2,1)S(1)} %all-to-all-done.1.kv_ref), custom_call_target="tpu_custom_call" | custom-call | tf_op jit(solution)/shard_map/pallas_call | solution.py:29
  63.7 19.4 %all_to_all.31.st_ref = bf16[12,48,256]{2,1,0:T(8,128)(2,1)S(1)} all-to-all(bf16[12,48,256]{2,1,0:T(8,128)(2,1)S(1)} %shard_map.97), channel_id=1, replica_groups=mesh['z'=12,'y'=8,'head'=8] {'z'}, dimensions={0} | all-to-all | bytes 589824 | tf_op jit(solution)/shard_map/all_to_all | solution.py:300
  83.1 1.7 %shard_map.98 = bf16[8,36,384]{2,1,0:T(8,128)(2,1)S(1)} custom-call(s32[8,96]{1,0:T(8,128)S(1)} %copy-done.6, bf16[12,36,256]{2,1,0:T(8,128)(2,1)S(1)} %all_gather.3.qg_ref, bf16[8,36,1024]{2,1,0:T(8,128)(2,1)S(1)} %all-to-all-done.1.kv_ref, bf16[12,48,256]{2,1,0:T(8,128)(2,1)S(1)} %all_to_all.31.st_ref), custom_call_target="tpu_custom_call" | custom-call | tf_op jit(solution)/shard_map/pallas_call | solution.py:29
  84.8 11.7 %all_to_all.32.back_ref = bf16[8,36,384]{2,1,0:T(8,128)(2,1)S(1)} all-to-all(bf16[8,36,384]{2,1,0:T(8,128)(2,1)S(1)} %shard_map.98), channel_id=1, replica_groups=mesh['z'=12,'y'=8,'head'=8] {'y'}, dimensions={0} | all-to-all | bytes 442368 | tf_op jit(solution)/shard_map/all_to_all | solution.py:300
  96.6 0.0 copy-done.4
  96.6 1.8 %shard_map.99 = (bf16[8,36,768]{2,1,0:T(8,128)(2,1)S(1)}, bf16[12,64,128]{2,1,0:T(8,128)(2,1)S(1)}) custom-call(bf16[8,36,384]{2,1,0:T(8,128)(2,1)S(1)} %all_to_all.32.back_ref, bf16[8,36,1024]{2,1,0:T(8,128)(2,1)S(1)} %all-to-all-done.1.kv_ref, bf16[6144,128]{1,0:T(8,128)(2,1)S(1)} %bitcast.6, bf16[6144,128]{1,0:T(8,128)(2,1)S(1)} %bitcast.8, ...), custom_call_target="tpu_custom_call" | custom-call | tf_op jit(solution)/shard_map/pallas_call | solution.py:29
  98.4 16.8 %all_to_all.33.t_ref = bf16[12,64,128]{2,1,0:T(8,128)(2,1)S(1)} all-to-all(bf16[12,64,128]{2,1,0:T(8,128)(2,1)S(1)} %get-tuple-element.23), channel_id=1, replica_groups=mesh['z'=12,'y'=8,'head'=8] {'z'}, dimensions={0} | all-to-all | bytes 393216 | tf_op jit(solution)/shard_map/all_to_all | solution.py:300
  115.2 18.7 %all_to_all.34.g_ref = bf16[8,36,768]{2,1,0:T(8,128)(2,1)S(1)} all-to-all(bf16[8,36,768]{2,1,0:T(8,128)(2,1)S(1)} %get-tuple-element.24), channel_id=1, replica_groups=mesh['z'=12,'y'=8,'head'=8] {'head'}, dimensions={0} | all-to-all | bytes 884736 | tf_op jit(solution)/shard_map/all_to_all | solution.py:300
  133.9 2.1 %shard_map.100 = (bf16[288,768]{1,0:T(8,128)(2,1)}, f32[64,128]{1,0:T(8,128)}) custom-call(s32[8,96]{1,0:T(8,128)S(1)} %copy-done.6, s32[8,128]{1,0:T(8,128)S(1)} %copy-done.7, bf16[8,36,768]{2,1,0:T(8,128)(2,1)S(1)} %all_to_all.34.g_ref, bf16[12,64,128]{2,1,0:T(8,128)(2,1)S(1)} %all_to_all.33.t_ref), custom_call_target="tpu_custom_call" | custom-call | tf_op jit(solution)/shard_map/pallas_call | solution.py:29
  (6 shorter events, 0.0 us)
Async XLA Ops:
  0.6 31.3 %copy-start.1 = (bf16[1,6144,128]{2,1,0:T(8,128)(2,1)S(1)}, bf16[1,6144,128]{2,1,0:T(8,128)(2,1)}, u32[]{:S(2)}) copy-start(bf16[1,6144,128]{2,1,0:T(8,128)(2,1)} %param.11) | copy-start | bytes 4718596
  0.6 31.3 %copy-start.3 = (bf16[1,6144,128]{2,1,0:T(8,128)(2,1)S(1)}, bf16[1,6144,128]{2,1,0:T(8,128)(2,1)}, u32[]{:S(2)}) copy-start(bf16[1,6144,128]{2,1,0:T(8,128)(2,1)} %param.12) | copy-start | bytes 4718596
  0.7 31.3 %copy-start.5 = (bf16[1,128,6144]{2,1,0:T(8,128)(2,1)S(1)}, bf16[1,128,6144]{2,1,0:T(8,128)(2,1)}, u32[]{:S(2)}) copy-start(bf16[1,128,6144]{2,1,0:T(8,128)(2,1)} %param.13) | copy-start | bytes 4718596
  4.3 27.6 %copy-start = (bf16[1,6144,128]{2,1,0:T(8,128)(2,1)S(1)}, bf16[1,6144,128]{2,1,0:T(8,128)(2,1)}, u32[]{:S(2)}) copy-start(bf16[1,6144,128]{2,1,0:T(8,128)(2,1)} %param.10) | copy-start | bytes 4718596
  4.3 27.6 %copy-start.6 = (s32[8,96]{1,0:T(8,128)S(1)}, s32[8,96]{1,0:T(8,128)}, u32[]{:S(2)}) copy-start(s32[8,96]{1,0:T(8,128)} %cnt_ref.4) | copy-start | bytes 9220
  34.2 27.6 %all-to-all-start.1 = ((bf16[8,36,1024]{2,1,0:T(8,128)(2,1)}), bf16[8,36,1024]{2,1,0:T(8,128)(2,1)S(1)}, u32[]{:S(2)}, u32[]{:S(2)}) async-start(bf16[8,36,1024]{2,1,0:T(8,128)(2,1)} %get-tuple-element.21), calls=%async_computation.1 | async-start | bytes 1310720 | tf_op jit(solution)/shard_map/all_to_all | solution.py:300
  61.8 34.8 %copy-start.2 = (bf16[1,6144,128]{2,1,0:T(8,128)(2,1)S(1)}, bf16[1,6144,128]{2,1,0:T(8,128)(2,1)}, u32[]{:S(2)}) copy-start(bf16[1,6144,128]{2,1,0:T(8,128)(2,1)} %param.11) | copy-start | bytes 4718596
  61.8 34.8 %copy-start.4 = (bf16[1,6144,128]{2,1,0:T(8,128)(2,1)S(1)}, bf16[1,6144,128]{2,1,0:T(8,128)(2,1)}, u32[]{:S(2)}) copy-start(bf16[1,6144,128]{2,1,0:T(8,128)(2,1)} %param.12) | copy-start | bytes 4718596
  96.6 37.3 %copy-start.7 = (s32[8,128]{1,0:T(8,128)S(1)}, s32[8,128]{1,0:T(8,128)}, u32[]{:S(2)}) copy-start(s32[8,128]{1,0:T(8,128)} %get-tuple-element.19.sel_ref) | copy-start | bytes 12292

commit v8 on v7

--- a/solution.py
+++ b/solution.py
@@ -243,7 +243,7 @@
     order_q, order_k = orders(cnt_ref, nz, 1)
     allowed = order_k <= order_q
     s = mm(k, q, NT) * scale
-    p = jnp.where(allowed, jnp.exp(jnp.where(allowed, s - log_total, NEG)), 0.0)
+    p = jnp.exp(jnp.where(allowed, s - log_total, NEG))
     ds = (p * (mm(v, g, NT) - delta)).astype(BF)
     grad_k = (mm(ds, q) * scale).astype(BF).reshape(NY, SLOT, hd)
     grad_v = mm(p.astype(BF), g).astype(BF).reshape(NY, SLOT, hd)
@@ -270,7 +270,7 @@
         g_ref[c] = mm(qkv, w, NT).astype(BF)
 
 
-def finish_kernel(cnt_ref, sel_ref, g_ref, t_ref, h_out, w_out, pad_ref):
+def finish_kernel(cnt_ref, sel_ref, g_ref, t_ref, h_out, w_out, pad_ref, ready, sems):
     heads, cap, cols = g_ref.shape
     toks = h_out.shape[0]
     block = lax.axis_index("z") * NY + lax.axis_index("y")
@@ -284,8 +284,15 @@
     lane = lax.broadcasted_iota(jnp.int32, (heads * SLOT, toks), 1)
     hit = jnp.where(lane == target, 1.0, 0.0).astype(BF)
     grads = padded(pad_ref, g_ref, 0, cols)
-    h_out[...] = mm(hit, grads, TN).astype(BF)
+    leave = []
+    for i in range(cols // WIDE):
+        at = pl.ds(i * WIDE, WIDE)
+        ready[:, at] = mm(hit, grads[:, i * WIDE : (i + 1) * WIDE], TN).astype(BF)
+        leave.append(pltpu.make_async_copy(ready.at[:, at], h_out.at[:, at], sems.at[i]))
+        leave[i].start()
     w_out[...] = jnp.sum(t_ref[...].astype(F32), axis=0)
+    for copy in leave:
+        copy.wait()
 
 
 def body(hidden, upstream, w_query, w_key, w_value, w_output, selected, select_count):
@@ -366,7 +373,12 @@
         (sds((toks, cols), BF), sds((piece // nz, hd), F32)),
         (count, mine, returned, terms),
         [SMEM] + [VMEM] * 3,
-        [pltpu.VMEM((heads, SLOT, cols), BF)],
+        [
+            pltpu.VMEM((heads, SLOT, cols), BF),
+            pltpu.VMEM((toks, cols), BF),
+            pltpu.SemaphoreType.DMA((cols // WIDE,)),
+        ],
+        out_specs=(HBM, VMEM),
     )
     return grad_hidden, grad_query[None]
 

time: 136 us -> 137 us (level)
  no operation moved by 1% of the time
where the time goes in v8:
time: 137 us; the launch traced here: 136 us
  blocking collectives  118 us (86%)
  Pallas kernels  13.8 us (10%)
  starting transfers between devices  3.55 us (3%)
    all_to_all x5, blocking collectives, swap(): return lax.all_to_all(x, axis, split_axis=0, concat_axis=0, tiled=True)  94.3 us
    all_gather x1, blocking collectives, body(): qg = lax.all_gather(to_z, 'z', axis=0, tiled=True)  24 us
    pallas_call x6, Pallas kernels, call(): pl.pallas_call(kernel, out_shape=outs, in_specs=specs, out_specs=out_spec...  13.8 us
    all_to_all x1, starting transfers between devices, swap(): return lax.all_to_all(x, axis, split_axis=0, concat_axis=0, tiled=True)  3.55 us
  transfers between devices with their start and end apart: 1, of which 0 were waited for; matrix products, arithmetic and copies ran while one was open for 0% of the time, Pallas kernels for 0%

profile of v8, /device:TPU:1, one launch (start us, length us, event | category | flops | bytes accessed | tf_op | source)
XLA Modules:
  0.0 136.5 jit_solution(2879673922747700745)
XLA Ops:
  0.6 0.0 copy-start.1
  0.6 0.0 copy-start.3
  0.7 0.0 copy-start.5
  0.7 3.7 %shard_map.95 = (bf16[8,72,768]{2,1,0:T(8,128)(2,1)}, s32[8,128]{1,0:T(8,128)}) custom-call(s32[8,3456]{1,0:T(8,128)} %sel_ref.1, bf16[288,768]{1,0:T(8,128)(2,1)} %hid_ref.1, bf16[288,768]{1,0:T(8,128)(2,1)} %up_ref.1), custom_call_target="tpu_custom_call" | custom-call | flops 20000000000 | tf_op jit(solution)/shard_map/pallas_call | solution.py:29
  4.3 0.0 copy-start
  4.3 0.0 copy-start.6
  4.4 27.6 %all_to_all.30.r_ref = bf16[8,72,768]{2,1,0:T(8,128)(2,1)S(1)} all-to-all(bf16[8,72,768]{2,1,0:T(8,128)(2,1)} %get-tuple-element.15), channel_id=1, replica_groups=mesh['z'=12,'y'=8,'head'=8] {'head'}, dimensions={0} | all-to-all | bytes 1769472 | tf_op jit(solution)/shard_map/all_to_all | solution.py:307
  31.9 0.0 copy-done.1
  32.0 0.0 copy-done.3
  32.0 0.0 copy-done.5
  32.0 0.0 copy-done
  32.0 0.0 copy-done.6
  32.0 2.2 %shard_map.96 = (bf16[1,36,256]{2,1,0:T(8,128)(2,1)S(1)}, bf16[8,36,1024]{2,1,0:T(8,128)(2,1)}) custom-call(s32[8,96]{1,0:T(8,128)S(1)} %copy-done.6, bf16[8,72,768]{2,1,0:T(8,128)(2,1)S(1)} %all_to_all.30.r_ref, bf16[6144,128]{1,0:T(8,128)(2,1)S(1)} %bitcast.5, bf16[6144,128]{1,0:T(8,128)(2,1)S(1)} %bitcast.7, bf16[6144,128]{1,0:T(8,128)(2,1)S(1)} %bitcast.9, ...), custom_call_target="tpu_custom_call" | custom-call | tf_op jit(solution)/shard_map/pallas_call | solution.py:29
  34.2 3.6 %all-to-all-start.1 = ((bf16[8,36,1024]{2,1,0:T(8,128)(2,1)}), bf16[8,36,1024]{2,1,0:T(8,128)(2,1)S(1)}, u32[]{:S(2)}, u32[]{:S(2)}) async-start(bf16[8,36,1024]{2,1,0:T(8,128)(2,1)} %get-tuple-element.21), calls=%async_computation.1 | async-start | bytes 1310720 | tf_op jit(solution)/shard_map/all_to_all | solution.py:307
  37.7 24.0 %all_gather.3.qg_ref = bf16[12,36,256]{2,1,0:T(8,128)(2,1)S(1)} all-gather(bf16[1,36,256]{2,1,0:T(8,128)(2,1)S(1)} %get-tuple-element.20), channel_id=1, replica_groups=mesh['z'=12,'y'=8,'head'=8] {'z'}, dimensions={0}, use_global_device_ids=true | all-gather | bytes 239616 | tf_op jit(solution)/shard_map/all_gather | solution.py:342
  61.8 0.0 all-to-all-done.1.kv_ref
  61.8 1.9 %shard_map.97 = bf16[12,48,256]{2,1,0:T(8,128)(2,1)S(1)} custom-call(s32[8,96]{1,0:T(8,128)S(1)} %copy-done.6, bf16[12,36,256]{2,1,0:T(8,128)(2,1)S(1)} %all_gather.3.qg_ref, bf16[8,36,1024]{2,1,0:T(8,128)(2,1)S(1)} %all-to-all-done.1.kv_ref), custom_call_target="tpu_custom_call" | custom-call | tf_op jit(solution)/shard_map/pallas_call | solution.py:29
  63.7 19.4 %all_to_all.31.st_ref = bf16[12,48,256]{2,1,0:T(8,128)(2,1)S(1)} all-to-all(bf16[12,48,256]{2,1,0:T(8,128)(2,1)S(1)} %shard_map.97), channel_id=1, replica_groups=mesh['z'=12,'y'=8,'head'=8] {'z'}, dimensions={0} | all-to-all | bytes 589824 | tf_op jit(solution)/shard_map/all_to_all | solution.py:307
  83.1 1.7 %shard_map.98 = bf16[8,36,384]{2,1,0:T(8,128)(2,1)S(1)} custom-call(s32[8,96]{1,0:T(8,128)S(1)} %copy-done.6, bf16[12,36,256]{2,1,0:T(8,128)(2,1)S(1)} %all_gather.3.qg_ref, bf16[8,36,1024]{2,1,0:T(8,128)(2,1)S(1)} %all-to-all-done.1.kv_ref, bf16[12,48,256]{2,1,0:T(8,128)(2,1)S(1)} %all_to_all.31.st_ref), custom_call_target="tpu_custom_call" | custom-call | tf_op jit(solution)/shard_map/pallas_call | solution.py:29
  84.8 11.7 %all_to_all.32.back_ref = bf16[8,36,384]{2,1,0:T(8,128)(2,1)S(1)} all-to-all(bf16[8,36,384]{2,1,0:T(8,128)(2,1)S(1)} %shard_map.98), channel_id=1, replica_groups=mesh['z'=12,'y'=8,'head'=8] {'y'}, dimensions={0} | all-to-all | bytes 442368 | tf_op jit(solution)/shard_map/all_to_all | solution.py:307
  96.5 1.8 %shard_map.99 = (bf16[8,36,768]{2,1,0:T(8,128)(2,1)S(1)}, bf16[12,64,128]{2,1,0:T(8,128)(2,1)S(1)}) custom-call(bf16[8,36,384]{2,1,0:T(8,128)(2,1)S(1)} %all_to_all.32.back_ref, bf16[8,36,1024]{2,1,0:T(8,128)(2,1)S(1)} %all-to-all-done.1.kv_ref, bf16[6144,128]{1,0:T(8,128)(2,1)S(1)} %bitcast.6, bf16[6144,128]{1,0:T(8,128)(2,1)S(1)} %bitcast.8, ...), custom_call_target="tpu_custom_call" | custom-call | tf_op jit(solution)/shard_map/pallas_call | solution.py:29
  98.3 16.8 %all_to_all.33.t_ref = bf16[12,64,128]{2,1,0:T(8,128)(2,1)S(1)} all-to-all(bf16[12,64,128]{2,1,0:T(8,128)(2,1)S(1)} %get-tuple-element.23), channel_id=1, replica_groups=mesh['z'=12,'y'=8,'head'=8] {'z'}, dimensions={0} | all-to-all | bytes 393216 | tf_op jit(solution)/shard_map/all_to_all | solution.py:307
  115.1 18.7 %all_to_all.34.g_ref = bf16[8,36,768]{2,1,0:T(8,128)(2,1)S(1)} all-to-all(bf16[8,36,768]{2,1,0:T(8,128)(2,1)S(1)} %get-tuple-element.24), channel_id=1, replica_groups=mesh['z'=12,'y'=8,'head'=8] {'head'}, dimensions={0} | all-to-all | bytes 884736 | tf_op jit(solution)/shard_map/all_to_all | solution.py:307
  133.8 2.6 %shard_map.100 = (bf16[288,768]{1,0:T(8,128)(2,1)}, f32[64,128]{1,0:T(8,128)}) custom-call(s32[8,96]{1,0:T(8,128)S(1)} %copy-done.6, s32[8,128]{1,0:T(8,128)S(1)} %copy-done.7, bf16[8,36,768]{2,1,0:T(8,128)(2,1)S(1)} %all_to_all.34.g_ref, bf16[12,64,128]{2,1,0:T(8,128)(2,1)S(1)} %all_to_all.33.t_ref), custom_call_target="tpu_custom_call" | custom-call | tf_op jit(solution)/shard_map/pallas_call | solution.py:29
  (6 shorter events, 0.0 us)
Async XLA Ops:
  0.6 31.3 %copy-start.1 = (bf16[1,6144,128]{2,1,0:T(8,128)(2,1)S(1)}, bf16[1,6144,128]{2,1,0:T(8,128)(2,1)}, u32[]{:S(2)}) copy-start(bf16[1,6144,128]{2,1,0:T(8,128)(2,1)} %param.11) | copy-start | bytes 4718596
  0.6 31.3 %copy-start.3 = (bf16[1,6144,128]{2,1,0:T(8,128)(2,1)S(1)}, bf16[1,6144,128]{2,1,0:T(8,128)(2,1)}, u32[]{:S(2)}) copy-start(bf16[1,6144,128]{2,1,0:T(8,128)(2,1)} %param.12) | copy-start | bytes 4718596
  0.7 31.3 %copy-start.5 = (bf16[1,128,6144]{2,1,0:T(8,128)(2,1)S(1)}, bf16[1,128,6144]{2,1,0:T(8,128)(2,1)}, u32[]{:S(2)}) copy-start(bf16[1,128,6144]{2,1,0:T(8,128)(2,1)} %param.13) | copy-start | bytes 4718596
  4.3 27.6 %copy-start = (bf16[1,6144,128]{2,1,0:T(8,128)(2,1)S(1)}, bf16[1,6144,128]{2,1,0:T(8,128)(2,1)}, u32[]{:S(2)}) copy-start(bf16[1,6144,128]{2,1,0:T(8,128)(2,1)} %param.10) | copy-start | bytes 4718596
  4.3 27.6 %copy-start.6 = (s32[8,96]{1,0:T(8,128)S(1)}, s32[8,96]{1,0:T(8,128)}, u32[]{:S(2)}) copy-start(s32[8,96]{1,0:T(8,128)} %cnt_ref.4) | copy-start | bytes 9220
  34.2 27.6 %all-to-all-start.1 = ((bf16[8,36,1024]{2,1,0:T(8,128)(2,1)}), bf16[8,36,1024]{2,1,0:T(8,128)(2,1)S(1)}, u32[]{:S(2)}, u32[]{:S(2)}) async-start(bf16[8,36,1024]{2,1,0:T(8,128)(2,1)} %get-tuple-element.21), calls=%async_computation.1 | async-start | bytes 1310720 | tf_op jit(solution)/shard_map/all_to_all | solution.py:307
  61.8 34.7 %copy-start.2 = (bf16[1,6144,128]{2,1,0:T(8,128)(2,1)S(1)}, bf16[1,6144,128]{2,1,0:T(8,128)(2,1)}, u32[]{:S(2)}) copy-start(bf16[1,6144,128]{2,1,0:T(8,128)(2,1)} %param.11) | copy-start | bytes 4718596
  61.8 34.7 %copy-start.4 = (bf16[1,6144,128]{2,1,0:T(8,128)(2,1)S(1)}, bf16[1,6144,128]{2,1,0:T(8,128)(2,1)}, u32[]{:S(2)}) copy-start(bf16[1,6144,128]{2,1,0:T(8,128)(2,1)} %param.12) | copy-start | bytes 4718596
  96.5 37.3 %copy-start.7 = (s32[8,128]{1,0:T(8,128)S(1)}, s32[8,128]{1,0:T(8,128)}, u32[]{:S(2)}) copy-start(s32[8,128]{1,0:T(8,128)} %get-tuple-element.19.sel_ref) | copy-start | bytes 12292
